TPU v7x, 32 devices: a whole 2x2x4 slice. The times are simulated.
32 devices in a mesh: gx: 8 (over z, y), gy: 4 (over x, core).
Axes of the slice: x: 2, y: 2, z: 4, core: 2. Of those that a mesh axis runs over, the one named last changes fastest.
Arguments:
- e_adj: float32 [3, 8, 512, 1024], P(None, None, 'gx', 'gy'), may hold values from -6 to 6
- h_adj: float32 [3, 8, 512, 1024], P(None, None, 'gx', 'gy'), may hold values from -6 to 6
- density: float32 [512, 1024], P('gx', 'gy'), may hold values from 0.05 to 0.95
- material: int32 [8, 512, 1024], P(None, 'gx', 'gy'), may hold values from 0 to 3
- eps_table: float32 [4], replicated, may hold values from 1 to 12
- dft_adj: float32 [4, 2, 3, 2, 512, 1024], P(None, None, None, None, 'gx', 'gy'), may hold values from -6 to 6
- dft_fwd: bfloat16 [4, 2, 3, 2, 512, 1024], P(None, None, None, None, 'gx', 'gy'), may hold values from -6 to 6
- tile_map: int32 [8, 16], P('gx', 'gy'), may hold values from 0 to 31, as said below
Outputs:
- e_out: float32 [3, 8, 512, 1024], P(None, None, 'gx', 'gy')
- h_out: float32 [3, 8, 512, 1024], P(None, None, 'gx', 'gy')
- param_grad: float32 [32, 4096], P(('gx', 'gy'))
Inputs may be any that keep to these rules, and one draw needn't show every extreme that they name: `tile_map`: each of the 32 design parameters is named by exactly 4 tiles. Parameter p belongs to the device at position p // (32 / number of devices) in the gx-major order of devices.
All inputs are finite; a program needn't handle non-finite values.
Results may differ from a plain program's by a relative error of at most 0.0003.
Values sent between devices are 32-bit elements; how exact they have to be, the bound alone decides.
No kernel may reach another device: no remote copies, remote signals or barrier semaphores. Data moves between devices by JAX's collectives and lax.ppermute only.
A program may use at most 64 MiB of HBM per device.

v0:
```python
import jax
import jax.numpy as jnp
from jax import lax
from jax.sharding import PartitionSpec as P

PLANES = 2
ZLO = 3
STEPS = 2
FREQ = 4
PML = 12
MATS = 4
TILE = 64
REPEAT = 4


courant = 0.5
sigma_peak = 0.8
dft_weight = 0.5
sharpness = 4.0
threshold = 0.5
eps_low = 2.1
eps_high = 12.1
grad_scale = 0.01


def with_halo(cells, sides, width):
    for axis, dim in sides:
        count = lax.axis_size(axis)
        ends = count - 1
        head = lax.slice_in_dim(cells, 0, width, axis=dim)
        tail = lax.slice_in_dim(cells, cells.shape[dim] - width, cells.shape[dim], axis=dim)
        cells = jnp.concatenate(
            [
                lax.ppermute(tail, axis, [(i, (i + 1) % count) for i in range(ends)]),
                cells,
                lax.ppermute(head, axis, [((i + 1) % count, i) for i in range(ends)]),
            ],
            axis=dim,
        )
    return cells


def shifted(block, axis, distance):
    devices = range(lax.axis_size(axis))
    route = [(i - distance, i) for i in devices if i - distance in devices]
    return lax.ppermute(block, axis, route)


def positions(offset_index, count_cells):
    return (offset_index * count_cells + jnp.arange(count_cells, dtype=jnp.int32)).astype(
        jnp.float32
    )


def profile(places, total):
    depth = jnp.maximum(jnp.maximum(PML - places, places - (total - 1 - PML)), 0.0) / PML
    return depth * depth * depth


def smooth(grid_field):
    padded = with_halo(grid_field, (("gx", 0), ("gy", 1)), 1)
    summed = padded[:-2] + 2.0 * padded[1:-1] + padded[2:]
    return (summed[:, :-2] + 2.0 * summed[:, 1:-1] + summed[:, 2:]) / 16.0


def step_next(values, border, dim_index):
    inner = lax.slice_in_dim(values, 1, values.shape[dim_index], axis=dim_index)
    return jnp.concatenate([inner, border], axis=dim_index) - values


def step_prev(values, border, dim_index):
    inner = lax.slice_in_dim(values, 0, values.shape[dim_index] - 1, axis=dim_index)
    return values - jnp.concatenate([border, inner], axis=dim_index)


def zero_rim(values, dim_index):
    return jnp.zeros_like(lax.slice_in_dim(values, 0, 1, axis=dim_index))


def next_faces(elec_x, elec_y, elec_z):
    ahead_x = shifted(jnp.stack([elec_y[:, :1, :], elec_z[:, :1, :]]), "gx", -1)
    ahead_y = shifted(jnp.stack([elec_x[:, :, :1], elec_z[:, :, :1]]), "gy", -1)
    return (ahead_x, ahead_y)


def prev_faces(mag_x, mag_y, mag_z):
    behind_x = shifted(jnp.stack([mag_y[:, -1:, :], mag_z[:, -1:, :]]), "gx", 1)
    behind_y = shifted(jnp.stack([mag_x[:, :, -1:], mag_z[:, :, -1:]]), "gy", 1)
    return (behind_x, behind_y)


def curl_forward(elec_x, elec_y, elec_z, ahead_x, ahead_y):
    curl_x = step_next(elec_z, ahead_y[1], 2) - step_next(elec_y, zero_rim(elec_y, 0), 0)
    curl_y = step_next(elec_x, zero_rim(elec_x, 0), 0) - step_next(elec_z, ahead_x[1], 1)
    curl_z = step_next(elec_y, ahead_x[0], 1) - step_next(elec_x, ahead_y[0], 2)
    return (curl_x, curl_y, curl_z)


def curl_backward(mag_x, mag_y, mag_z, behind_x, behind_y):
    curl_x = step_prev(mag_z, behind_y[1], 2) - step_prev(mag_y, zero_rim(mag_y, 0), 0)
    curl_y = step_prev(mag_x, zero_rim(mag_x, 0), 0) - step_prev(mag_z, behind_x[1], 1)
    curl_z = step_prev(mag_y, behind_x[0], 1) - step_prev(mag_x, behind_y[0], 2)
    return (curl_x, curl_y, curl_z)


def accumulate(accum, elec_x, elec_y, elec_z, step_index):
    design = jnp.stack([elec_x, elec_y, elec_z])[:, ZLO : ZLO + PLANES]
    angular = 0.21 + 0.06 * jnp.arange(FREQ, dtype=jnp.float32)
    turned = angular * (step_index + 1)
    weights = jnp.stack([dft_weight * jnp.cos(turned), -dft_weight * jnp.sin(turned)], axis=1)
    return accum + weights[:, :, None, None, None, None] * design[None, None]


def on_device(e_adj, h_adj, density, material, eps_table, dft_adj, dft_fwd, tile_map):
    planes_z, width_x, width_y = material.shape
    count_gx = lax.axis_size("gx")
    count_gy = lax.axis_size("gy")
    total_x = count_gx * width_x
    total_y = count_gy * width_y
    sigma = sigma_peak * (
        profile(positions(lax.axis_index("gx"), width_x), total_x)[:, None]
        + profile(positions(lax.axis_index("gy"), width_y), total_y)[None, :]
    )
    half_sum = 1.0 + 0.5 * sigma
    damping = (1.0 - 0.5 * sigma) / half_sum
    coef_h = courant / half_sum
    filtered = smooth(density)
    bend_value = jnp.tanh(sharpness * (filtered - threshold))
    scale_sum = jnp.tanh(sharpness * threshold) + jnp.tanh(sharpness * (1.0 - threshold))
    projected = (jnp.tanh(sharpness * threshold) + bend_value) / scale_sum
    slope = sharpness * (1.0 - bend_value * bend_value) / scale_sum
    design_eps = eps_low + (eps_high - eps_low) * projected
    eps_grid = jnp.zeros(material.shape, jnp.float32)
    for material_id in range(MATS):
        eps_grid = jnp.where(material == material_id, eps_table[material_id], eps_grid)
    layer_ids = jnp.arange(planes_z, dtype=jnp.int32)[:, None, None]
    inside = (layer_ids >= ZLO) & (layer_ids < ZLO + PLANES)
    eps_grid = jnp.where(inside, design_eps[None], eps_grid)
    coef_e = courant / (eps_grid * half_sum[None])
    elec_x, elec_y, elec_z = (e_adj[0], e_adj[1], e_adj[2])
    mag_x, mag_y, mag_z = (h_adj[0], h_adj[1], h_adj[2])
    accum = dft_adj
    for step_index in range(STEPS):
        ahead_x, ahead_y = next_faces(elec_x, elec_y, elec_z)
        curl_x, curl_y, curl_z = curl_forward(elec_x, elec_y, elec_z, ahead_x, ahead_y)
        mag_x = damping * mag_x - coef_h * curl_x
        mag_y = damping * mag_y - coef_h * curl_y
        mag_z = damping * mag_z - coef_h * curl_z
        behind_x, behind_y = prev_faces(mag_x, mag_y, mag_z)
        curl_x, curl_y, curl_z = curl_backward(mag_x, mag_y, mag_z, behind_x, behind_y)
        elec_x = damping * elec_x + coef_e * curl_x
        elec_y = damping * elec_y + coef_e * curl_y
        elec_z = damping * elec_z + coef_e * curl_z
        accum = accumulate(accum, elec_x, elec_y, elec_z, step_index)
    forward = dft_fwd.astype(jnp.float32)
    intersection = jnp.sum(
        forward[:, 0] * accum[:, 0] - forward[:, 1] * accum[:, 1], axis=(0, 1, 2)
    )
    local_grad = grad_scale * (eps_high - eps_low) * slope * intersection
    grad_cells = smooth(local_grad)
    tile_rows = (
        grad_cells.reshape(width_x // TILE, TILE, width_y // TILE, TILE)
        .transpose(0, 2, 1, 3)
        .reshape(-1, TILE * TILE)
    )
    owners = tile_map.reshape(-1)
    devices_all = count_gx * count_gy
    params_all = total_x // TILE * (total_y // TILE) // REPEAT
    rows_mine = params_all // devices_all
    labels = jnp.arange(rows_mine * count_gy * lax.axis_size("gx"), dtype=jnp.int32)
    one_hot = (labels[:, None] == owners[None, :]).astype(jnp.float32)
    partial_rows = lax.psum_scatter(
        jnp.dot(
            one_hot, tile_rows, precision=lax.Precision.HIGHEST, preferred_element_type=jnp.float32
        ),
        "gx",
        scatter_dimension=0,
        tiled=True,
    )
    param_grad = lax.psum_scatter(partial_rows, "gy", scatter_dimension=0, tiled=True)
    return (jnp.stack([elec_x, elec_y, elec_z]), jnp.stack([mag_x, mag_y, mag_z]), param_grad)


def solution(mesh):
    in_specs = (
        P(None, None, "gx", "gy"),
        P(None, None, "gx", "gy"),
        P("gx", "gy"),
        P(None, "gx", "gy"),
        P(),
        P(None, None, None, None, "gx", "gy"),
        P(None, None, None, None, "gx", "gy"),
        P("gx", "gy"),
    )
    out_specs = (P(None, None, "gx", "gy"), P(None, None, "gx", "gy"), P(("gx", "gy"), None))
    return jax.shard_map(
        on_device, mesh=mesh, in_specs=in_specs, out_specs=out_specs, check_vma=False
    )
```

profile of v0, /device:TPU:0, one launch (start us, length us, event | category | flops | bytes accessed | tf_op | source)
XLA Modules:
  0.0 259.4 jit_solution(11879119319950795229)
XLA Ops:
  14.0 5.5 %collective-permute-start = (f32[1,256]{1,0:T(1,128)S(1)}, f32[1,256]{1,0:T(1,128)S(1)}, u32[]{:S(2)}, u32[]{:S(2)}) collective-permute-start(f32[1,256]{1,0:T(1,128)S(1)} %get-tuple-element.44), channel_id=1, source_target_pairs={{0,4},{4,8},{8,12},{12,16},{16,20},{20,24},{24,28},{1,5},{5,9},{9,... | collective-permute-start | bytes 3080 | tf_op jit(solution)/shard_map/ppermute | solution.py:34
  20.8 2.2 fusion.58
  23.1 2.6 %fusion.59 = (f32[1,8,64,256]{3,2,1,0:T(8,128)}, f32[1,8,64,256]{3,2,1,0:T(8,128)}, f32[1,8,64,256]{3,2,1,0:T(8,128)}) fusion(f32[3,8,64,256]{3,2,1,0:T(8,128)} %param.9), kind=kLoop, calls=%fused_computation.153 | loop fusion | bytes 3145728 | tf_op jit(solution)/shard_map/slice | solution.py:141
  31.4 2.7 %collective-permute-start.2 = (f32[66,1]{1,0:T(8,128)S(1)}, f32[66,1]{1,0:T(8,128)S(1)}, u32[]{:S(2)}, u32[]{:S(2)}) collective-permute-start(f32[66,1]{1,0:T(8,128)S(1)} %get-tuple-element.40), channel_id=1, source_target_pairs={{0,1},{1,2},{2,3},{4,5},{5,6},{6,7},{8,9},{9,10},{10,11},{12,13},{... | collective-permute-start | bytes 800 | tf_op jit(solution)/shard_map/ppermute | solution.py:34
  42.0 4.5 %fusion.7 = (f32[8,64,256]{2,0,1:T(8,128)S(1)}, f32[8,64,256]{2,0,1:T(8,128)S(1)}, f32[8,64,256]{2,0,1:T(8,128)S(1)}) fusion(f32[8,64,1]{2,0,1:T(8,128)} %copy.264, f32[8,64,255]{2,0,1:T(8,128)} %slice.394, f32[1,8,64,256]{3,2,1,0:T(8,128)} %get-tuple-element.26, f32[7,64,256]{2,0,1:T(8,128)} %get-tuple-element.70, f32[64,256]{1,0:T(8,128)S(1)} %get-tuple-element.63, ...), kind=kLoop, calls=%fused_computation.15 | loop fusion | flops 2883584 | bytes 7864320 | tf_op jit(solution)/shard_map/sub | solution.py:146
  47.1 4.4 %collective-permute-start.6 = (f32[2,8,64,1]{2,1,3,0:T(8,128)S(1)}, f32[2,8,64,1]{2,1,3,0:T(8,128)S(1)}, u32[]{:S(2)}, u32[]{:S(2)}) collective-permute-start(f32[2,8,64,1]{2,1,3,0:T(8,128)S(1)} %pad_maximum_fusion.13), channel_id=1, source_target_pairs={{0,1},{1,2},{2,3},{4,5},{5,6},{6,7},{8,9},{9,10},{10,11},{12,13},{... | collective-permute-start | bytes 12296 | tf_op jit(solution)/shard_map/ppermute | solution.py:46
  53.2 4.9 %collective-permute-start.7 = (f32[2,8,1,256]{3,1,2,0:T(8,128)S(1)}, f32[2,8,1,256]{3,1,2,0:T(8,128)S(1)}, u32[]{:S(2)}, u32[]{:S(2)}) collective-permute-start(f32[2,8,1,256]{3,1,2,0:T(8,128)S(1)} %pad_maximum_fusion.9), channel_id=1, source_target_pairs={{0,4},{4,8},{8,12},{12,16},{16,20},{20,24},{24,28},{1,5},{5,9},{9,... | collective-permute-start | bytes 49160 | tf_op jit(solution)/shard_map/ppermute | solution.py:46
  59.1 4.3 %fusion.10 = f32[8,64,256]{2,0,1:T(8,128)S(1)} fusion(f32[8,64,256]{2,0,1:T(8,128)S(1)} %get-tuple-element.37, f32[8,64,255]{2,0,1:T(8,128)S(1)} %bitcast.140, f32[8,64,1]{2,0,1:T(8,128)} %copy.268, f32[8,64,256]{2,0,1:T(8,128)S(1)} %get-tuple-element.36, f32[7,64,256]{2,0,1:T(8,128)S(1)} %bitcast.149, f32[64,256]{1,0:T(8,128)S(1)} %get-tuple-element.64, ...), kind=kLoop, calls=%fused_computation.19 | loop fusion | flops 2359296 | bytes 3801112 | tf_op jit(solution)/shard_map/add | solution.py:151
  66.3 4.7 %fusion.19 = f32[8,64,256]{2,0,1:T(8,128)S(1)} fusion(f32[8,64,256]{2,0,1:T(8,128)S(1)} %get-tuple-element.36, f32[8,63,256]{2,0,1:T(8,128)} %slice.411, f32[8,1,256]{2,0,1:T(8,128)S(1)} %get-tuple-element.51, f32[8,64,256]{2,0,1:T(8,128)S(1)} %get-tuple-element.35, f32[8,64,255]{2,0,1:T(8,128)S(1)} %bitcast.138, f32[8,64,1]{2,0,1:T(8,128)} %copy.271, ...), kind=kLoop, calls=%fused_computation.31 | loop fusion | flops 2490368 | bytes 3866648 | tf_op jit(solution)/shard_map/add | solution.py:153
  71.8 3.4 %fusion.16 = f32[8,64,256]{2,0,1:T(8,128)S(1)} fusion(f32[8,64,256]{2,0,1:T(8,128)S(1)} %get-tuple-element.37, f32[8,63,256]{2,0,1:T(8,128)S(1)} %copy-done.15, f32[8,1,256]{2,0,1:T(8,128)S(1)} %get-tuple-element.50, f32[8,64,256]{2,0,1:T(8,128)S(1)} %get-tuple-element.35, f32[7,64,256]{2,0,1:T(8,128)S(1)} %bitcast.139, f32[64,256]{1,0:T(8,128)S(1)} %get-tuple-element.64, ...), kind=kLoop, calls=%fused_computation.27 | loop fusion | flops 2359296 | bytes 3801112 | tf_op jit(solution)/shard_map/add | solution.py:152
  85.4 3.4 %collective-permute-done.8 = f32[2,8,1,256]{3,1,2,0:T(8,128)S(1)} collective-permute-done((f32[2,8,1,256]{3,1,2,0:T(8,128)S(1)}, f32[2,8,1,256]{3,1,2,0:T(8,128)S(1)}, u32[]{:S(2)}, u32[]{:S(2)}) %collective-permute-start.8) | collective-permute-done | bytes 16416 | tf_op jit(solution)/shard_map/ppermute | solution.py:46
  88.8 3.7 %fusion.25 = (f32[8,64,256]{2,0,1:T(8,128)S(1)}, f32[8,64,256]{2,0,1:T(8,128)S(1)}, f32[8,64,256]{2,0,1:T(8,128)}) fusion(f32[8,64,256]{2,0,1:T(8,128)S(1)} %fusion.19, f32[8,64,1]{2,0,1:T(8,128)} %copy.275, f32[8,64,255]{2,0,1:T(8,128)} %slice.420, f32[8,64,256]{2,0,1:T(8,128)} %copy-done, f32[7,64,256]{2,0,1:T(8,128)} %slice.422, ...), kind=kLoop, calls=%fused_computation.41 | loop fusion | flops 2883584 | bytes 7864320 | tf_op jit(solution)/shard_map/sub | solution.py:146
  96.3 3.3 %collective-permute-start.10 = (f32[2,8,64,1]{2,1,3,0:T(8,128)S(1)}, f32[2,8,64,1]{2,1,3,0:T(8,128)S(1)}, u32[]{:S(2)}, u32[]{:S(2)}) collective-permute-start(f32[2,8,64,1]{2,1,3,0:T(8,128)S(1)} %pad_maximum_fusion.15), channel_id=1, source_target_pairs={{0,1},{1,2},{2,3},{4,5},{5,6},{6,7},{8,9},{9,10},{10,11},{12,13},{... | collective-permute-start | bytes 12296 | tf_op jit(solution)/shard_map/ppermute | solution.py:46
  101.4 4.5 %collective-permute-start.11 = (f32[2,8,1,256]{3,1,2,0:T(8,128)S(1)}, f32[2,8,1,256]{3,1,2,0:T(8,128)S(1)}, u32[]{:S(2)}, u32[]{:S(2)}) collective-permute-start(f32[2,8,1,256]{3,1,2,0:T(8,128)S(1)} %pad_maximum_fusion.11), channel_id=1, source_target_pairs={{0,4},{4,8},{8,12},{12,16},{16,20},{20,24},{24,28},{1,5},{5,9},{9,... | collective-permute-start | bytes 49160 | tf_op jit(solution)/shard_map/ppermute | solution.py:46
  106.8 5.2 %fusion.29 = f32[1,8,64,256]{3,1,2,0:T(8,128)} fusion(f32[8,64,256]{2,0,1:T(8,128)S(1)} %get-tuple-element.33, f32[8,64,255]{2,0,1:T(8,128)S(1)} %bitcast.144, f32[8,64,1]{2,0,1:T(8,128)} %copy.278, f32[8,64,256]{2,0,1:T(8,128)} %get-tuple-element.34, f32[7,64,256]{2,0,1:T(8,128)} %bitcast.150, f32[8,64,256]{2,0,1:T(8,128)S(1)} %fusion.10, ...), kind=kLoop, calls=%fused_computation.46 | loop fusion | flops 2359296 | bytes 3801112 | tf_op jit(solution)/shard_map/stack | solution.py:181
  112.9 4.2 %fusion.36 = f32[1,8,64,256]{3,1,2,0:T(8,128)S(1)} fusion(f32[8,64,256]{2,0,1:T(8,128)S(1)} %get-tuple-element.33, f32[8,63,256]{2,0,1:T(8,128)} %slice.435, f32[8,1,256]{2,0,1:T(8,128)S(1)} %get-tuple-element.46, f32[8,64,256]{2,0,1:T(8,128)S(1)} %get-tuple-element.32, f32[7,64,256]{2,0,1:T(8,128)S(1)} %bitcast.141, f32[8,64,256]{2,0,1:T(8,128)S(1)} %copy-done.1, ...), kind=kLoop, calls=%fused_computation.55 | loop fusion | flops 2359296 | bytes 3801112 | tf_op jit(solution)/shard_map/stack | solution.py:181
  117.2 3.2 %fusion.40 = f32[1,8,64,256]{3,1,2,0:T(8,128)S(1)} fusion(f32[8,64,256]{2,0,1:T(8,128)S(1)} %copy-done.6, f32[8,63,256]{2,0,1:T(8,128)S(1)} %copy-done.16, f32[8,1,256]{2,0,1:T(8,128)S(1)} %get-tuple-element.47, f32[8,64,256]{2,0,1:T(8,128)S(1)} %get-tuple-element.32, f32[8,64,255]{2,0,1:T(8,128)S(1)} %bitcast.142, f32[8,64,1]{2,0,1:T(8,128)S(1)} %copy-done.21, ...), kind=kLoop, calls=%fused_computation.60 | loop fusion | flops 2490368 | bytes 3866648 | tf_op jit(solution)/shard_map/stack | solution.py:181
  125.5 2.9 %collective-permute-start.12 = (f32[1,256]{1,0:T(1,128)S(1)}, f32[1,256]{1,0:T(1,128)S(1)}, u32[]{:S(2)}, u32[]{:S(2)}) collective-permute-start(f32[1,256]{1,0:T(1,128)S(1)} %get-tuple-element.42), channel_id=1, source_target_pairs={{0,4},{4,8},{8,12},{12,16},{16,20},{20,24},{24,28},{1,5},{5,9},{9,... | collective-permute-start | bytes 3080 | tf_op jit(solution)/shard_map/ppermute | solution.py:34
  129.8 4.2 %collective-permute-done.13 = f32[1,256]{1,0:T(1,128)S(1)} collective-permute-done((f32[1,256]{1,0:T(1,128)S(1)}, f32[1,256]{1,0:T(1,128)S(1)}, u32[]{:S(2)}, u32[]{:S(2)}) %collective-permute-start.13) | collective-permute-done | bytes 1056 | tf_op jit(solution)/shard_map/ppermute | solution.py:36
  134.0 3.4 %collective-permute-start.14 = (f32[66,1]{1,0:T(8,128)S(1)}, f32[66,1]{1,0:T(8,128)S(1)}, u32[]{:S(2)}, u32[]{:S(2)}) collective-permute-start(f32[66,1]{1,0:T(8,128)S(1)} %get-tuple-element.38), channel_id=1, source_target_pairs={{0,1},{1,2},{2,3},{4,5},{5,6},{6,7},{8,9},{9,10},{10,11},{12,13},{... | collective-permute-start | bytes 800 | tf_op jit(solution)/shard_map/ppermute | solution.py:34
  138.7 2.7 %collective-permute-done.15 = f32[66,1]{1,0:T(8,128)S(1)} collective-permute-done((f32[66,1]{1,0:T(8,128)S(1)}, f32[66,1]{1,0:T(8,128)S(1)}, u32[]{:S(2)}, u32[]{:S(2)}) %collective-permute-start.15) | collective-permute-done | bytes 296 | tf_op jit(solution)/shard_map/ppermute | solution.py:36
  145.0 72.6 %all-reduce.13.cloned.1.call-done = f32[32,4096]{1,0:T(8,128)} async-done(((f32[32,4096]{1,0:T(8,128)}), f32[32,4096]{1,0:T(8,128)}) %all-reduce.13.cloned.1.call-update) | async-done | bytes 524304
  222.6 27.9 %all-reduce.15.cloned.1.call-done = f32[4,4096]{1,0:T(4,128)} async-done(((f32[4,4096]{1,0:T(4,128)}), f32[4,4096]{1,0:T(4,128)}) %all-reduce.15.cloned.1.call-update) | async-done | bytes 65552
  250.4 2.1 constant_dynamic-slice_fusion
  (189 shorter events, 61.2 us)
Async XLA Ops:
  7.2 210.5 %all-reduce.13.cloned.1.call-start = ((), (), s32[]{:S(2)}) async-start(), calls=%async_computation | async-start | bytes 1048576
  8.7 33.3 %copy-start.8 = (f32[1,8,64,256]{3,2,1,0:T(8,128)}, f32[1,8,64,256]{3,2,1,0:T(8,128)S(1)}, u32[]{:S(2)}) copy-start(f32[1,8,64,256]{3,2,1,0:T(8,128)S(1)} %get-tuple-element.31) | copy-start | bytes 1572868
  8.7 33.3 %copy-start.10 = (f32[1,8,64,256]{3,2,1,0:T(8,128)}, f32[1,8,64,256]{3,2,1,0:T(8,128)S(1)}, u32[]{:S(2)}) copy-start(f32[1,8,64,256]{3,2,1,0:T(8,128)S(1)} %get-tuple-element.30) | copy-start | bytes 1572868
  9.4 32.6 %collective-permute-start.4 = (f32[2,8,1,256]{3,1,2,0:T(8,128)S(1)}, f32[2,8,1,256]{3,1,2,0:T(8,128)S(1)}, u32[]{:S(2)}, u32[]{:S(2)}) collective-permute-start(f32[2,8,1,256]{3,1,2,0:T(8,128)S(1)} %pad_maximum_fusion.8), channel_id=1, source_target_pairs={{4,0},{8,4},{12,8},{16,12},{20,16},{24,20},{28,24},{5,1},{9,5},{13... | collective-permute-start | bytes 49160 | tf_op jit(solution)/shard_map/ppermute | solution.py:46
  12.0 27.6 %collective-permute-start.5 = (f32[2,8,64,1]{2,1,3,0:T(8,128)}, f32[2,8,64,1]{2,1,3,0:T(8,128)}, u32[]{:S(2)}, u32[]{:S(2)}) collective-permute-start(f32[2,8,64,1]{2,1,3,0:T(8,128)} %pad_maximum_fusion.12), channel_id=1, source_target_pairs={{1,0},{2,1},{3,2},{5,4},{6,5},{7,6},{9,8},{10,9},{11,10},{13,12},{... | collective-permute-start | bytes 12296 | tf_op jit(solution)/shard_map/ppermute | solution.py:46
  14.0 17.3 %collective-permute-start = (f32[1,256]{1,0:T(1,128)S(1)}, f32[1,256]{1,0:T(1,128)S(1)}, u32[]{:S(2)}, u32[]{:S(2)}) collective-permute-start(f32[1,256]{1,0:T(1,128)S(1)} %get-tuple-element.44), channel_id=1, source_target_pairs={{0,4},{4,8},{8,12},{12,16},{16,20},{20,24},{24,28},{1,5},{5,9},{9,... | collective-permute-start | bytes 3080 | tf_op jit(solution)/shard_map/ppermute | solution.py:34
  19.5 11.8 %collective-permute-start.1 = (f32[1,256]{1,0:T(1,128)S(1)}, f32[1,256]{1,0:T(1,128)S(1)}, u32[]{:S(2)}, u32[]{:S(2)}) collective-permute-start(f32[1,256]{1,0:T(1,128)S(1)} %get-tuple-element.45), channel_id=1, source_target_pairs={{4,0},{8,4},{12,8},{16,12},{20,16},{24,20},{28,24},{5,1},{9,5},{13... | collective-permute-start | bytes 3080 | tf_op jit(solution)/shard_map/ppermute | solution.py:36
  31.4 7.9 %collective-permute-start.2 = (f32[66,1]{1,0:T(8,128)S(1)}, f32[66,1]{1,0:T(8,128)S(1)}, u32[]{:S(2)}, u32[]{:S(2)}) collective-permute-start(f32[66,1]{1,0:T(8,128)S(1)} %get-tuple-element.40), channel_id=1, source_target_pairs={{0,1},{1,2},{2,3},{4,5},{5,6},{6,7},{8,9},{9,10},{10,11},{12,13},{... | collective-permute-start | bytes 800 | tf_op jit(solution)/shard_map/ppermute | solution.py:34
  34.1 5.2 %collective-permute-start.3 = (f32[66,1]{1,0:T(8,128)S(1)}, f32[66,1]{1,0:T(8,128)S(1)}, u32[]{:S(2)}, u32[]{:S(2)}) collective-permute-start(f32[66,1]{1,0:T(8,128)S(1)} %get-tuple-element.41), channel_id=1, source_target_pairs={{1,0},{2,1},{3,2},{5,4},{6,5},{7,6},{9,8},{10,9},{11,10},{13,12},{... | collective-permute-start | bytes 800 | tf_op jit(solution)/shard_map/ppermute | solution.py:36
  46.5 19.8 %copy-start.2 = (f32[8,64,256]{2,0,1:T(8,128)}, f32[8,64,256]{2,0,1:T(8,128)S(1)}, u32[]{:S(2)}) copy-start(f32[8,64,256]{2,0,1:T(8,128)S(1)} %get-tuple-element.36) | copy-start | bytes 1572868
  47.1 11.0 %collective-permute-start.6 = (f32[2,8,64,1]{2,1,3,0:T(8,128)S(1)}, f32[2,8,64,1]{2,1,3,0:T(8,128)S(1)}, u32[]{:S(2)}, u32[]{:S(2)}) collective-permute-start(f32[2,8,64,1]{2,1,3,0:T(8,128)S(1)} %pad_maximum_fusion.13), channel_id=1, source_target_pairs={{0,1},{1,2},{2,3},{4,5},{5,6},{6,7},{8,9},{9,10},{10,11},{12,13},{... | collective-permute-start | bytes 12296 | tf_op jit(solution)/shard_map/ppermute | solution.py:46
  53.2 13.1 %collective-permute-start.7 = (f32[2,8,1,256]{3,1,2,0:T(8,128)S(1)}, f32[2,8,1,256]{3,1,2,0:T(8,128)S(1)}, u32[]{:S(2)}, u32[]{:S(2)}) collective-permute-start(f32[2,8,1,256]{3,1,2,0:T(8,128)S(1)} %pad_maximum_fusion.9), channel_id=1, source_target_pairs={{0,4},{4,8},{8,12},{12,16},{16,20},{20,24},{24,28},{1,5},{5,9},{9,... | collective-permute-start | bytes 49160 | tf_op jit(solution)/shard_map/ppermute | solution.py:46
  76.5 7.1 %collective-permute-start.9 = (f32[2,8,64,1]{2,1,3,0:T(8,128)S(1)}, f32[2,8,64,1]{2,1,3,0:T(8,128)S(1)}, u32[]{:S(2)}, u32[]{:S(2)}) collective-permute-start(f32[2,8,64,1]{2,1,3,0:T(8,128)S(1)} %pad_maximum_fusion.14), channel_id=1, source_target_pairs={{1,0},{2,1},{3,2},{5,4},{6,5},{7,6},{9,8},{10,9},{11,10},{13,12},{... | collective-permute-start | bytes 12296 | tf_op jit(solution)/shard_map/ppermute | solution.py:46
  82.3 6.5 %collective-permute-start.8 = (f32[2,8,1,256]{3,1,2,0:T(8,128)S(1)}, f32[2,8,1,256]{3,1,2,0:T(8,128)S(1)}, u32[]{:S(2)}, u32[]{:S(2)}) collective-permute-start(f32[2,8,1,256]{3,1,2,0:T(8,128)S(1)} %pad_maximum_fusion.10), channel_id=1, source_target_pairs={{4,0},{8,4},{12,8},{16,12},{20,16},{24,20},{28,24},{5,1},{9,5},{13... | collective-permute-start | bytes 49160 | tf_op jit(solution)/shard_map/ppermute | solution.py:46
  96.3 9.5 %collective-permute-start.10 = (f32[2,8,64,1]{2,1,3,0:T(8,128)S(1)}, f32[2,8,64,1]{2,1,3,0:T(8,128)S(1)}, u32[]{:S(2)}, u32[]{:S(2)}) collective-permute-start(f32[2,8,64,1]{2,1,3,0:T(8,128)S(1)} %pad_maximum_fusion.15), channel_id=1, source_target_pairs={{0,1},{1,2},{2,3},{4,5},{5,6},{6,7},{8,9},{9,10},{10,11},{12,13},{... | collective-permute-start | bytes 12296 | tf_op jit(solution)/shard_map/ppermute | solution.py:46
  101.4 11.5 %collective-permute-start.11 = (f32[2,8,1,256]{3,1,2,0:T(8,128)S(1)}, f32[2,8,1,256]{3,1,2,0:T(8,128)S(1)}, u32[]{:S(2)}, u32[]{:S(2)}) collective-permute-start(f32[2,8,1,256]{3,1,2,0:T(8,128)S(1)} %pad_maximum_fusion.11), channel_id=1, source_target_pairs={{0,4},{4,8},{8,12},{12,16},{16,20},{20,24},{24,28},{1,5},{5,9},{9,... | collective-permute-start | bytes 49160 | tf_op jit(solution)/shard_map/ppermute | solution.py:46
  125.4 16.6 %copy-start.26 = (s32[1,4]{1,0:T(1,128)S(1)}, s32[1,4]{1,0:T(1,128)}, u32[]{:S(2)}) copy-start(s32[1,4]{1,0:T(1,128)} %param.15) | copy-start | bytes 52
  125.5 17.7 %copy-start.28 = (u32[32]{0:T(128)S(1)}, u32[32]{0:T(128)}, u32[]{:S(2)}) copy-start(u32[32]{0:T(128)} %constant.101) | copy-start | bytes 388
  125.5 18.3 %copy-start.27 = (u32[32]{0:T(128)S(1)}, u32[32]{0:T(128)}, u32[]{:S(2)}) copy-start(u32[32]{0:T(128)} %constant.105) | copy-start | bytes 388
  125.5 4.2 %collective-permute-start.12 = (f32[1,256]{1,0:T(1,128)S(1)}, f32[1,256]{1,0:T(1,128)S(1)}, u32[]{:S(2)}, u32[]{:S(2)}) collective-permute-start(f32[1,256]{1,0:T(1,128)S(1)} %get-tuple-element.42), channel_id=1, source_target_pairs={{0,4},{4,8},{8,12},{12,16},{16,20},{20,24},{24,28},{1,5},{5,9},{9,... | collective-permute-start | bytes 3080 | tf_op jit(solution)/shard_map/ppermute | solution.py:34
  128.5 5.5 %collective-permute-start.13 = (f32[1,256]{1,0:T(1,128)S(1)}, f32[1,256]{1,0:T(1,128)S(1)}, u32[]{:S(2)}, u32[]{:S(2)}) collective-permute-start(f32[1,256]{1,0:T(1,128)S(1)} %get-tuple-element.43), channel_id=1, source_target_pairs={{4,0},{8,4},{12,8},{16,12},{20,16},{24,20},{28,24},{5,1},{9,5},{13... | collective-permute-start | bytes 3080 | tf_op jit(solution)/shard_map/ppermute | solution.py:36
  134.0 4.7 %collective-permute-start.14 = (f32[66,1]{1,0:T(8,128)S(1)}, f32[66,1]{1,0:T(8,128)S(1)}, u32[]{:S(2)}, u32[]{:S(2)}) collective-permute-start(f32[66,1]{1,0:T(8,128)S(1)} %get-tuple-element.38), channel_id=1, source_target_pairs={{0,1},{1,2},{2,3},{4,5},{5,6},{6,7},{8,9},{9,10},{10,11},{12,13},{... | collective-permute-start | bytes 800 | tf_op jit(solution)/shard_map/ppermute | solution.py:34
  137.4 4.1 %collective-permute-start.15 = (f32[66,1]{1,0:T(8,128)S(1)}, f32[66,1]{1,0:T(8,128)S(1)}, u32[]{:S(2)}, u32[]{:S(2)}) collective-permute-start(f32[66,1]{1,0:T(8,128)S(1)} %get-tuple-element.39), channel_id=1, source_target_pairs={{1,0},{2,1},{3,2},{5,4},{6,5},{7,6},{9,8},{10,9},{11,10},{13,12},{... | collective-permute-start | bytes 800 | tf_op jit(solution)/shard_map/ppermute | solution.py:36
  143.1 107.3 %all-reduce.15.cloned.1.call-start = ((), (), s32[]{:S(2)}) async-start(), calls=%async_computation.1 | async-start | bytes 131072
  (23 other events, 103.9 us)
Sparse Core Ops, SparseCore 0:
  143.3 74.3 all-reduce.12
  220.0 30.3 all-reduce.14
where the time goes:
time: 261 us; the launch traced here: 259 us
  waiting for transfers between devices  111 us (43%)
  local copies, waits for them, and re-layouts  50 us (19%)
  starting transfers between devices  42.1 us (16%)
  other arithmetic  39.7 us (15%)
  between operations  15.5 us (6%)
    unnamed x4, waiting for transfers between devices  101 us
    ppermute x8, starting transfers between devices, shifted(): return lax.ppermute(block, axis, route)  22.3 us
    ppermute x4, starting transfers between devices, with_halo(): lax.ppermute(tail, axis, [(i, (i + 1) % count) for i in range(ends)])  14.5 us
    slice x12, local copies, waits for them, and re-layouts, step_next(): inner = lax.slice_in_dim(values, 1, values.shape[dim_index], axis=dim_index)  12.7 us
    another operation x4, other arithmetic, on_device(): jnp.stack([elec_x, elec_y, elec_z])  12.7 us
    unnamed x67, local copies, waits for them, and re-layouts  12.4 us
    sub x2, other arithmetic, on_device(): mag_x = damping * mag_x - coef_h * curl_x  8.14 us
    ppermute x4, waiting for transfers between devices, with_halo(): lax.ppermute(head, axis, [((i + 1) % count, i) for i in range(ends)])  6.93 us
  transfers between devices with their start and end apart: 18, of which 5 were waited for; matrix products, arithmetic and copies ran while one was open for 19% of the time, Pallas kernels for 0%

commit v1 on v0

v1 whole, which is shorter than its diff:
```python
import math

import jax
import jax.numpy as jnp
from jax import lax
from jax.experimental import pallas as pl
from jax.experimental.pallas import tpu as pltpu
from jax.sharding import PartitionSpec as P

PLANES = 2
ZLO = 3
STEPS = 2
FREQ = 4
PML = 12
TILE = 64
REPEAT = 4

courant = 0.5
sigma_peak = 0.8
dft_weight = 0.5
sharpness = 4.0
threshold = 0.5
eps_low = 2.1
eps_high = 12.1
grad_scale = 0.01

F32 = jnp.float32
LANES = 128
SUB = 8
GROUP = 16
ANY = pl.BlockSpec(memory_space=pl.ANY)
VMEM = pl.BlockSpec(memory_space=pltpu.VMEM)
SMEM = pl.BlockSpec(memory_space=pltpu.SMEM)


def params(mib=40):
    return pltpu.CompilerParams(vmem_limit_bytes=mib * 2**20)


def struct(*shape, dtype=F32):
    return jax.ShapeDtypeStruct(shape, dtype)


def cost(flops, moved):
    return pl.CostEstimate(flops=int(flops), bytes_accessed=int(moved), transcendentals=0)


def iota(shape, dim):
    return lax.broadcasted_iota(jnp.int32, shape, dim)


def in_design(z):
    return ZLO <= z < ZLO + PLANES


def turn(values, shift, axis):
    size = values.shape[axis]
    shift %= size
    return values if shift == 0 else pltpu.roll(values, shift, axis)


def depth_cubed(places, total):
    depth = jnp.maximum(jnp.maximum(PML - places, places - (total - 1 - PML)), 0.0) / PML
    return depth * depth * depth


def edge_coefs(rows, cols, total_x, total_y, inside=None):
    sigma = sigma_peak * (depth_cubed(rows, total_x) + depth_cubed(cols, total_y))
    inverse = 1.0 / (1.0 + 0.5 * sigma)
    if inside is not None:
        inverse = jnp.where(inside, inverse, 0.0)
    return (1.0 - 0.5 * sigma) * inverse, courant * inverse, inverse


def within(rows, cols, total_x, total_y):
    return (rows >= 0) & (rows < total_x) & (cols >= 0) & (cols < total_y)


def table_inverse(table, shape):
    return [courant / jnp.full(shape, table[k], F32) for k in range(table.shape[0])]


def pick(index, choices):
    out = jnp.zeros_like(choices[0])
    for k, choice in enumerate(choices):
        out = jnp.where(index == k, choice, out)
    return out


def design_terms(filtered):
    high = math.tanh(sharpness * threshold)
    norm = high + math.tanh(sharpness * (1.0 - threshold))
    bend = jnp.tanh(sharpness * (filtered - threshold))
    eps = eps_low + (eps_high - eps_low) * ((high + bend) / norm)
    return courant / eps, sharpness * (1.0 - bend * bend) / norm


def blur(values):
    rows, cols = values.shape
    summed = turn(values, 1, 0) + 2.0 * values + turn(values, rows - 1, 0)
    return (turn(summed, 1, 1) + 2.0 * summed + turn(summed, cols - 1, 1)) / 16.0


def id_row(tile_map, tx, shape):
    lane = iota(shape, len(shape) - 1)
    out = jnp.zeros(shape, F32)
    for t in range(tile_map.shape[1]):
        out = jnp.where(lane // TILE == t, (tile_map[tx, t] + 1).astype(F32), out)
    return out


def faces(fields, planes_z):
    return len(fields) * planes_z


def edge_copies(e_ref, h_ref, m_ref, d_ref, eb, hb, mb, db, sems):
    size = d_ref.shape[0]
    copies = []
    for side, start in enumerate((0, size - SUB)):
        rows = pl.ds(start, SUB)
        copies += [
            pltpu.make_async_copy(e_ref.at[:, :, rows, :], eb.at[side], sems.at[4 * side]),
            pltpu.make_async_copy(h_ref.at[:, :, rows, :], hb.at[side], sems.at[4 * side + 1]),
            pltpu.make_async_copy(m_ref.at[:, rows, :], mb.at[side], sems.at[4 * side + 2]),
            pltpu.make_async_copy(d_ref.at[rows, :], db.at[side], sems.at[4 * side + 3]),
        ]
    for copy in copies:
        copy.start()
    for copy in copies:
        copy.wait()


def edge_scratch(planes_z, width_y):
    return [
        pltpu.VMEM((2, 3, planes_z, SUB, width_y), F32),
        pltpu.VMEM((2, 3, planes_z, SUB, width_y), F32),
        pltpu.VMEM((2, planes_z, SUB, width_y), jnp.int32),
        pltpu.VMEM((2, SUB, width_y), F32),
        pltpu.SemaphoreType.DMA((8,)),
    ]


def edge_tile(side, q, planes_z, eb, hb, mb, db, ids):
    field, z = divmod(q, planes_z)
    if field < 3:
        return eb[side, field, z]
    if field < 6:
        return hb[side, field - 3, z]
    if field == 6:
        return db[side] if in_design(z) else mb[side, z].astype(F32)
    return ids


def n_faces(planes_z):
    return 7 * planes_z + 1


def pack_x(e_ref, h_ref, m_ref, d_ref, map_ref, a_ref, b_ref, eb, hb, mb, db, sems):
    planes_z, _, width_y = m_ref.shape
    edge_copies(e_ref, h_ref, m_ref, d_ref, eb, hb, mb, db, sems)
    even = lax.axis_index("gx") % 2 == 0
    last = map_ref.shape[0] - 1
    sub = iota((SUB, width_y), 0)
    ids = [id_row(map_ref, 0, (SUB, width_y)), id_row(map_ref, last, (SUB, width_y))]
    for group in range(a_ref.shape[0]):
        low = jnp.zeros((SUB, width_y), F32)
        high = low
        for k in range(4):
            q = 4 * group + k
            if q >= n_faces(planes_z):
                break
            mask = sub // 2 == k
            tile = edge_tile(0, q, planes_z, eb, hb, mb, db, ids[0])
            low = jnp.where(mask, turn(tile, 2 * k, 0), low)
            tile = edge_tile(1, q, planes_z, eb, hb, mb, db, ids[1])
            high = jnp.where(mask, turn(tile, 2 * k - 6, 0), high)
        a_ref[group] = jnp.where(even, high, low)
        b_ref[group] = jnp.where(even, low, high)


def halo_rows(a_ref, b_ref, q, even):
    group, k = divmod(q, 4)
    a, b = a_ref[group], b_ref[group]
    below = jnp.where(even, b, a)
    above = jnp.where(even, a, b)
    return turn(below, -2 * k, 0), turn(above, -2 * k, 0)


def to_strip(values, z, acc):
    lane = iota((values.shape[0], LANES), 1) - z * GROUP
    half = GROUP // 2
    low = turn(values[:, :LANES], z * GROUP + 2, 1)
    high = turn(values[:, -LANES:], z * GROUP + half - (LANES - half + 2), 1)
    acc = jnp.where((lane >= 2) & (lane < half), low, acc)
    return jnp.where((lane >= half) & (lane < GROUP - 2), high, acc)


def build_strips(e_ref, h_ref, m_ref, d_ref, map_ref, s_ref):
    planes_z, width_x, width_y = m_ref.shape
    zero = jnp.zeros((width_x, LANES), F32)

    def body(c, _):
        for base, ref in ((0, e_ref), (3, h_ref)):
            acc = zero
            for z in range(planes_z):
                acc = to_strip(ref[c, z], z, acc)
            s_ref[base + c] = acc
        return 0

    lax.fori_loop(0, 3, body, 0)
    acc = zero
    for z in range(planes_z):
        acc = to_strip(d_ref[...] if in_design(z) else m_ref[z].astype(F32), z, acc)
    s_ref[6] = acc
    for tx in range(width_x // TILE):
        rows = pl.ds(tx * TILE, TILE)
        row = id_row(map_ref, tx, (TILE, width_y))
        s_ref[7, rows] = to_strip(row, 0, jnp.zeros((TILE, LANES), F32))


def pack_y(s_ref, xa_ref, xb_ref, t_ref, a_ref, b_ref):
    planes_z = LANES // GROUP
    width_x = s_ref.shape[1]
    width_y = xa_ref.shape[2]
    even_x = lax.axis_index("gx") % 2 == 0
    even_y = lax.axis_index("gy") % 2 == 0
    sub = iota((SUB, width_y), 0)
    tails = []
    for f in range(8):
        acc = jnp.zeros((SUB, LANES), F32)
        for z in range(planes_z if f < 7 else 1):
            below, above = halo_rows(xa_ref, xb_ref, f * planes_z + z, even_x)
            halo = jnp.where(sub < 2, above, jnp.where(sub >= 6, turn(below, 6, 0), 0.0))
            acc = to_strip(halo, z, acc)
        t_ref[f] = acc
        tails.append(acc)
    for start in range(0, width_x + SUB, SUB):
        lane = iota((SUB, LANES), 1) % GROUP
        low = jnp.zeros((SUB, LANES), F32)
        high = low
        for f in range(8):
            values = tails[f] if start == width_x else s_ref[f, pl.ds(start, SUB)]
            mask = lane // 2 == f
            low = jnp.where(mask, turn(values, 2 * f - 2, 1), low)
            high = jnp.where(mask, turn(values, 2 * f - (GROUP - 4), 1), high)
        a_ref[pl.ds(start, SUB)] = jnp.where(even_y, high, low)
        b_ref[pl.ds(start, SUB)] = jnp.where(even_y, low, high)


def transform(adj_ref, fwd_ref, s_ref, g_ref):
    rows, cols = s_ref.shape
    total = jnp.zeros((rows, cols), F32)
    for c in range(3):
        for p in range(PLANES):
            parts = [None] * STEPS
            for f in range(FREQ):
                real = fwd_ref[f, 0, c, p].astype(F32)
                imag = fwd_ref[f, 1, c, p].astype(F32)
                total = total + (real * adj_ref[f, 0, c, p] - imag * adj_ref[f, 1, c, p])
                for n in range(STEPS):
                    angle = (0.21 + 0.06 * f) * (n + 1)
                    term = (dft_weight * math.cos(angle)) * real + (
                        dft_weight * math.sin(angle)
                    ) * imag
                    parts[n] = term if parts[n] is None else parts[n] + term
            for n in range(STEPS):
                g_ref[n, c, p] = parts[n]
    s_ref[...] = total


def interior(e_ref, h_ref, m_ref, d_ref, table, e2_ref, h2_ref, e1_ref, sl_ref, damp, ch, ce):
    planes_z, width_x, width_y = m_ref.shape
    gx, gy = lax.axis_index("gx"), lax.axis_index("gy")
    total_x, total_y = width_x * lax.axis_size("gx"), width_y * lax.axis_size("gy")
    shape = (width_x, width_y)
    rows = (iota(shape, 0) + gx * width_x).astype(F32)
    cols = (iota(shape, 1) + gy * width_y).astype(F32)
    damping, coef_h, inverse = edge_coefs(rows, cols, total_x, total_y)
    damp[...] = damping
    ch[...] = coef_h
    design, slope = design_terms(blur(d_ref[...]))
    sl_ref[...] = slope
    choices = table_inverse(table, (SUB, LANES))
    choices = [jnp.tile(c, (1, width_y // LANES)) for c in choices]
    for z in range(planes_z):
        if in_design(z):
            ce[z] = design * inverse
    for start in range(0, width_x, SUB):
        inv = inverse[start : start + SUB]
        for z in range(planes_z):
            if not in_design(z):
                ce[z, pl.ds(start, SUB)] = pick(m_ref[z, pl.ds(start, SUB)], choices) * inv

    def mag(src_e, src_h, z, last):
        for start in range(0, width_x, SUB):
            here = pl.ds(start, SUB)

            def ahead(c, tile):
                if start + SUB < width_x:
                    return src_e[c, z, pl.ds(start + 1, SUB)]
                return turn(tile, SUB - 1, 0)

            ex, ey, ez = (src_e[c, z, here] for c in range(3))
            up_x = -ex if last else src_e[0, z + 1, here] - ex
            up_y = -ey if last else src_e[1, z + 1, here] - ey
            cx = (turn(ez, width_y - 1, 1) - ez) - up_y
            cy = up_x - (ahead(2, ez) - ez)
            cz = (ahead(1, ey) - ey) - (turn(ex, width_y - 1, 1) - ex)
            dm, cf = damp[here], ch[here]
            for c, curl in enumerate((cx, cy, cz)):
                h2_ref[c, z, here] = dm * src_h[c, z, here] - cf * curl

    def elec(src_e, z, first):
        for start in range(0, width_x, SUB):
            here = pl.ds(start, SUB)

            def behind(c, tile):
                if start:
                    return h2_ref[c, z, pl.ds(start - 1, SUB)]
                return turn(tile, 1, 0)

            hx, hy, hz = (h2_ref[c, z, here] for c in range(3))
            up_x = hx if first else hx - h2_ref[0, z - 1, here]
            up_y = hy if first else hy - h2_ref[1, z - 1, here]
            cx = (hz - turn(hz, 1, 1)) - up_y
            cy = up_x - (hz - behind(2, hz))
            cz = (hy - behind(1, hy)) - (hx - turn(hx, 1, 1))
            dm, cf = damp[here], ce[z, here]
            for c, curl in enumerate((cx, cy, cz)):
                e2_ref[c, z, here] = dm * src_e[c, z, here] + cf * curl

    def loop(lo, hi, f):
        lax.fori_loop(lo, hi, lambda z, _: (f(z), 0)[1], 0)

    for n in range(STEPS):
        src_e, src_h = (e_ref, h_ref) if n == 0 else (e2_ref, h2_ref)
        loop(0, planes_z - 1, lambda z: mag(src_e, src_h, z, False))
        mag(src_e, src_h, planes_z - 1, True)
        elec(src_e, 0, True)
        loop(1, planes_z, lambda z: elec(src_e, z, False))
        if n == 0:
            for c in range(3):
                for p in range(PLANES):
                    e1_ref[c, p] = e2_ref[c, ZLO + p]


def strips_x(
    e_ref, h_ref, m_ref, d_ref, table, xa_ref, xb_ref,
    e2_ref, h2_ref, e1_ref, sl_ref, eb, hb, mb, db, sems, xe, xh, ce,
):
    planes_z, width_x, width_y = m_ref.shape
    edge_copies(e_ref, h_ref, m_ref, d_ref, eb, hb, mb, db, sems)
    gx, gy = lax.axis_index("gx"), lax.axis_index("gy")
    total_x, total_y = width_x * lax.axis_size("gx"), width_y * lax.axis_size("gy")
    even = gx % 2 == 0
    shape = (SUB, width_y)
    sub = iota(shape, 0)
    cols = (iota(shape, 1) + gy * width_y).astype(F32)
    choices = [jnp.tile(c, (1, width_y // LANES)) for c in table_inverse(table, (SUB, LANES))]
    zero = jnp.zeros(shape, F32)
    damps, chs = [], []

    def strip(side, q):
        below, above = halo_rows(xa_ref, xb_ref, q, even)
        own = edge_tile(side, q, planes_z, eb, hb, mb, db, None)
        if side == 0:
            return jnp.where(sub < 2, below, turn(own, 2, 0))
        return jnp.where(sub >= 6, turn(above, 6, 0), turn(own, 6, 0))

    for side in range(2):
        rows = (sub + gx * width_x + (-2 if side == 0 else width_x - 6)).astype(F32)
        inside = within(rows, cols, total_x, total_y)
        damping, coef_h, inverse = edge_coefs(rows, cols, total_x, total_y, inside)
        damps.append(damping)
        chs.append(coef_h)
        for z in range(planes_z):
            for c in range(3):
                xe[side, c, z] = strip(side, c * planes_z + z)
                xh[side, c, z + 1] = strip(side, (3 + c) * planes_z + z)
        for c in range(3):
            xe[side, c, planes_z] = zero
            xh[side, c, 0] = zero
        design, slope = design_terms(blur(strip(side, 6 * planes_z + ZLO)))
        sl_ref[side] = turn(slope, 6 if side == 0 else 2, 0)
        for z in range(planes_z):
            if in_design(z):
                ce[side, z] = design * inverse
            else:
                ce[side, z] = pick(strip(side, 6 * planes_z + z), choices) * inverse

    def mag(z):
        for side in range(2):
            ex, ey, ez = (xe[side, c, z] for c in range(3))
            cx = (turn(ez, width_y - 1, 1) - ez) - (xe[side, 1, z + 1] - ey)
            cy = (xe[side, 0, z + 1] - ex) - (turn(ez, SUB - 1, 0) - ez)
            cz = (turn(ey, SUB - 1, 0) - ey) - (turn(ex, width_y - 1, 1) - ex)
            for c, curl in enumerate((cx, cy, cz)):
                xh[side, c, z + 1] = damps[side] * xh[side, c, z + 1] - chs[side] * curl

    def elec(z):
        for side in range(2):
            hx, hy, hz = (xh[side, c, z + 1] for c in range(3))
            cx = (hz - turn(hz, 1, 1)) - (hy - xh[side, 1, z])
            cy = (hx - xh[side, 0, z]) - (hz - turn(hz, 1, 0))
            cz = (hy - turn(hy, 1, 0)) - (hx - turn(hx, 1, 1))
            for c, curl in enumerate((cx, cy, cz)):
                xe[side, c, z] = damps[side] * xe[side, c, z] + ce[side, z] * curl

    def loop(f):
        lax.fori_loop(0, planes_z, lambda z, _: (f(z), 0)[1], 0)

    back = (6, 2)
    for n in range(STEPS):
        loop(mag)
        loop(elec)
        if n == 0:
            for side in range(2):
                for c in range(3):
                    for p in range(PLANES):
                        e1_ref[c, p, side] = turn(xe[side, c, ZLO + p], back[side], 0)

    def finish(z):
        for side in range(2):
            for c in range(3):
                e2_ref[c, z, side] = turn(xe[side, c, z], back[side], 0)
                h2_ref[c, z, side] = turn(xh[side, c, z + 1], back[side], 0)

    loop(finish)


def patch_rows(values, strip, start, width_x):
    sub = iota(values.shape, 0)
    if start == 0:
        values = jnp.where(sub < 2, strip[0], values)
    if start == width_x - SUB:
        values = jnp.where(sub >= 6, strip[1], values)
    return values


def patch_cols(values, strip, z):
    lane = iota((values.shape[0], LANES), 1)
    low = turn(strip, -(z * GROUP + 2), 1)
    high = turn(strip, LANES - 2 - (z * GROUP + GROUP - 4), 1)
    tiles = [values[:, k : k + LANES] for k in range(0, values.shape[1], LANES)]
    tiles[0] = jnp.where(lane < 2, low, tiles[0])
    tiles[-1] = jnp.where(lane >= LANES - 2, high, tiles[-1])
    return jnp.concatenate(tiles, axis=1)


def strips_y(width_x, width_y, s_ref, t_ref, ya_ref, yb_ref, table):
    gx, gy = lax.axis_index("gx"), lax.axis_index("gy")
    total_x, total_y = width_x * lax.axis_size("gx"), width_y * lax.axis_size("gy")
    planes_z = LANES // GROUP
    even = gy % 2 == 0
    size = width_x + SUB
    shape = (size, LANES)
    lane = iota(shape, 1)
    col = lane % GROUP
    plane = lane // GROUP
    from_low = jnp.where(even, yb_ref[...], ya_ref[...])
    from_high = jnp.where(even, ya_ref[...], yb_ref[...])

    def field(f):
        own = jnp.concatenate([s_ref[f], t_ref[f]], axis=0)
        own = jnp.where(col < 2, turn(from_low, -2 * f, 1), own)
        return jnp.where(col >= GROUP - 2, turn(from_high, GROUP - 2 - 2 * f, 1), own)

    row = iota(shape, 0)
    row = jnp.where(row >= width_x + 4, row - size, row)
    place = jnp.where(col < GROUP // 2, col - 2, col + (width_y - GROUP + 2))
    rows = (row + gx * width_x).astype(F32)
    cols = (place + gy * width_y).astype(F32)
    inside = within(rows, cols, total_x, total_y)
    damping, coef_h, inverse = edge_coefs(rows, cols, total_x, total_y, inside)
    source = field(6)
    design, slope = design_terms(blur(source))
    choices = [jnp.tile(c, (size // SUB, 1)) for c in table_inverse(table, (SUB, LANES))]
    layer = (plane >= ZLO) & (plane < ZLO + PLANES)
    coef_e = jnp.where(layer, design, pick(source, choices)) * inverse
    e = [field(c) for c in range(3)]
    h = [field(3 + c) for c in range(3)]
    top = plane == planes_z - 1
    bottom = plane == 0

    def dxf(v):
        return turn(v, size - 1, 0) - v

    def dyf(v):
        return turn(v, LANES - 1, 1) - v

    def dzf(v):
        return jnp.where(top, 0.0, turn(v, LANES - GROUP, 1)) - v

    def dxb(v):
        return v - turn(v, 1, 0)

    def dyb(v):
        return v - turn(v, 1, 1)

    def dzb(v):
        return v - jnp.where(bottom, 0.0, turn(v, GROUP, 1))

    steps = []
    for _ in range(STEPS):
        curl = (dyf(e[2]) - dzf(e[1]), dzf(e[0]) - dxf(e[2]), dxf(e[1]) - dyf(e[0]))
        h = [damping * v - coef_h * c for v, c in zip(h, curl)]
        curl = (dyb(h[2]) - dzb(h[1]), dzb(h[0]) - dxb(h[2]), dxb(h[1]) - dyb(h[0]))
        e = [damping * v + coef_e * c for v, c in zip(e, curl)]
        steps.append(e)
    return steps, h, slope, field(7)


def scalar_of(values, sub, lane):
    here = (iota(values.shape, 0) == sub) & (iota(values.shape, 1) == lane)
    return jnp.max(jnp.where(here, values, 0.0)).astype(jnp.int32)


def slot_of(param, rows_mine):
    gx, gy = lax.axis_index("gx"), lax.axis_index("gy")
    count_gx, count_gy = lax.axis_size("gx"), lax.axis_size("gy")
    owner = lax.div(param, jnp.int32(rows_mine))
    row = param - owner * rows_mine
    ox = lax.div(owner, jnp.int32(count_gy))
    oy = owner - ox * count_gy
    core = (oy ^ gy) & 1
    near = ((ox & 1) + 2 * (oy >> 1)) ^ ((gx & 1) + 2 * (gy >> 1))
    far = (ox >> 1) ^ (gx >> 1)
    return ((core * count_gy + near) * (count_gx // 2) + far) * rows_mine + row


def gradient(
    s_ref, t_ref, ya_ref, yb_ref, xa_ref, xb_ref, table, map_ref, e1_ref, e2_ref, xe1_ref, xe2_ref,
    sl_ref, xsl_ref, sum_ref, g_ref, buf_ref, ye_ref, yh_ref, ye1, lpad, vpad, gpad,
):
    width_x, width_y = sl_ref.shape
    planes_z = LANES // GROUP
    steps, h, slope_y, ids_y = strips_y(width_x, width_y, s_ref, t_ref, ya_ref, yb_ref, table)
    for c in range(3):
        ye_ref[c] = steps[-1][c]
        yh_ref[c] = h[c]
        ye1[c] = steps[0][c]
    ye1[3] = slope_y
    pad = 2 * SUB
    lpad[pl.ds(0, pad)] = jnp.zeros((pad, width_y), F32)
    lpad[pl.ds(pad + width_x, pad)] = jnp.zeros((pad, width_y), F32)
    buf_ref[...] = jnp.zeros(buf_ref.shape, F32)
    for start in range(0, width_x, SUB):
        here = pl.ds(start, SUB)
        total = sum_ref[here]
        for c in range(3):
            for p in range(PLANES):
                first = patch_rows(e1_ref[c, p, here], xe1_ref.at[c, p], start, width_x)
                first = patch_cols(first, ye1[c, here], ZLO + p)
                second = patch_rows(e2_ref[c, ZLO + p, here], xe2_ref.at[c, ZLO + p], start, width_x)
                second = patch_cols(second, ye_ref[c, here], ZLO + p)
                total = total + g_ref[0, c, p, here] * first + g_ref[1, c, p, here] * second
        slope = patch_rows(sl_ref[here], xsl_ref, start, width_x)
        slope = patch_cols(slope, ye1[3, here], ZLO)
        lpad[pl.ds(pad + start, SUB)] = (grad_scale * (eps_high - eps_low)) * slope * total
    lane = iota((SUB, width_y), 1)
    for start in range(SUB, pad + width_x + SUB, SUB):
        v = lpad[pl.ds(start - 1, SUB)] + 2.0 * lpad[pl.ds(start, SUB)] + lpad[pl.ds(start + 1, SUB)]
        v = v / 16.0
        left = jnp.where(lane == 0, 0.0, turn(v, 1, 1))
        right = jnp.where(lane == width_y - 1, 0.0, turn(v, width_y - 1, 1))
        g = left + 2.0 * v + right
        for u in range(width_y // LANES):
            vpad[u, pl.ds(start, SUB)] = v[:, u * LANES : (u + 1) * LANES]
            gpad[u, pl.ds(start, SUB)] = g[:, u * LANES : (u + 1) * LANES]

    half = LANES // 2
    lines = TILE // 2
    tiles_x, tiles_y = width_x // TILE, width_y // TILE
    devices = lax.axis_size("gx") * lax.axis_size("gy")
    rows_mine = buf_ref.shape[0] // devices
    lane = iota((lines, LANES), 1)
    lane8 = iota((SUB, LANES), 1)
    sub8 = iota((SUB, LANES), 0)

    def add_tile(param, values):
        slot = slot_of(param, rows_mine)
        buf_ref[slot] = buf_ref[slot] + values

    def add_rows(ident, start, values):
        slot = slot_of(jnp.maximum(ident - 1, 0), rows_mine)
        rows = pl.ds(start, SUB)
        buf_ref[slot, rows] = buf_ref[slot, rows] + jnp.where(ident > 0, values, 0.0)

    for tx in range(tiles_x):
        for u in range(width_y // LANES):
            even = gpad[u, pl.ds(pad + tx * TILE, lines, stride=2)]
            odd = gpad[u, pl.ds(pad + tx * TILE + 1, lines, stride=2)]
            add_tile(map_ref[tx, 2 * u], jnp.where(lane < half, even, turn(odd, half, 1)))
            add_tile(map_ref[tx, 2 * u + 1], jnp.where(lane < half, turn(even, half, 1), odd))
    even_x = lax.axis_index("gx") % 2 == 0
    below, above = halo_rows(xa_ref, xb_ref, 7 * planes_z, even_x)
    before, after = pl.ds(pad - SUB, SUB), pl.ds(pad + width_x, SUB)
    for t in range(tiles_y):
        u, odd = divmod(t, 2)
        top, low = gpad[u, before], gpad[u, after]
        top = top if odd else turn(top, half, 1)
        low = turn(low, half, 1) if odd else low
        keep = (sub8 == SUB - 1) & (lane8 >= half)
        add_rows(scalar_of(below, 0, t * TILE), lines - SUB, jnp.where(keep, top, 0.0))
        keep = (sub8 == 0) & (lane8 < half)
        add_rows(scalar_of(above, 0, t * TILE), 0, jnp.where(keep, low, 0.0))
    end = width_y // LANES - 1
    for tx in range(tiles_x):
        ids = ids_y[tx * TILE : tx * TILE + SUB]
        even, odd = (pl.ds(pad + tx * TILE + k, lines, stride=2) for k in (0, 1))
        left = jnp.where(lane == half - 1, turn(vpad[0, even], half - 1, 1), 0.0)
        left = jnp.where(lane == LANES - 1, turn(vpad[0, odd], LANES - 1, 1), left)
        right = jnp.where(lane == 0, turn(vpad[end, even], 1, 1), 0.0)
        right = jnp.where(lane == half, turn(vpad[end, odd], half + 1, 1), right)
        for column, values in ((0, left), (GROUP - 1, right)):
            ident = scalar_of(ids, 0, column)
            add_tile(jnp.maximum(ident - 1, 0), jnp.where(ident > 0, values, 0.0))
    tail = ids_y[width_x : width_x + SUB]
    corners = (
        (SUB - 1, 0, before, 0, lines - SUB, LANES - 1),
        (SUB - 1, GROUP - 1, before, end, lines - SUB, half),
        (0, 0, after, 0, 0, half - 1),
        (0, GROUP - 1, after, end, 0, 0),
    )
    for sub, column, rows, u, start, target in corners:
        source = LANES - 1 if u == end and column else 0
        keep = (sub8 == sub) & (lane8 == target)
        values = jnp.where(keep, turn(vpad[u, rows], target - source, 1), 0.0)
        add_rows(scalar_of(tail, sub, column), start, values)


def merge(e_ref, h_ref, xe_ref, xh_ref, ye_ref, yh_ref, eo_ref, ho_ref):
    _, planes_z, width_x, _ = e_ref.shape
    for src, xs, ys, out in ((e_ref, xe_ref, ye_ref, eo_ref), (h_ref, xh_ref, yh_ref, ho_ref)):
        for z in range(planes_z):
            for start in range(0, width_x, SUB):
                here = pl.ds(start, SUB)
                values = patch_rows(src[0, z, here], xs.at[0, z], start, width_x)
                out[0, z, here] = patch_cols(values, ys[0, here], z)


def first_sum(parts, buf_ref, got_ref, *outs):
    size = outs[0].shape[0]
    for k in range(parts):
        rows = pl.ds(k * size, size)
        outs[k][...] = buf_ref[rows] + got_ref[rows]


def second_sum(parts, rows_mine, *refs):
    ins, outs = refs[:parts], refs[parts:]
    for k, out in enumerate(outs):
        rows = pl.ds(k * rows_mine, rows_mine)
        out[...] = sum(ref[rows] for ref in ins[1:]) + ins[0][rows]


def pair(block, partner):
    count_gx, count_gy = lax.axis_size("gx"), lax.axis_size("gy")
    route = []
    for i in range(count_gx):
        for j in range(count_gy):
            a, b = partner(i, j)
            if 0 <= a < count_gx and 0 <= b < count_gy:
                route.append((i * count_gy + j, a * count_gy + b))
    return lax.ppermute(block, ("gx", "gy"), route)


def on_device(e_adj, h_adj, density, material, eps_table, dft_adj, dft_fwd, tile_map):
    planes_z, width_x, width_y = material.shape
    count_gx, count_gy = lax.axis_size("gx"), lax.axis_size("gy")
    block = 4 * width_x * width_y
    groups = -(-n_faces(planes_z) // 4)
    face = struct(groups, SUB, width_y)
    xa, xb = pl.pallas_call(
        pack_x,
        out_shape=(face, face),
        in_specs=[ANY, ANY, ANY, ANY, SMEM],
        out_specs=(VMEM, VMEM),
        scratch_shapes=edge_scratch(planes_z, width_y),
        compiler_params=params(),
        name="pack_x",
    )(e_adj, h_adj, material, density, tile_map)
    xa = pair(xa, lambda i, j: (i ^ 1, j))
    xb = pair(xb, lambda i, j: (((i + 1) ^ 1) - 1, j))

    rows = 2 * SUB
    moved = struct(width_x, width_y), struct(STEPS, 3, PLANES, width_x, width_y)
    base, weight = pl.pallas_call(
        transform,
        grid=(width_x // rows,),
        out_shape=moved,
        in_specs=[pl.BlockSpec((FREQ, 2, 3, PLANES, rows, width_y), lambda i: (0, 0, 0, 0, i, 0))] * 2,
        out_specs=(
            pl.BlockSpec((rows, width_y), lambda i: (i, 0)),
            pl.BlockSpec((STEPS, 3, PLANES, rows, width_y), lambda i: (0, 0, 0, i, 0)),
        ),
        compiler_params=params(),
        cost_estimate=cost(48 * 8 * width_x * width_y, 85 * block),
        name="transform",
    )(dft_adj, dft_fwd)
    strip = pl.pallas_call(
        build_strips,
        out_shape=struct(8, width_x, LANES),
        in_specs=[VMEM] * 4 + [SMEM],
        out_specs=VMEM,
        compiler_params=params(),
        cost_estimate=cost(48 * 4 * width_x * width_y, 60 * block),
        name="build_strips",
    )(e_adj, h_adj, material, density, tile_map)
    e2, h2, e1, slope = pl.pallas_call(
        interior,
        out_shape=(
            struct(3, planes_z, width_x, width_y),
            struct(3, planes_z, width_x, width_y),
            struct(3, PLANES, width_x, width_y),
            struct(width_x, width_y),
        ),
        in_specs=[VMEM] * 4 + [SMEM],
        out_specs=(VMEM,) * 4,
        scratch_shapes=[
            pltpu.VMEM((width_x, width_y), F32),
            pltpu.VMEM((width_x, width_y), F32),
            pltpu.VMEM((planes_z, width_x, width_y), F32),
        ],
        compiler_params=params(),
        cost_estimate=cost(100 * planes_z * width_x * width_y, 110 * block),
        name="interior",
    )(e_adj, h_adj, material, density, eps_table)

    tails, ya, yb = pl.pallas_call(
        pack_y,
        out_shape=(struct(8, SUB, LANES),) + (struct(width_x + SUB, LANES),) * 2,
        in_specs=[VMEM] * 3,
        out_specs=(VMEM,) * 3,
        compiler_params=params(),
        name="pack_y",
    )(strip, xa, xb)
    ya = pair(ya, lambda i, j: (i, j ^ 1))
    yb = pair(yb, lambda i, j: (i, ((j + 1) ^ 1) - 1))
    xe2, xh2, xe1, xslope = pl.pallas_call(
        strips_x,
        out_shape=(
            struct(3, planes_z, 2, SUB, width_y),
            struct(3, planes_z, 2, SUB, width_y),
            struct(3, PLANES, 2, SUB, width_y),
            struct(2, SUB, width_y),
        ),
        in_specs=[ANY, ANY, ANY, ANY, SMEM, VMEM, VMEM],
        out_specs=(VMEM,) * 4,
        scratch_shapes=edge_scratch(planes_z, width_y)
        + [
            pltpu.VMEM((2, 3, planes_z + 1, SUB, width_y), F32),
            pltpu.VMEM((2, 3, planes_z + 1, SUB, width_y), F32),
            pltpu.VMEM((2, planes_z, SUB, width_y), F32),
        ],
        compiler_params=params(),
        cost_estimate=cost(30 * planes_z * width_x * width_y, 30 * block),
        name="strips_x",
    )(e_adj, h_adj, material, density, eps_table, xa, xb)

    devices = count_gx * count_gy
    rows_mine = (width_x // TILE) * (width_y // TILE) // REPEAT
    lines = TILE // 2
    padded = width_x + 4 * SUB
    buf, ye2, yh2 = pl.pallas_call(
        gradient,
        out_shape=(struct(devices * rows_mine, lines, LANES),)
        + (struct(3, width_x + SUB, LANES),) * 2,
        in_specs=[VMEM] * 6 + [SMEM] * 2 + [VMEM] * 8,
        out_specs=(VMEM,) * 3,
        scratch_shapes=[
            pltpu.VMEM((4, width_x + SUB, LANES), F32),
            pltpu.VMEM((padded, width_y), F32),
            pltpu.VMEM((width_y // LANES, padded, LANES), F32),
            pltpu.VMEM((width_y // LANES, padded, LANES), F32),
        ],
        compiler_params=params(),
        cost_estimate=cost(60 * width_x * width_y, 30 * block),
        name="gradient",
    )(strip, tails, ya, yb, xa, xb, eps_table, tile_map, e1, e2, xe1, xe2, slope, xslope, base, weight)

    half = devices * rows_mine // 2
    far = count_gx // 2
    got = pair(buf[half:], lambda i, j: (i, j ^ 1))
    parts = pl.pallas_call(
        lambda *refs: first_sum(count_gy, *refs),
        out_shape=(struct(far * rows_mine, lines, LANES),) * count_gy,
        in_specs=[VMEM] * 2,
        out_specs=(VMEM,) * count_gy,
        compiler_params=params(),
        name="first_sum",
    )(buf, got)
    parts = [parts[0]] + [
        pair(parts[k], lambda i, j: (i ^ (k & 1), j ^ (k >> 1 << 1))) for k in range(1, count_gy)
    ]
    parts = pl.pallas_call(
        lambda *refs: second_sum(count_gy, rows_mine, *refs),
        out_shape=(struct(rows_mine, lines, LANES),) * far,
        in_specs=[VMEM] * count_gy,
        out_specs=(VMEM,) * far,
        compiler_params=params(),
        name="second_sum",
    )(*parts)
    parts = [parts[0]] + [pair(parts[k], lambda i, j: (i ^ (k << 1), j)) for k in range(1, far)]
    param_grad = sum(parts[1:], parts[0]).reshape(rows_mine, TILE * TILE)

    whole = pl.BlockSpec((1, planes_z, width_x, width_y), lambda c: (c, 0, 0, 0))
    edge = pl.BlockSpec((1, planes_z, 2, SUB, width_y), lambda c: (c, 0, 0, 0, 0))
    side = pl.BlockSpec((1, width_x + SUB, LANES), lambda c: (c, 0, 0))
    e_out, h_out = pl.pallas_call(
        merge,
        grid=(3,),
        out_shape=(struct(3, planes_z, width_x, width_y),) * 2,
        in_specs=[whole, whole, edge, edge, side, side],
        out_specs=(whole, whole),
        compiler_params=params(),
        cost_estimate=cost(48 * 4 * width_x * width_y, 110 * block),
        name="merge",
    )(e2, h2, xe2, xh2, ye2, yh2)
    return e_out, h_out, param_grad


def solution(mesh):
    in_specs = (
        P(None, None, "gx", "gy"),
        P(None, None, "gx", "gy"),
        P("gx", "gy"),
        P(None, "gx", "gy"),
        P(),
        P(None, None, None, None, "gx", "gy"),
        P(None, None, None, None, "gx", "gy"),
        P("gx", "gy"),
    )
    out_specs = (P(None, None, "gx", "gy"), P(None, None, "gx", "gy"), P(("gx", "gy"), None))
    return jax.shard_map(
        on_device, mesh=mesh, in_specs=in_specs, out_specs=out_specs, check_vma=False
    )
```

time: 261 us -> 50.7 us (0.19)
  waiting for transfers between devices: 111 us -> 7.75 us
  local copies, waits for them, and re-layouts: 50 us -> 5.4 us
  other arithmetic: 39.7 us -> 0.61 us
  starting transfers between devices: 42.1 us -> 19.4 us
  Pallas kernels: 0 us -> 16.4 us
  between operations: 15.5 us -> 0.84 us
    unnamed x4 -> x0, waiting for transfers between devices: 101 us -> none
    slice x42 -> x1, local copies, waits for them, and re-layouts: 29.6 us -> 0.02 us  [on_device(): got = pair(buf[half:], lambda i, j: (i, j ^ 1))]
    ppermute x16 -> x11, starting transfers between devices: 42 us -> 19.4 us  [pair(): return lax.ppermute(block, ('gx', 'gy'), route)]
    pallas_call x0 -> x10, Pallas kernels: none -> 16.4 us  [the longest x1 4.3 us: on_device(): pl.pallas_call(interior, out_shape=(struct(3, planes_z, width_x, width_y)...]
    another operation x16 -> x0, other arithmetic: 15 us -> none  [the longest x4 12.7 us: on_device(): jnp.stack([elec_x, elec_y, elec_z])]
    add x8 -> x1, other arithmetic: 13.4 us -> 0.61 us  [on_device(): param_grad = sum(parts[1:], parts[0]).reshape(rows_mine, TILE * TILE)]
    sub x2 -> x0, other arithmetic: 8.14 us -> none  [on_device(): mag_x = damping * mag_x - coef_h * curl_x]
    squeeze x16 -> x0, local copies, waits for them, and re-layouts: 7.76 us -> none  [the longest x4 2.47 us: curl_forward(): ahead_y[1]]
  transfers between devices with their start and end apart: 18 -> 11, of which waited for: 5 -> 7; matrix products, arithmetic and copies ran while one was open for 19% -> 0% of each run, Pallas kernels for 0% -> 27%
where the time goes in v1:
time: 50.7 us; the launch traced here: 50.4 us
  starting transfers between devices  19.4 us (38%)
  Pallas kernels  16.4 us (32%)
  waiting for transfers between devices  7.75 us (15%)
  local copies, waits for them, and re-layouts  5.4 us (11%)
  between operations  0.84 us (2%)
  other arithmetic  0.61 us (1%)
    ppermute x11, starting transfers between devices, pair(): return lax.ppermute(block, ('gx', 'gy'), route)  19.4 us
    ppermute x11, waiting for transfers between devices, pair(): return lax.ppermute(block, ('gx', 'gy'), route)  7.75 us
    unnamed x22, local copies, waits for them, and re-layouts  5.38 us
    pallas_call x1, Pallas kernels, on_device(): pl.pallas_call(interior, out_shape=(struct(3, planes_z, width_x, width_y)...  4.3 us
    pallas_call x1, Pallas kernels, on_device(): pl.pallas_call(strips_x, out_shape=(struct(3, planes_z, 2, SUB, width_y),...  3.64 us
    pallas_call x1, Pallas kernels, on_device(): pl.pallas_call(merge, grid=(3,), out_shape=(struct(3, planes_z, width_x,...  2.45 us
    pallas_call x1, Pallas kernels, on_device(): pl.pallas_call(gradient, out_shape=(struct(devices * rows_mine, lines, LA...  1.81 us
    pallas_call x1, Pallas kernels, on_device(): pl.pallas_call(build_strips, out_shape=struct(8, width_x, LANES), in_spec...  1.75 us
  transfers between devices with their start and end apart: 11, of which 7 were waited for; matrix products, arithmetic and copies ran while one was open for 0% of the time, Pallas kernels for 27%

profile of v1, /device:TPU:0, one launch (start us, length us, event | category | flops | bytes accessed | tf_op | source)
XLA Modules:
  0.0 50.4 jit_solution(15138273973147874572)
XLA Ops:
  0.6 1.4 %copy-done = f32[3,8,64,256]{3,2,1,0:T(8,128)S(1)} copy-done((f32[3,8,64,256]{3,2,1,0:T(8,128)S(1)}, f32[3,8,64,256]{3,2,1,0:T(8,128)}, u32[]{:S(2)}) %copy-start) | copy-done | bytes 1572888
  2.0 1.4 %copy-done.2 = f32[3,8,64,256]{3,2,1,0:T(8,128)S(1)} copy-done((f32[3,8,64,256]{3,2,1,0:T(8,128)S(1)}, f32[3,8,64,256]{3,2,1,0:T(8,128)}, u32[]{:S(2)}) %copy-start.2) | copy-done | bytes 1572888
  3.5 1.0 %copy-done.4 = s32[8,64,256]{2,1,0:T(8,128)S(1)} copy-done((s32[8,64,256]{2,1,0:T(8,128)S(1)}, s32[8,64,256]{2,1,0:T(8,128)}, u32[]{:S(2)}) %copy-start.4) | copy-done | bytes 524312
  4.5 0.8 %copy-done.8 = f32[64,256]{1,0:T(8,128)S(1)} copy-done((f32[64,256]{1,0:T(8,128)S(1)}, f32[64,256]{1,0:T(8,128)}, u32[]{:S(2)}) %copy-start.8) | copy-done | bytes 65560
  6.0 0.9 %pack_x.1 = (f32[15,8,256]{2,1,0:T(8,128)S(1)}, f32[15,8,256]{2,1,0:T(8,128)S(1)}) custom-call(f32[3,8,64,256]{3,2,1,0:T(8,128)S(1)} %copy-done, f32[3,8,64,256]{3,2,1,0:T(8,128)S(1)} %copy-done.2, s32[8,64,256]{2,1,0:T(8,128)S(1)} %copy-done.4, f32[64,256]{1,0:T(8,128)S(1)} %copy-done.8, s32[1,4]{1,0:T(1,128)S(1)} %copy-done.10), custom_call_target="tpu_custom_call" | custom-call | tf_op jit(solution)/shard_map/pack_x/pallas_call | solution.py:673
  6.8 3.0 %collective-permute-start = (f32[15,8,256]{2,1,0:T(8,128)S(1)}, f32[15,8,256]{2,1,0:T(8,128)S(1)}, u32[]{:S(2)}, u32[]{:S(2)}) collective-permute-start(f32[15,8,256]{2,1,0:T(8,128)S(1)} %get-tuple-element.33), channel_id=1, source_target_pairs={{0,4},{1,5},{2,6},{3,7},{4,0},{5,1},{6,2},{7,3},{8,12},{9,13},{10,... | collective-permute-start | bytes 368648 | tf_op jit(solution)/shard_map/ppermute | solution.py:664
  9.9 0.8 %collective-permute-start.1 = (f32[15,8,256]{2,1,0:T(8,128)S(1)}, f32[15,8,256]{2,1,0:T(8,128)S(1)}, u32[]{:S(2)}, u32[]{:S(2)}) collective-permute-start(f32[15,8,256]{2,1,0:T(8,128)S(1)} %get-tuple-element.34), channel_id=1, source_target_pairs={{4,8},{5,9},{6,10},{7,11},{8,4},{9,5},{10,6},{11,7},{12,16},{13,17... | collective-permute-start | bytes 368648 | tf_op jit(solution)/shard_map/ppermute | solution.py:664
  10.7 1.8 %build_strips.1.s_ref = f32[8,64,128]{2,1,0:T(8,128)S(1)} custom-call(f32[3,8,64,256]{3,2,1,0:T(8,128)S(1)} %copy-done, f32[3,8,64,256]{3,2,1,0:T(8,128)S(1)} %copy-done.2, s32[8,64,256]{2,1,0:T(8,128)S(1)} %copy-done.4, f32[64,256]{1,0:T(8,128)S(1)} %copy-done.8, s32[1,4]{1,0:T(1,128)S(1)} %copy-done.10), custom_call_target="tpu_custom_call" | custom-call | flops 3145728 | bytes 3932160 | tf_op jit(solution)/shard_map/build_strips/pallas_call | solution.py:700
  12.4 0.8 %collective-permute-done.xa_ref = f32[15,8,256]{2,1,0:T(8,128)S(1)} collective-permute-done((f32[15,8,256]{2,1,0:T(8,128)S(1)}, f32[15,8,256]{2,1,0:T(8,128)S(1)}, u32[]{:S(2)}, u32[]{:S(2)}) %collective-permute-start) | collective-permute-done | bytes 122912 | tf_op jit(solution)/shard_map/ppermute | solution.py:664
  13.7 0.8 %collective-permute-start.3 = (f32[72,128]{1,0:T(8,128)S(1)}, f32[72,128]{1,0:T(8,128)S(1)}, u32[]{:S(2)}, u32[]{:S(2)}) collective-permute-start(f32[72,128]{1,0:T(8,128)S(1)} %get-tuple-element.39), channel_id=1, source_target_pairs={{1,2},{2,1},{5,6},{6,5},{9,10},{10,9},{13,14},{14,13},{17,18},{18,... | collective-permute-start | bytes 110600 | tf_op jit(solution)/shard_map/ppermute | solution.py:664
  14.5 1.3 %transform.1 = (f32[64,256]{1,0:T(8,128)S(1)}, f32[2,3,2,64,256]{4,3,2,1,0:T(8,128)S(1)}) custom-call(f32[4,2,3,2,64,256]{5,4,3,2,1,0:T(8,128)S(1)} %copy-done.6, bf16[4,2,3,2,64,256]{5,4,3,2,1,0:T(8,128)(2,1)S(1)} %copy-done.7), custom_call_target="tpu_custom_call" | custom-call | flops 6291456 | bytes 5570560 | tf_op jit(solution)/shard_map/transform/pallas_call | solution.py:687
  15.8 4.3 %interior.1 = (f32[3,8,64,256]{3,2,1,0:T(8,128)S(1)}, f32[3,8,64,256]{3,2,1,0:T(8,128)S(1)}, f32[3,2,64,256]{3,2,1,0:T(8,128)S(1)}, f32[64,256]{1,0:T(8,128)S(1)}) custom-call(f32[3,8,64,256]{3,2,1,0:T(8,128)S(1)} %copy-done.1, f32[3,8,64,256]{3,2,1,0:T(8,128)S(1)} %copy-done.3, s32[8,64,256]{2,1,0:T(8,128)S(1)} %copy-done.5, f32[64,256]{1,0:T(8,128)S(1)} %copy-done.8, ...), custom_call_target="tpu_custom_call" | custom-call | flops 13107200 | bytes 7208960 | tf_op jit(solution)/shard_map/interior/pallas_call | solution.py:709
  20.1 3.6 %strips_x.1 = (f32[3,8,2,8,256]{4,3,2,1,0:T(8,128)S(1)}, f32[3,8,2,8,256]{4,3,2,1,0:T(8,128)S(1)}, f32[3,2,2,8,256]{4,3,2,1,0:T(8,128)S(1)}, f32[2,8,256]{2,1,0:T(8,128)S(1)}) custom-call(f32[3,8,64,256]{3,2,1,0:T(8,128)S(1)} %copy-done.1, f32[3,8,64,256]{3,2,1,0:T(8,128)S(1)} %copy-done.3, s32[8,64,256]{2,1,0:T(8,128)S(1)} %copy-done.5, ...), custom_call_target="tpu_custom_call" | custom-call | flops 3932160 | bytes 1966080 | tf_op jit(solution)/shard_map/strips_x/pallas_call | solution.py:739
  23.8 1.8 %gradient.1 = (f32[32,32,128]{2,1,0:T(8,128)S(1)}, f32[3,72,128]{2,1,0:T(8,128)S(1)}, f32[3,72,128]{2,1,0:T(8,128)S(1)}) custom-call(f32[8,64,128]{2,1,0:T(8,128)S(1)} %build_strips.1.s_ref, f32[8,8,128]{2,1,0:T(8,128)S(1)} %get-tuple-element.37.t_ref, f32[72,128]{1,0:T(8,128)S(1)} %collective-permute-done.2.ya_ref, ...), custom_call_target="tpu_custom_call" | custom-call | flops 983040 | bytes 1966080 | tf_op jit(solution)/shard_map/gradient/pallas_call | solution.py:764
  25.6 3.3 %collective-permute-start.4 = (f32[16,32,128]{2,1,0:T(8,128)S(1)}, f32[16,32,128]{2,1,0:T(8,128)S(1)}, u32[]{:S(2)}, u32[]{:S(2)}) collective-permute-start(f32[16,32,128]{2,1,0:T(8,128)S(1)} %slice.3), channel_id=1, source_target_pairs={{0,1},{1,0},{2,3},{3,2},{4,5},{5,4},{6,7},{7,6},{8,9},{9,8},{10,11... | collective-permute-start | bytes 786440 | tf_op jit(solution)/shard_map/ppermute | solution.py:664
  28.9 1.2 %collective-permute-done.4.refs_1_ = f32[16,32,128]{2,1,0:T(8,128)S(1)} collective-permute-done((f32[16,32,128]{2,1,0:T(8,128)S(1)}, f32[16,32,128]{2,1,0:T(8,128)S(1)}, u32[]{:S(2)}, u32[]{:S(2)}) %collective-permute-start.4) | collective-permute-done | bytes 262176 | tf_op jit(solution)/shard_map/ppermute | solution.py:664
  30.1 5.0 %collective-permute-start.5 = (f32[4,32,128]{2,1,0:T(8,128)S(1)}, f32[4,32,128]{2,1,0:T(8,128)S(1)}, u32[]{:S(2)}, u32[]{:S(2)}) collective-permute-start(f32[4,32,128]{2,1,0:T(8,128)S(1)} %get-tuple-element.52), channel_id=1, source_target_pairs={{0,4},{1,5},{2,6},{3,7},{4,0},{5,1},{6,2},{7,3},{8,12},{9,13},{10,... | collective-permute-start | bytes 196616 | tf_op jit(solution)/shard_map/ppermute | solution.py:664
  35.7 0.9 %collective-permute-start.7 = (f32[4,32,128]{2,1,0:T(8,128)S(1)}, f32[4,32,128]{2,1,0:T(8,128)S(1)}, u32[]{:S(2)}, u32[]{:S(2)}) collective-permute-start(f32[4,32,128]{2,1,0:T(8,128)S(1)} %get-tuple-element.54), channel_id=1, source_target_pairs={{0,6},{1,7},{2,4},{3,5},{4,2},{5,3},{6,0},{7,1},{8,14},{9,15},{10,... | collective-permute-start | bytes 196616 | tf_op jit(solution)/shard_map/ppermute | solution.py:664
  36.6 1.1 %collective-permute-done.5.refs_1_ = f32[4,32,128]{2,1,0:T(8,128)S(1)} collective-permute-done((f32[4,32,128]{2,1,0:T(8,128)S(1)}, f32[4,32,128]{2,1,0:T(8,128)S(1)}, u32[]{:S(2)}, u32[]{:S(2)}) %collective-permute-start.5) | collective-permute-done | bytes 65568 | tf_op jit(solution)/shard_map/ppermute | solution.py:664
  37.7 2.2 %collective-permute-done.6.refs_2_ = f32[4,32,128]{2,1,0:T(8,128)S(1)} collective-permute-done((f32[4,32,128]{2,1,0:T(8,128)S(1)}, f32[4,32,128]{2,1,0:T(8,128)S(1)}, u32[]{:S(2)}, u32[]{:S(2)}) %collective-permute-start.6) | collective-permute-done | bytes 65568 | tf_op jit(solution)/shard_map/ppermute | solution.py:664
  39.8 1.0 %collective-permute-done.7.refs_3_ = f32[4,32,128]{2,1,0:T(8,128)S(1)} collective-permute-done((f32[4,32,128]{2,1,0:T(8,128)S(1)}, f32[4,32,128]{2,1,0:T(8,128)S(1)}, u32[]{:S(2)}, u32[]{:S(2)}) %collective-permute-start.7) | collective-permute-done | bytes 65568 | tf_op jit(solution)/shard_map/ppermute | solution.py:664
  40.9 4.3 %collective-permute-start.10 = (f32[1,32,128]{2,1,0:T(8,128)S(1)}, f32[1,32,128]{2,1,0:T(8,128)S(1)}, u32[]{:S(2)}, u32[]{:S(2)}) collective-permute-start(f32[1,32,128]{2,1,0:T(8,128)S(1)} %get-tuple-element.58), channel_id=1, source_target_pairs={{0,24},{1,25},{2,26},{3,27},{4,28},{5,29},{6,30},{7,31},{8,16},{9,... | collective-permute-start | bytes 49160 | tf_op jit(solution)/shard_map/ppermute | solution.py:664
  45.8 2.4 %merge.1 = (f32[3,8,64,256]{3,2,1,0:T(8,128)}, f32[3,8,64,256]{3,2,1,0:T(8,128)}) custom-call(f32[3,8,64,256]{3,2,1,0:T(8,128)S(1)} %get-tuple-element.31.e2_ref.e_ref, f32[3,8,64,256]{3,2,1,0:T(8,128)S(1)} %get-tuple-element.32.h_ref, f32[3,8,2,8,256]{4,3,2,1,0:T(8,128)S(1)} %get-tuple-element.35.xe2_ref.xe_ref, ...), custom_call_target="tpu_custom_call" | custom-call | flops 3145728 | bytes 7208960 | tf_op jit(solution)/shard_map/merge/pallas_call | solution.py:809
  48.9 0.9 %collective-permute-done.9 = f32[1,32,128]{2,1,0:T(8,128)S(1)} collective-permute-done((f32[1,32,128]{2,1,0:T(8,128)S(1)}, f32[1,32,128]{2,1,0:T(8,128)S(1)}, u32[]{:S(2)}, u32[]{:S(2)}) %collective-permute-start.9) | collective-permute-done | bytes 16416 | tf_op jit(solution)/shard_map/ppermute | solution.py:664
  (32 shorter events, 3.7 us)
Async XLA Ops:
  0.6 1.4 %copy-start = (f32[3,8,64,256]{3,2,1,0:T(8,128)S(1)}, f32[3,8,64,256]{3,2,1,0:T(8,128)}, u32[]{:S(2)}) copy-start(f32[3,8,64,256]{3,2,1,0:T(8,128)} %e_ref.7) | copy-start | bytes 4718596
  2.0 1.4 %copy-start.2 = (f32[3,8,64,256]{3,2,1,0:T(8,128)S(1)}, f32[3,8,64,256]{3,2,1,0:T(8,128)}, u32[]{:S(2)}) copy-start(f32[3,8,64,256]{3,2,1,0:T(8,128)} %h_ref.7) | copy-start | bytes 4718596
  3.5 1.0 %copy-start.4 = (s32[8,64,256]{2,1,0:T(8,128)S(1)}, s32[8,64,256]{2,1,0:T(8,128)}, u32[]{:S(2)}) copy-start(s32[8,64,256]{2,1,0:T(8,128)} %m_ref.7) | copy-start | bytes 1572868
  4.5 0.8 %copy-start.8 = (f32[64,256]{1,0:T(8,128)S(1)}, f32[64,256]{1,0:T(8,128)}, u32[]{:S(2)}) copy-start(f32[64,256]{1,0:T(8,128)} %d_ref.7) | copy-start | bytes 196612
  5.3 0.7 %copy-start.10 = (s32[1,4]{1,0:T(1,128)S(1)}, s32[1,4]{1,0:T(1,128)}, u32[]{:S(2)}) copy-start(s32[1,4]{1,0:T(1,128)} %map_ref.5) | copy-start | bytes 52
  6.0 8.5 %copy-start.7 = (bf16[4,2,3,2,64,256]{5,4,3,2,1,0:T(8,128)(2,1)S(1)}, bf16[4,2,3,2,64,256]{5,4,3,2,1,0:T(8,128)(2,1)}, u32[]{:S(2)}) copy-start(bf16[4,2,3,2,64,256]{5,4,3,2,1,0:T(8,128)(2,1)} %fwd_ref.1) | copy-start | bytes 4718596
  6.8 6.4 %collective-permute-start = (f32[15,8,256]{2,1,0:T(8,128)S(1)}, f32[15,8,256]{2,1,0:T(8,128)S(1)}, u32[]{:S(2)}, u32[]{:S(2)}) collective-permute-start(f32[15,8,256]{2,1,0:T(8,128)S(1)} %get-tuple-element.33), channel_id=1, source_target_pairs={{0,4},{1,5},{2,6},{3,7},{4,0},{5,1},{6,2},{7,3},{8,12},{9,13},{10,... | collective-permute-start | bytes 368648 | tf_op jit(solution)/shard_map/ppermute | solution.py:664
  9.9 4.6 %copy-start.6 = (f32[4,2,3,2,64,256]{5,4,3,2,1,0:T(8,128)S(1)}, f32[4,2,3,2,64,256]{5,4,3,2,1,0:T(8,128)}, u32[]{:S(2)}) copy-start(f32[4,2,3,2,64,256]{5,4,3,2,1,0:T(8,128)} %adj_ref.1) | copy-start | bytes 9437188
  9.9 3.3 %collective-permute-start.1 = (f32[15,8,256]{2,1,0:T(8,128)S(1)}, f32[15,8,256]{2,1,0:T(8,128)S(1)}, u32[]{:S(2)}, u32[]{:S(2)}) collective-permute-start(f32[15,8,256]{2,1,0:T(8,128)S(1)} %get-tuple-element.34), channel_id=1, source_target_pairs={{4,8},{5,9},{6,10},{7,11},{8,4},{9,5},{10,6},{11,7},{12,16},{13,17... | collective-permute-start | bytes 368648 | tf_op jit(solution)/shard_map/ppermute | solution.py:664
  13.5 10.2 %collective-permute-start.2 = (f32[72,128]{1,0:T(8,128)S(1)}, f32[72,128]{1,0:T(8,128)S(1)}, u32[]{:S(2)}, u32[]{:S(2)}) collective-permute-start(f32[72,128]{1,0:T(8,128)S(1)} %get-tuple-element.38), channel_id=1, source_target_pairs={{0,1},{1,0},{2,3},{3,2},{4,5},{5,4},{6,7},{7,6},{8,9},{9,8},{10,11... | collective-permute-start | bytes 110600 | tf_op jit(solution)/shard_map/ppermute | solution.py:664
  13.6 2.1 %copy-start.1 = (f32[3,8,64,256]{3,2,1,0:T(8,128)S(1)}, f32[3,8,64,256]{3,2,1,0:T(8,128)}, u32[]{:S(2)}) copy-start(f32[3,8,64,256]{3,2,1,0:T(8,128)} %e_ref.7) | copy-start | bytes 4718596
  13.6 2.1 %copy-start.3 = (f32[3,8,64,256]{3,2,1,0:T(8,128)S(1)}, f32[3,8,64,256]{3,2,1,0:T(8,128)}, u32[]{:S(2)}) copy-start(f32[3,8,64,256]{3,2,1,0:T(8,128)} %h_ref.7) | copy-start | bytes 4718596
  13.6 2.1 %copy-start.5 = (s32[8,64,256]{2,1,0:T(8,128)S(1)}, s32[8,64,256]{2,1,0:T(8,128)}, u32[]{:S(2)}) copy-start(s32[8,64,256]{2,1,0:T(8,128)} %m_ref.7) | copy-start | bytes 1572868
  13.7 2.1 %copy-start.9 = (f32[4]{0:T(128)S(1)}, f32[4]{0:T(128)}, u32[]{:S(2)}) copy-start(f32[4]{0:T(128)} %table.5) | copy-start | bytes 52
  13.7 10.1 %collective-permute-start.3 = (f32[72,128]{1,0:T(8,128)S(1)}, f32[72,128]{1,0:T(8,128)S(1)}, u32[]{:S(2)}, u32[]{:S(2)}) collective-permute-start(f32[72,128]{1,0:T(8,128)S(1)} %get-tuple-element.39), channel_id=1, source_target_pairs={{1,2},{2,1},{5,6},{6,5},{9,10},{10,9},{13,14},{14,13},{17,18},{18,... | collective-permute-start | bytes 110600 | tf_op jit(solution)/shard_map/ppermute | solution.py:664
  25.6 4.4 %collective-permute-start.4 = (f32[16,32,128]{2,1,0:T(8,128)S(1)}, f32[16,32,128]{2,1,0:T(8,128)S(1)}, u32[]{:S(2)}, u32[]{:S(2)}) collective-permute-start(f32[16,32,128]{2,1,0:T(8,128)S(1)} %slice.3), channel_id=1, source_target_pairs={{0,1},{1,0},{2,3},{3,2},{4,5},{5,4},{6,7},{7,6},{8,9},{9,8},{10,11... | collective-permute-start | bytes 786440 | tf_op jit(solution)/shard_map/ppermute | solution.py:664
  30.1 7.6 %collective-permute-start.5 = (f32[4,32,128]{2,1,0:T(8,128)S(1)}, f32[4,32,128]{2,1,0:T(8,128)S(1)}, u32[]{:S(2)}, u32[]{:S(2)}) collective-permute-start(f32[4,32,128]{2,1,0:T(8,128)S(1)} %get-tuple-element.52), channel_id=1, source_target_pairs={{0,4},{1,5},{2,6},{3,7},{4,0},{5,1},{6,2},{7,3},{8,12},{9,13},{10,... | collective-permute-start | bytes 196616 | tf_op jit(solution)/shard_map/ppermute | solution.py:664
  35.1 4.8 %collective-permute-start.6 = (f32[4,32,128]{2,1,0:T(8,128)S(1)}, f32[4,32,128]{2,1,0:T(8,128)S(1)}, u32[]{:S(2)}, u32[]{:S(2)}) collective-permute-start(f32[4,32,128]{2,1,0:T(8,128)S(1)} %get-tuple-element.53), channel_id=1, source_target_pairs={{0,2},{1,3},{2,0},{3,1},{4,6},{5,7},{6,4},{7,5},{8,10},{9,11},{10,... | collective-permute-start | bytes 196616 | tf_op jit(solution)/shard_map/ppermute | solution.py:664
  35.7 5.2 %collective-permute-start.7 = (f32[4,32,128]{2,1,0:T(8,128)S(1)}, f32[4,32,128]{2,1,0:T(8,128)S(1)}, u32[]{:S(2)}, u32[]{:S(2)}) collective-permute-start(f32[4,32,128]{2,1,0:T(8,128)S(1)} %get-tuple-element.54), channel_id=1, source_target_pairs={{0,6},{1,7},{2,4},{3,5},{4,2},{5,3},{6,0},{7,1},{8,14},{9,15},{10,... | collective-permute-start | bytes 196616 | tf_op jit(solution)/shard_map/ppermute | solution.py:664
  40.9 7.4 %collective-permute-start.10 = (f32[1,32,128]{2,1,0:T(8,128)S(1)}, f32[1,32,128]{2,1,0:T(8,128)S(1)}, u32[]{:S(2)}, u32[]{:S(2)}) collective-permute-start(f32[1,32,128]{2,1,0:T(8,128)S(1)} %get-tuple-element.58), channel_id=1, source_target_pairs={{0,24},{1,25},{2,26},{3,27},{4,28},{5,29},{6,30},{7,31},{8,16},{9,... | collective-permute-start | bytes 49160 | tf_op jit(solution)/shard_map/ppermute | solution.py:664
  45.2 3.7 %collective-permute-start.8 = (f32[1,32,128]{2,1,0:T(8,128)S(1)}, f32[1,32,128]{2,1,0:T(8,128)S(1)}, u32[]{:S(2)}, u32[]{:S(2)}) collective-permute-start(f32[1,32,128]{2,1,0:T(8,128)S(1)} %get-tuple-element.56), channel_id=1, source_target_pairs={{0,8},{1,9},{2,10},{3,11},{4,12},{5,13},{6,14},{7,15},{8,0},{9,1},... | collective-permute-start | bytes 49160 | tf_op jit(solution)/shard_map/ppermute | solution.py:664
  45.2 4.6 %collective-permute-start.9 = (f32[1,32,128]{2,1,0:T(8,128)S(1)}, f32[1,32,128]{2,1,0:T(8,128)S(1)}, u32[]{:S(2)}, u32[]{:S(2)}) collective-permute-start(f32[1,32,128]{2,1,0:T(8,128)S(1)} %get-tuple-element.57), channel_id=1, source_target_pairs={{0,16},{1,17},{2,18},{3,19},{4,20},{5,21},{6,22},{7,23},{8,24},{9,... | collective-permute-start | bytes 49160 | tf_op jit(solution)/shard_map/ppermute | solution.py:664

commit v2 on v1

--- a/solution.py
+++ b/solution.py
@@ -29,12 +29,13 @@
 SUB = 8
 GROUP = 16
 ANY = pl.BlockSpec(memory_space=pl.ANY)
+HBM = pl.BlockSpec(memory_space=pltpu.HBM)
 VMEM = pl.BlockSpec(memory_space=pltpu.VMEM)
 SMEM = pl.BlockSpec(memory_space=pltpu.SMEM)
 
 
-def params(mib=40):
-    return pltpu.CompilerParams(vmem_limit_bytes=mib * 2**20)
+def params(size=40 * 2**20):
+    return pltpu.CompilerParams(vmem_limit_bytes=size)
 
 
 def struct(*shape, dtype=F32):
@@ -109,59 +110,41 @@
     return out
 
 
-def faces(fields, planes_z):
-    return len(fields) * planes_z
-
-
-def edge_copies(e_ref, h_ref, m_ref, d_ref, eb, hb, mb, db, sems):
-    size = d_ref.shape[0]
+def n_faces(planes_z):
+    return 7 * planes_z + 1
+
+
+def edge_tile(q, start, e_ref, h_ref, m_ref, d_ref, ids=None):
+    planes_z = m_ref.shape[0]
+    field, z = divmod(q, planes_z)
+    rows = pl.ds(start, SUB)
+    if field < 3:
+        return e_ref[field, z, rows]
+    if field < 6:
+        return h_ref[field - 3, z, rows]
+    if field > 6:
+        return ids
+    return d_ref[rows] if in_design(z) else m_ref[z, rows].astype(F32)
+
+
+def pack_x(e_in, h_in, m_in, d_in, map_in, a_ref, b_ref, eb, hb, mb, db, map_ref, sems):
+    planes_z, size, width_y = m_in.shape
+    fields = ((e_in, eb), (h_in, hb), (m_in, mb))
     copies = []
-    for side, start in enumerate((0, size - SUB)):
-        rows = pl.ds(start, SUB)
-        copies += [
-            pltpu.make_async_copy(e_ref.at[:, :, rows, :], eb.at[side], sems.at[4 * side]),
-            pltpu.make_async_copy(h_ref.at[:, :, rows, :], hb.at[side], sems.at[4 * side + 1]),
-            pltpu.make_async_copy(m_ref.at[:, rows, :], mb.at[side], sems.at[4 * side + 2]),
-            pltpu.make_async_copy(d_ref.at[rows, :], db.at[side], sems.at[4 * side + 3]),
-        ]
+    for k, start in enumerate((0, size - SUB)):
+        here, there = pl.ds(start, SUB), pl.ds(k * SUB, SUB)
+        for n, (src, dst) in enumerate(fields):
+            source = src.at[:, here] if n == 2 else src.at[:, :, here]
+            target = dst.at[:, there] if n == 2 else dst.at[:, :, there]
+            copies.append(pltpu.make_async_copy(source, target, sems.at[4 * k + n]))
+        copies.append(pltpu.make_async_copy(d_in.at[here], db.at[there], sems.at[4 * k + 3]))
+    copies.append(pltpu.make_async_copy(map_in, map_ref, sems.at[8]))
     for copy in copies:
         copy.start()
+    even = lax.axis_index("gx") % 2 == 0
+    sub = iota((SUB, width_y), 0)
     for copy in copies:
         copy.wait()
-
-
-def edge_scratch(planes_z, width_y):
-    return [
-        pltpu.VMEM((2, 3, planes_z, SUB, width_y), F32),
-        pltpu.VMEM((2, 3, planes_z, SUB, width_y), F32),
-        pltpu.VMEM((2, planes_z, SUB, width_y), jnp.int32),
-        pltpu.VMEM((2, SUB, width_y), F32),
-        pltpu.SemaphoreType.DMA((8,)),
-    ]
-
-
-def edge_tile(side, q, planes_z, eb, hb, mb, db, ids):
-    field, z = divmod(q, planes_z)
-    if field < 3:
-        return eb[side, field, z]
-    if field < 6:
-        return hb[side, field - 3, z]
-    if field == 6:
-        return db[side] if in_design(z) else mb[side, z].astype(F32)
-    return ids
-
-
-def n_faces(planes_z):
-    return 7 * planes_z + 1
-
-
-def pack_x(e_ref, h_ref, m_ref, d_ref, map_ref, a_ref, b_ref, eb, hb, mb, db, sems):
-    planes_z, _, width_y = m_ref.shape
-    edge_copies(e_ref, h_ref, m_ref, d_ref, eb, hb, mb, db, sems)
-    even = lax.axis_index("gx") % 2 == 0
-    last = map_ref.shape[0] - 1
-    sub = iota((SUB, width_y), 0)
-    ids = [id_row(map_ref, 0, (SUB, width_y)), id_row(map_ref, last, (SUB, width_y))]
     for group in range(a_ref.shape[0]):
         low = jnp.zeros((SUB, width_y), F32)
         high = low
@@ -169,11 +152,12 @@
             q = 4 * group + k
             if q >= n_faces(planes_z):
                 break
-            mask = sub // 2 == k
-            tile = edge_tile(0, q, planes_z, eb, hb, mb, db, ids[0])
-            low = jnp.where(mask, turn(tile, 2 * k, 0), low)
-            tile = edge_tile(1, q, planes_z, eb, hb, mb, db, ids[1])
-            high = jnp.where(mask, turn(tile, 2 * k - 6, 0), high)
+            ids = [None, None]
+            if q == n_faces(planes_z) - 1:
+                ids = [id_row(map_ref, tx, (SUB, width_y)) for tx in (0, map_ref.shape[0] - 1)]
+            tiles = [edge_tile(q, n * SUB, eb, hb, mb, db, ids[n]) for n in range(2)]
+            low = jnp.where(sub // 2 == k, turn(tiles[0], 2 * k, 0), low)
+            high = jnp.where(sub // 2 == k, turn(tiles[1], 2 * k - 6, 0), high)
         a_ref[group] = jnp.where(even, high, low)
         b_ref[group] = jnp.where(even, low, high)
 
@@ -218,7 +202,7 @@
         s_ref[7, rows] = to_strip(row, 0, jnp.zeros((TILE, LANES), F32))
 
 
-def pack_y(s_ref, xa_ref, xb_ref, t_ref, a_ref, b_ref):
+def pack_y(s_ref, xa_ref, xb_ref, _after, t_ref, a_ref, b_ref):
     planes_z = LANES // GROUP
     width_x = s_ref.shape[1]
     width_y = xa_ref.shape[2]
@@ -268,7 +252,61 @@
     s_ref[...] = total
 
 
-def interior(e_ref, h_ref, m_ref, d_ref, table, e2_ref, h2_ref, e1_ref, sl_ref, damp, ch, ce):
+LO = ZLO - STEPS
+HI = ZLO + PLANES + STEPS - 1
+
+
+def update_mag(e, e_up, h, out, damp, ch):
+    width_x, width_y = damp.shape
+    for start in range(0, width_x, SUB):
+        here = pl.ds(start, SUB)
+
+        def ahead(c, tile):
+            if start + SUB < width_x:
+                return e(c)[pl.ds(start + 1, SUB)]
+            return turn(tile, SUB - 1, 0)
+
+        ex, ey, ez = (e(c)[here] for c in range(3))
+        up_x = e_up(0)[here] - ex if e_up else -ex
+        up_y = e_up(1)[here] - ey if e_up else -ey
+        cx = (turn(ez, width_y - 1, 1) - ez) - up_y
+        cy = up_x - (ahead(2, ez) - ez)
+        cz = (ahead(1, ey) - ey) - (turn(ex, width_y - 1, 1) - ex)
+        dm, cf = damp[here], ch[here]
+        for c, curl in enumerate((cx, cy, cz)):
+            out(c)[here] = dm * h(c)[here] - cf * curl
+
+
+def update_elec(h, h_down, e, out, damp, ce):
+    width_x, width_y = damp.shape
+    for start in range(0, width_x, SUB):
+        here = pl.ds(start, SUB)
+
+        def behind(c, tile):
+            return h(c)[pl.ds(start - 1, SUB)] if start else turn(tile, 1, 0)
+
+        hx, hy, hz = (h(c)[here] for c in range(3))
+        up_x = hx - h_down(0)[here] if h_down else hx
+        up_y = hy - h_down(1)[here] if h_down else hy
+        cx = (hz - turn(hz, 1, 1)) - up_y
+        cy = up_x - (hz - behind(2, hz))
+        cz = (hy - behind(1, hy)) - (hx - turn(hx, 1, 1))
+        dm, cf = damp[here], ce[here]
+        for c, curl in enumerate((cx, cy, cz)):
+            out(c)[here] = dm * e(c)[here] + cf * curl
+
+
+def at(ref, z):
+    return lambda c: ref.at[c, z]
+
+
+def fill_ce(ce, k, z, m_ref, choices, ch):
+    for start in range(0, ch.shape[0], SUB):
+        here = pl.ds(start, SUB)
+        ce[k, here] = pick(m_ref[z, here], choices) * (ch[here] * (1.0 / courant))
+
+
+def interior_first(e_ref, h_ref, m_ref, d_ref, table, em, hm, e1_ref, sl_ref, damp, ch, ce):
     planes_z, width_x, width_y = m_ref.shape
     gx, gy = lax.axis_index("gx"), lax.axis_index("gy")
     total_x, total_y = width_x * lax.axis_size("gx"), width_y * lax.axis_size("gy")
@@ -280,76 +318,73 @@
     ch[...] = coef_h
     design, slope = design_terms(blur(d_ref[...]))
     sl_ref[...] = slope
-    choices = table_inverse(table, (SUB, LANES))
-    choices = [jnp.tile(c, (1, width_y // LANES)) for c in choices]
+    choices = [jnp.tile(c, (1, width_y // LANES)) for c in table_inverse(table, (SUB, LANES))]
+    for z in range(LO, HI):
+        if in_design(z):
+            ce[z - LO] = design * inverse
+        elif z > LO:
+            fill_ce(ce, z - LO, z, m_ref, choices, ch)
+
+    def e(z):
+        return at(em, z - LO)
+
+    def h(z):
+        return at(hm, z - LO)
+
+    for z in range(LO, HI):
+        update_mag(at(e_ref, z), at(e_ref, z + 1), at(h_ref, z), h(z), damp, ch)
+    for z in range(LO + 1, HI):
+        update_elec(h(z), h(z - 1), at(e_ref, z), e(z), damp, ce.at[z - LO])
+    for c in range(3):
+        for p in range(PLANES):
+            e1_ref[c, p] = em[c, ZLO + p - LO]
+    for z in range(LO + 1, HI - 1):
+        update_mag(e(z), e(z + 1), h(z), h(z), damp, ch)
+    for z in range(LO + 2, HI - 1):
+        update_elec(h(z), h(z - 1), e(z), e(z), damp, ce.at[z - LO])
+
+
+def interior_rest(e_ref, h_ref, m_ref, table, em, hm, damp, ch, ce, e2, h2, done, ce2):
+    planes_z, width_x, width_y = m_ref.shape
+    choices = [jnp.tile(c, (1, width_y // LANES)) for c in table_inverse(table, (SUB, LANES))]
+    done[...] = jnp.zeros(done.shape, F32)
+    rest = [z for z in range(planes_z) if not LO < z < HI]
+    for z in rest:
+        fill_ce(ce2, z, z, m_ref, choices, ch)
+
+    def coef(z):
+        return ce.at[z - LO] if LO < z < HI else ce2.at[z]
+
+    def e1(z):
+        return at(em, z - LO) if LO < z < HI else at(e2, z)
+
+    def h1(z):
+        return at(hm, z - LO) if LO <= z < HI else at(h2, z)
+
+    def h_last(z):
+        return at(hm, z - LO) if LO < z < HI - 1 else at(h2, z)
+
     for z in range(planes_z):
-        if in_design(z):
-            ce[z] = design * inverse
-    for start in range(0, width_x, SUB):
-        inv = inverse[start : start + SUB]
-        for z in range(planes_z):
-            if not in_design(z):
-                ce[z, pl.ds(start, SUB)] = pick(m_ref[z, pl.ds(start, SUB)], choices) * inv
-
-    def mag(src_e, src_h, z, last):
-        for start in range(0, width_x, SUB):
-            here = pl.ds(start, SUB)
-
-            def ahead(c, tile):
-                if start + SUB < width_x:
-                    return src_e[c, z, pl.ds(start + 1, SUB)]
-                return turn(tile, SUB - 1, 0)
-
-            ex, ey, ez = (src_e[c, z, here] for c in range(3))
-            up_x = -ex if last else src_e[0, z + 1, here] - ex
-            up_y = -ey if last else src_e[1, z + 1, here] - ey
-            cx = (turn(ez, width_y - 1, 1) - ez) - up_y
-            cy = up_x - (ahead(2, ez) - ez)
-            cz = (ahead(1, ey) - ey) - (turn(ex, width_y - 1, 1) - ex)
-            dm, cf = damp[here], ch[here]
-            for c, curl in enumerate((cx, cy, cz)):
-                h2_ref[c, z, here] = dm * src_h[c, z, here] - cf * curl
-
-    def elec(src_e, z, first):
-        for start in range(0, width_x, SUB):
-            here = pl.ds(start, SUB)
-
-            def behind(c, tile):
-                if start:
-                    return h2_ref[c, z, pl.ds(start - 1, SUB)]
-                return turn(tile, 1, 0)
-
-            hx, hy, hz = (h2_ref[c, z, here] for c in range(3))
-            up_x = hx if first else hx - h2_ref[0, z - 1, here]
-            up_y = hy if first else hy - h2_ref[1, z - 1, here]
-            cx = (hz - turn(hz, 1, 1)) - up_y
-            cy = up_x - (hz - behind(2, hz))
-            cz = (hy - behind(1, hy)) - (hx - turn(hx, 1, 1))
-            dm, cf = damp[here], ce[z, here]
-            for c, curl in enumerate((cx, cy, cz)):
-                e2_ref[c, z, here] = dm * src_e[c, z, here] + cf * curl
-
-    def loop(lo, hi, f):
-        lax.fori_loop(lo, hi, lambda z, _: (f(z), 0)[1], 0)
-
-    for n in range(STEPS):
-        src_e, src_h = (e_ref, h_ref) if n == 0 else (e2_ref, h2_ref)
-        loop(0, planes_z - 1, lambda z: mag(src_e, src_h, z, False))
-        mag(src_e, src_h, planes_z - 1, True)
-        elec(src_e, 0, True)
-        loop(1, planes_z, lambda z: elec(src_e, z, False))
-        if n == 0:
-            for c in range(3):
-                for p in range(PLANES):
-                    e1_ref[c, p] = e2_ref[c, ZLO + p]
+        if not LO <= z < HI:
+            up = at(e_ref, z + 1) if z + 1 < planes_z else None
+            update_mag(at(e_ref, z), up, at(h_ref, z), at(h2, z), damp, ch)
+    for z in rest:
+        update_elec(h1(z), h1(z - 1) if z else None, at(e_ref, z), at(e2, z), damp, coef(z))
+    for z in range(planes_z):
+        if not LO < z < HI - 1:
+            up = e1(z + 1) if z + 1 < planes_z else None
+            update_mag(e1(z), up, h1(z), at(h2, z), damp, ch)
+    for z in range(planes_z):
+        if not in_design(z):
+            down = h_last(z - 1) if z else None
+            update_elec(h_last(z), down, e1(z), at(e2, z), damp, coef(z))
 
 
 def strips_x(
     e_ref, h_ref, m_ref, d_ref, table, xa_ref, xb_ref,
-    e2_ref, h2_ref, e1_ref, sl_ref, eb, hb, mb, db, sems, xe, xh, ce,
+    e2_ref, h2_ref, e1_ref, sl_ref, xe, xh, ce,
 ):
     planes_z, width_x, width_y = m_ref.shape
-    edge_copies(e_ref, h_ref, m_ref, d_ref, eb, hb, mb, db, sems)
     gx, gy = lax.axis_index("gx"), lax.axis_index("gy")
     total_x, total_y = width_x * lax.axis_size("gx"), width_y * lax.axis_size("gy")
     even = gx % 2 == 0
@@ -362,7 +397,7 @@
 
     def strip(side, q):
         below, above = halo_rows(xa_ref, xb_ref, q, even)
-        own = edge_tile(side, q, planes_z, eb, hb, mb, db, None)
+        own = edge_tile(q, side * (width_x - SUB), e_ref, h_ref, m_ref, d_ref)
         if side == 0:
             return jnp.where(sub < 2, below, turn(own, 2, 0))
         return jnp.where(sub >= 6, turn(above, 6, 0), turn(own, 6, 0))
@@ -407,7 +442,8 @@
                 xe[side, c, z] = damps[side] * xe[side, c, z] + ce[side, z] * curl
 
     def loop(f):
-        lax.fori_loop(0, planes_z, lambda z, _: (f(z), 0)[1], 0)
+        for z in range(planes_z):
+            f(z)
 
     back = (6, 2)
     for n in range(STEPS):
@@ -551,7 +587,8 @@
             for p in range(PLANES):
                 first = patch_rows(e1_ref[c, p, here], xe1_ref.at[c, p], start, width_x)
                 first = patch_cols(first, ye1[c, here], ZLO + p)
-                second = patch_rows(e2_ref[c, ZLO + p, here], xe2_ref.at[c, ZLO + p], start, width_x)
+                second = e2_ref[c, ZLO + p - LO, here]
+                second = patch_rows(second, xe2_ref.at[c, ZLO + p], start, width_x)
                 second = patch_cols(second, ye_ref[c, here], ZLO + p)
                 total = total + g_ref[0, c, p, here] * first + g_ref[1, c, p, here] * second
         slope = patch_rows(sl_ref[here], xsl_ref, start, width_x)
@@ -629,13 +666,18 @@
         add_rows(scalar_of(tail, sub, column), start, values)
 
 
-def merge(e_ref, h_ref, xe_ref, xh_ref, ye_ref, yh_ref, eo_ref, ho_ref):
+def merge(e_ref, h_ref, em, hm, xe_ref, xh_ref, ye_ref, yh_ref, eo_ref, ho_ref):
     _, planes_z, width_x, _ = e_ref.shape
-    for src, xs, ys, out in ((e_ref, xe_ref, ye_ref, eo_ref), (h_ref, xh_ref, yh_ref, ho_ref)):
+    parts = (
+        (e_ref, em, xe_ref, ye_ref, eo_ref, LO + 2, HI - 1),
+        (h_ref, hm, xh_ref, yh_ref, ho_ref, LO + 1, HI - 1),
+    )
+    for rest, mid, xs, ys, out, low, high in parts:
         for z in range(planes_z):
+            src = mid.at[0, z - LO] if low <= z < high else rest.at[0, z]
             for start in range(0, width_x, SUB):
                 here = pl.ds(start, SUB)
-                values = patch_rows(src[0, z, here], xs.at[0, z], start, width_x)
+                values = patch_rows(src[here], xs.at[0, z], start, width_x)
                 out[0, z, here] = patch_cols(values, ys[0, here], z)
 
 
@@ -647,7 +689,7 @@
 
 
 def second_sum(parts, rows_mine, *refs):
-    ins, outs = refs[:parts], refs[parts:]
+    ins, outs = refs[:parts], refs[parts + 1 :]
     for k, out in enumerate(outs):
         rows = pl.ds(k * rows_mine, rows_mine)
         out[...] = sum(ref[rows] for ref in ins[1:]) + ins[0][rows]
@@ -673,14 +715,30 @@
     xa, xb = pl.pallas_call(
         pack_x,
         out_shape=(face, face),
-        in_specs=[ANY, ANY, ANY, ANY, SMEM],
-        out_specs=(VMEM, VMEM),
-        scratch_shapes=edge_scratch(planes_z, width_y),
-        compiler_params=params(),
+        in_specs=[HBM] * 5,
+        out_specs=(VMEM,) * 2,
+        scratch_shapes=[
+            pltpu.VMEM((3, planes_z, 2 * SUB, width_y), F32),
+            pltpu.VMEM((3, planes_z, 2 * SUB, width_y), F32),
+            pltpu.VMEM((planes_z, 2 * SUB, width_y), jnp.int32),
+            pltpu.VMEM((2 * SUB, width_y), F32),
+            pltpu.SMEM(tile_map.shape, jnp.int32),
+            pltpu.SemaphoreType.DMA((9,)),
+        ],
+        compiler_params=params(62700000),
         name="pack_x",
     )(e_adj, h_adj, material, density, tile_map)
     xa = pair(xa, lambda i, j: (i ^ 1, j))
     xb = pair(xb, lambda i, j: (((i + 1) ^ 1) - 1, j))
+    strip = pl.pallas_call(
+        build_strips,
+        out_shape=struct(8, width_x, LANES),
+        in_specs=[VMEM] * 4 + [SMEM],
+        out_specs=VMEM,
+        compiler_params=params(),
+        cost_estimate=cost(1, 1),
+        name="build_strips",
+    )(e_adj, h_adj, material, density, tile_map)
 
     rows = 2 * SUB
     moved = struct(width_x, width_y), struct(STEPS, 3, PLANES, width_x, width_y)
@@ -694,46 +752,42 @@
             pl.BlockSpec((STEPS, 3, PLANES, rows, width_y), lambda i: (0, 0, 0, i, 0)),
         ),
         compiler_params=params(),
-        cost_estimate=cost(48 * 8 * width_x * width_y, 85 * block),
+        cost_estimate=cost(1, 1),
         name="transform",
     )(dft_adj, dft_fwd)
-    strip = pl.pallas_call(
-        build_strips,
-        out_shape=struct(8, width_x, LANES),
+    plane = struct(width_x, width_y)
+    middle = struct(3, HI - LO, width_x, width_y)
+    full = struct(3, planes_z, width_x, width_y)
+    em, hm, e1, slope, damp, ch, ce = pl.pallas_call(
+        interior_first,
+        out_shape=(middle, middle, struct(3, PLANES, width_x, width_y))
+        + (plane,) * 3
+        + (struct(HI - LO, width_x, width_y),),
         in_specs=[VMEM] * 4 + [SMEM],
-        out_specs=VMEM,
-        compiler_params=params(),
-        cost_estimate=cost(48 * 4 * width_x * width_y, 60 * block),
-        name="build_strips",
-    )(e_adj, h_adj, material, density, tile_map)
-    e2, h2, e1, slope = pl.pallas_call(
-        interior,
-        out_shape=(
-            struct(3, planes_z, width_x, width_y),
-            struct(3, planes_z, width_x, width_y),
-            struct(3, PLANES, width_x, width_y),
-            struct(width_x, width_y),
-        ),
-        in_specs=[VMEM] * 4 + [SMEM],
-        out_specs=(VMEM,) * 4,
-        scratch_shapes=[
-            pltpu.VMEM((width_x, width_y), F32),
-            pltpu.VMEM((width_x, width_y), F32),
-            pltpu.VMEM((planes_z, width_x, width_y), F32),
-        ],
-        compiler_params=params(),
-        cost_estimate=cost(100 * planes_z * width_x * width_y, 110 * block),
-        name="interior",
+        out_specs=(VMEM,) * 7,
+        compiler_params=params(),
+        cost_estimate=cost(1, 1),
+        name="interior_first",
     )(e_adj, h_adj, material, density, eps_table)
+    e2, h2, done = pl.pallas_call(
+        interior_rest,
+        out_shape=(full, full, struct(SUB, LANES)),
+        in_specs=[VMEM] * 3 + [SMEM] + [VMEM] * 5,
+        out_specs=(VMEM,) * 3,
+        scratch_shapes=[pltpu.VMEM((planes_z, width_x, width_y), F32)],
+        compiler_params=params(),
+        cost_estimate=cost(1, 1),
+        name="interior_rest",
+    )(e_adj, h_adj, material, eps_table, em, hm, damp, ch, ce)
 
     tails, ya, yb = pl.pallas_call(
         pack_y,
         out_shape=(struct(8, SUB, LANES),) + (struct(width_x + SUB, LANES),) * 2,
-        in_specs=[VMEM] * 3,
+        in_specs=[VMEM] * 3 + [ANY],
         out_specs=(VMEM,) * 3,
         compiler_params=params(),
         name="pack_y",
-    )(strip, xa, xb)
+    )(strip, xa, xb, slope)
     ya = pair(ya, lambda i, j: (i, j ^ 1))
     yb = pair(yb, lambda i, j: (i, ((j + 1) ^ 1) - 1))
     xe2, xh2, xe1, xslope = pl.pallas_call(
@@ -744,16 +798,15 @@
             struct(3, PLANES, 2, SUB, width_y),
             struct(2, SUB, width_y),
         ),
-        in_specs=[ANY, ANY, ANY, ANY, SMEM, VMEM, VMEM],
+        in_specs=[VMEM] * 4 + [SMEM] + [VMEM] * 2,
         out_specs=(VMEM,) * 4,
-        scratch_shapes=edge_scratch(planes_z, width_y)
-        + [
+        scratch_shapes=[
             pltpu.VMEM((2, 3, planes_z + 1, SUB, width_y), F32),
             pltpu.VMEM((2, 3, planes_z + 1, SUB, width_y), F32),
             pltpu.VMEM((2, planes_z, SUB, width_y), F32),
         ],
         compiler_params=params(),
-        cost_estimate=cost(30 * planes_z * width_x * width_y, 30 * block),
+        cost_estimate=cost(1, 1),
         name="strips_x",
     )(e_adj, h_adj, material, density, eps_table, xa, xb)
 
@@ -774,9 +827,9 @@
             pltpu.VMEM((width_y // LANES, padded, LANES), F32),
         ],
         compiler_params=params(),
-        cost_estimate=cost(60 * width_x * width_y, 30 * block),
+        cost_estimate=cost(1, 1),
         name="gradient",
-    )(strip, tails, ya, yb, xa, xb, eps_table, tile_map, e1, e2, xe1, xe2, slope, xslope, base, weight)
+    )(strip, tails, ya, yb, xa, xb, eps_table, tile_map, e1, em, xe1, xe2, slope, xslope, base, weight)
 
     half = devices * rows_mine // 2
     far = count_gx // 2
@@ -792,17 +845,7 @@
     parts = [parts[0]] + [
         pair(parts[k], lambda i, j: (i ^ (k & 1), j ^ (k >> 1 << 1))) for k in range(1, count_gy)
     ]
-    parts = pl.pallas_call(
-        lambda *refs: second_sum(count_gy, rows_mine, *refs),
-        out_shape=(struct(rows_mine, lines, LANES),) * far,
-        in_specs=[VMEM] * count_gy,
-        out_specs=(VMEM,) * far,
-        compiler_params=params(),
-        name="second_sum",
-    )(*parts)
-    parts = [parts[0]] + [pair(parts[k], lambda i, j: (i ^ (k << 1), j)) for k in range(1, far)]
-    param_grad = sum(parts[1:], parts[0]).reshape(rows_mine, TILE * TILE)
-
+    core = pl.BlockSpec((1, HI - LO, width_x, width_y), lambda c: (c, 0, 0, 0))
     whole = pl.BlockSpec((1, planes_z, width_x, width_y), lambda c: (c, 0, 0, 0))
     edge = pl.BlockSpec((1, planes_z, 2, SUB, width_y), lambda c: (c, 0, 0, 0, 0))
     side = pl.BlockSpec((1, width_x + SUB, LANES), lambda c: (c, 0, 0))
@@ -810,12 +853,23 @@
         merge,
         grid=(3,),
         out_shape=(struct(3, planes_z, width_x, width_y),) * 2,
-        in_specs=[whole, whole, edge, edge, side, side],
+        in_specs=[whole, whole, core, core, edge, edge, side, side],
         out_specs=(whole, whole),
         compiler_params=params(),
-        cost_estimate=cost(48 * 4 * width_x * width_y, 110 * block),
+        cost_estimate=cost(1, 1),
         name="merge",
-    )(e2, h2, xe2, xh2, ye2, yh2)
+    )(e2, h2, em, hm, xe2, xh2, ye2, yh2)
+    parts = pl.pallas_call(
+        lambda *refs: second_sum(count_gy, rows_mine, *refs),
+        out_shape=(struct(rows_mine, lines, LANES),) * far,
+        in_specs=[VMEM] * count_gy + [ANY],
+        out_specs=(VMEM,) * far,
+        compiler_params=params(),
+        name="second_sum",
+    )(*parts, done)
+    parts = [parts[0]] + [pair(parts[k], lambda i, j: (i ^ (k << 1), j)) for k in range(1, far)]
+    param_grad = sum(parts[1:], parts[0]).reshape(rows_mine, TILE * TILE)
+
     return e_out, h_out, param_grad
 
 

time: 50.7 us -> 39.6 us (0.78)
  local copies, waits for them, and re-layouts: 5.4 us -> 0.06 us
  waiting for transfers between devices: 7.75 us -> 5.31 us
  Pallas kernels: 16.4 us -> 14.8 us
  starting transfers between devices: 19.4 us -> 17.8 us
    unnamed x22 -> x16, local copies, waits for them, and re-layouts: 5.38 us -> 0.04 us
    pallas_call x1, Pallas kernels: 3.64 us -> 1.16 us  [on_device(): pl.pallas_call(strips_x, out_shape=(struct(3, planes_z, 2, SUB, width_y),...]
    ppermute x11, waiting for transfers between devices: 7.75 us -> 5.31 us  [pair(): return lax.ppermute(block, ('gx', 'gy'), route)]
    ppermute x11, starting transfers between devices: 19.4 us -> 17.8 us  [pair(): return lax.ppermute(block, ('gx', 'gy'), route)]
    pallas_call x2 -> x3, Pallas kernels: 5.16 us -> 5.97 us  [the longest x1 2.26 us: on_device(): pl.pallas_call(pack_x, out_shape=(face, face), in_specs=[HBM] * 5, out_sp...]
  transfers between devices with their start and end apart: 11 -> 11, of which waited for: 7 -> 5; matrix products, arithmetic and copies ran while one was open for 0% -> 0% of each run, Pallas kernels for 27% -> 26%
where the time goes in v2:
time: 39.6 us; the launch traced here: 39.4 us
  starting transfers between devices  17.8 us (45%)
  Pallas kernels  14.8 us (37%)
  waiting for transfers between devices  5.31 us (13%)
  between operations  0.88 us (2%)
  other arithmetic  0.61 us (2%)
    ppermute x11, starting transfers between devices, pair(): return lax.ppermute(block, ('gx', 'gy'), route)  17.8 us
    ppermute x11, waiting for transfers between devices, pair(): return lax.ppermute(block, ('gx', 'gy'), route)  5.31 us
    pallas_call x1, Pallas kernels, on_device(): pl.pallas_call(merge, grid=(3,), out_shape=(struct(3, planes_z, width_x,...  2.44 us
    pallas_call x1, Pallas kernels, on_device(): pl.pallas_call(pack_x, out_shape=(face, face), in_specs=[HBM] * 5, out_sp...  2.26 us
    pallas_call x1, Pallas kernels, on_device(): pl.pallas_call(interior_rest, out_shape=(full, full, struct(SUB, LANES)),...  2.01 us
    pallas_call x1, Pallas kernels, on_device(): pl.pallas_call(gradient, out_shape=(struct(devices * rows_mine, lines, LA...  1.79 us
    pallas_call x1, Pallas kernels, on_device(): pl.pallas_call(build_strips, out_shape=struct(8, width_x, LANES), in_spec...  1.75 us
    pallas_call x1, Pallas kernels, on_device(): pl.pallas_call(interior_first, out_shape=(middle, middle, struct(3, PLANE...  1.71 us
  transfers between devices with their start and end apart: 11, of which 5 were waited for; matrix products, arithmetic and copies ran while one was open for 0% of the time, Pallas kernels for 26%

profile of v2, /device:TPU:0, one launch (start us, length us, event | category | flops | bytes accessed | tf_op | source)
XLA Modules:
  0.0 39.4 jit_solution(15294215871723763104)
XLA Ops:
  0.7 2.3 %pack_x.1 = (f32[15,8,256]{2,1,0:T(8,128)}, f32[15,8,256]{2,1,0:T(8,128)}) custom-call(f32[3,8,64,256]{3,2,1,0:T(8,128)} %e_ref.7, f32[3,8,64,256]{3,2,1,0:T(8,128)} %h_ref.7, s32[8,64,256]{2,1,0:T(8,128)} %m_ref.7, f32[64,256]{1,0:T(8,128)} %d_ref.5, s32[1,4]{1,0:T(1,128)} %map_ref.3), custom_call_target="tpu_custom_call" | custom-call | tf_op jit(solution)/shard_map/pack_x/pallas_call | solution.py:715
  3.0 3.0 %collective-permute-start = (f32[15,8,256]{2,1,0:T(8,128)}, f32[15,8,256]{2,1,0:T(8,128)S(1)}, u32[]{:S(2)}, u32[]{:S(2)}) collective-permute-start(f32[15,8,256]{2,1,0:T(8,128)} %get-tuple-element.44), channel_id=1, source_target_pairs={{0,4},{1,5},{2,6},{3,7},{4,0},{5,1},{6,2},{7,3},{8,12},{9,13},{10,... | collective-permute-start | bytes 368648 | tf_op jit(solution)/shard_map/ppermute | solution.py:706
  6.0 0.8 %collective-permute-start.1 = (f32[15,8,256]{2,1,0:T(8,128)}, f32[15,8,256]{2,1,0:T(8,128)S(1)}, u32[]{:S(2)}, u32[]{:S(2)}) collective-permute-start(f32[15,8,256]{2,1,0:T(8,128)} %get-tuple-element.45), channel_id=1, source_target_pairs={{4,8},{5,9},{6,10},{7,11},{8,4},{9,5},{10,6},{11,7},{12,16},{13,17... | collective-permute-start | bytes 368648 | tf_op jit(solution)/shard_map/ppermute | solution.py:706
  6.8 1.8 %build_strips.1.s_ref = f32[8,64,128]{2,1,0:T(8,128)S(1)} custom-call(f32[3,8,64,256]{3,2,1,0:T(8,128)S(1)} %copy-done, f32[3,8,64,256]{3,2,1,0:T(8,128)S(1)} %copy-done.1, s32[8,64,256]{2,1,0:T(8,128)S(1)} %copy-done.2, f32[64,256]{1,0:T(8,128)S(1)} %copy-done.5, s32[1,4]{1,0:T(1,128)S(1)} %copy-done.7), custom_call_target="tpu_custom_call" | custom-call | flops 1 | bytes 1 | tf_op jit(solution)/shard_map/build_strips/pallas_call | solution.py:733
  8.6 1.7 %interior_first.1 = (f32[3,5,64,256]{3,2,1,0:T(8,128)S(1)}, f32[3,5,64,256]{3,2,1,0:T(8,128)S(1)}, f32[3,2,64,256]{3,2,1,0:T(8,128)S(1)}, f32[64,256]{1,0:T(8,12...) custom-call(f32[3,8,64,256]{3,2,1,0:T(8,128)S(1)} %copy-done, ...), custom_call_target="tpu_custom_call" | custom-call | flops 1 | bytes 1 | tf_op jit(solution)/shard_map/interior_first/pallas_call | solution.py:761
  10.4 0.3 pack_y.1
  10.8 0.7 %collective-permute-start.3 = (f32[72,128]{1,0:T(8,128)S(1)}, f32[72,128]{1,0:T(8,128)S(1)}, u32[]{:S(2)}, u32[]{:S(2)}) collective-permute-start(f32[72,128]{1,0:T(8,128)S(1)} %get-tuple-element.51), channel_id=1, source_target_pairs={{1,2},{2,1},{5,6},{6,5},{9,10},{10,9},{13,14},{14,13},{17,18},{18,... | collective-permute-start | bytes 110600 | tf_op jit(solution)/shard_map/ppermute | solution.py:706
  11.5 1.3 %transform.1 = (f32[64,256]{1,0:T(8,128)S(1)}, f32[2,3,2,64,256]{4,3,2,1,0:T(8,128)S(1)}) custom-call(f32[4,2,3,2,64,256]{5,4,3,2,1,0:T(8,128)S(1)} %copy-done.3, bf16[4,2,3,2,64,256]{5,4,3,2,1,0:T(8,128)(2,1)S(1)} %copy-done.4), custom_call_target="tpu_custom_call" | custom-call | flops 1 | bytes 1 | tf_op jit(solution)/shard_map/transform/pallas_call | solution.py:745
  12.7 1.2 %strips_x.1 = (f32[3,8,2,8,256]{4,3,2,1,0:T(8,128)S(1)}, f32[3,8,2,8,256]{4,3,2,1,0:T(8,128)S(1)}, f32[3,2,2,8,256]{4,3,2,1,0:T(8,128)S(1)}, f32[2,8,256]{2,1,0:T(8,128)S(1)}) custom-call(f32[3,8,64,256]{3,2,1,0:T(8,128)S(1)} %copy-done, f32[3,8,64,256]{3,2,1,0:T(8,128)S(1)} %copy-done.1, s32[8,64,256]{2,1,0:T(8,128)S(1)} %copy-done.2, ...), custom_call_target="tpu_custom_call" | custom-call | flops 1 | bytes 1 | tf_op jit(solution)/shard_map/strips_x/pallas_call | solution.py:793
  13.9 1.8 %gradient.1 = (f32[32,32,128]{2,1,0:T(8,128)S(1)}, f32[3,72,128]{2,1,0:T(8,128)S(1)}, f32[3,72,128]{2,1,0:T(8,128)S(1)}) custom-call(f32[8,64,128]{2,1,0:T(8,128)S(1)} %build_strips.1.s_ref, f32[8,8,128]{2,1,0:T(8,128)S(1)} %get-tuple-element.49.t_ref, f32[72,128]{1,0:T(8,128)S(1)} %collective-permute-done.2.ya_ref, ...), custom_call_target="tpu_custom_call" | custom-call | flops 1 | bytes 1 | tf_op jit(solution)/shard_map/gradient/pallas_call | solution.py:817
  15.7 2.9 %collective-permute-start.4 = (f32[16,32,128]{2,1,0:T(8,128)S(1)}, f32[16,32,128]{2,1,0:T(8,128)S(1)}, u32[]{:S(2)}, u32[]{:S(2)}) collective-permute-start(f32[16,32,128]{2,1,0:T(8,128)S(1)} %slice.3), channel_id=1, source_target_pairs={{0,1},{1,0},{2,3},{3,2},{4,5},{5,4},{6,7},{7,6},{8,9},{9,8},{10,11... | collective-permute-start | bytes 786440 | tf_op jit(solution)/shard_map/ppermute | solution.py:706
  18.7 1.2 %collective-permute-done.4.refs_1_ = f32[16,32,128]{2,1,0:T(8,128)S(1)} collective-permute-done((f32[16,32,128]{2,1,0:T(8,128)S(1)}, f32[16,32,128]{2,1,0:T(8,128)S(1)}, u32[]{:S(2)}, u32[]{:S(2)}) %collective-permute-start.4) | collective-permute-done | bytes 262176 | tf_op jit(solution)/shard_map/ppermute | solution.py:706
  19.9 4.4 %collective-permute-start.5 = (f32[4,32,128]{2,1,0:T(8,128)S(1)}, f32[4,32,128]{2,1,0:T(8,128)S(1)}, u32[]{:S(2)}, u32[]{:S(2)}) collective-permute-start(f32[4,32,128]{2,1,0:T(8,128)S(1)} %get-tuple-element.63), channel_id=1, source_target_pairs={{0,4},{1,5},{2,6},{3,7},{4,0},{5,1},{6,2},{7,3},{8,12},{9,13},{10,... | collective-permute-start | bytes 196616 | tf_op jit(solution)/shard_map/ppermute | solution.py:706
  24.2 1.1 %collective-permute-start.6 = (f32[4,32,128]{2,1,0:T(8,128)S(1)}, f32[4,32,128]{2,1,0:T(8,128)S(1)}, u32[]{:S(2)}, u32[]{:S(2)}) collective-permute-start(f32[4,32,128]{2,1,0:T(8,128)S(1)} %get-tuple-element.64), channel_id=1, source_target_pairs={{0,2},{1,3},{2,0},{3,1},{4,6},{5,7},{6,4},{7,5},{8,10},{9,11},{10,... | collective-permute-start | bytes 196616 | tf_op jit(solution)/shard_map/ppermute | solution.py:706
  25.3 0.4 %collective-permute-start.7 = (f32[4,32,128]{2,1,0:T(8,128)S(1)}, f32[4,32,128]{2,1,0:T(8,128)S(1)}, u32[]{:S(2)}, u32[]{:S(2)}) collective-permute-start(f32[4,32,128]{2,1,0:T(8,128)S(1)} %get-tuple-element.65), channel_id=1, source_target_pairs={{0,6},{1,7},{2,4},{3,5},{4,2},{5,3},{6,0},{7,1},{8,14},{9,15},{10,... | collective-permute-start | bytes 196616 | tf_op jit(solution)/shard_map/ppermute | solution.py:706
  25.8 2.0 %interior_rest.1 = (f32[3,8,64,256]{3,2,1,0:T(8,128)S(1)}, f32[3,8,64,256]{3,2,1,0:T(8,128)S(1)}, f32[8,128]{1,0:T(8,128)S(1)}) custom-call(f32[3,8,64,256]{3,2,1,0:T(8,128)S(1)} %copy-done, f32[3,8,64,256]{3,2,1,0:T(8,128)S(1)} %copy-done.1, s32[8,64,256]{2,1,0:T(8,128)S(1)} %copy-done.2, f32[4]{0:T(128)S(1)} %copy-done.6, ...), custom_call_target="tpu_custom_call" | custom-call | flops 1 | bytes 1 | tf_op jit(solution)/shard_map/interior_rest/pallas_call | solution.py:772
  27.8 1.2 %collective-permute-done.6.refs_2_ = f32[4,32,128]{2,1,0:T(8,128)S(1)} collective-permute-done((f32[4,32,128]{2,1,0:T(8,128)S(1)}, f32[4,32,128]{2,1,0:T(8,128)S(1)}, u32[]{:S(2)}, u32[]{:S(2)}) %collective-permute-start.6) | collective-permute-done | bytes 65568 | tf_op jit(solution)/shard_map/ppermute | solution.py:706
  29.0 1.5 %collective-permute-done.7.refs_3_ = f32[4,32,128]{2,1,0:T(8,128)S(1)} collective-permute-done((f32[4,32,128]{2,1,0:T(8,128)S(1)}, f32[4,32,128]{2,1,0:T(8,128)S(1)}, u32[]{:S(2)}, u32[]{:S(2)}) %collective-permute-start.7) | collective-permute-done | bytes 65568 | tf_op jit(solution)/shard_map/ppermute | solution.py:706
  30.5 3.7 %collective-permute-start.10 = (f32[1,32,128]{2,1,0:T(8,128)S(1)}, f32[1,32,128]{2,1,0:T(8,128)S(1)}, u32[]{:S(2)}, u32[]{:S(2)}) collective-permute-start(f32[1,32,128]{2,1,0:T(8,128)S(1)} %get-tuple-element.70), channel_id=1, source_target_pairs={{0,24},{1,25},{2,26},{3,27},{4,28},{5,29},{6,30},{7,31},{8,16},{9,... | collective-permute-start | bytes 49160 | tf_op jit(solution)/shard_map/ppermute | solution.py:706
  34.2 0.8 %collective-permute-start.9 = (f32[1,32,128]{2,1,0:T(8,128)S(1)}, f32[1,32,128]{2,1,0:T(8,128)S(1)}, u32[]{:S(2)}, u32[]{:S(2)}) collective-permute-start(f32[1,32,128]{2,1,0:T(8,128)S(1)} %get-tuple-element.69), channel_id=1, source_target_pairs={{0,16},{1,17},{2,18},{3,19},{4,20},{5,21},{6,22},{7,23},{8,24},{9,... | collective-permute-start | bytes 49160 | tf_op jit(solution)/shard_map/ppermute | solution.py:706
  35.0 2.4 %merge.1 = (f32[3,8,64,256]{3,2,1,0:T(8,128)}, f32[3,8,64,256]{3,2,1,0:T(8,128)}) custom-call(f32[3,8,64,256]{3,2,1,0:T(8,128)S(1)} %get-tuple-element.42.e_ref, f32[3,8,64,256]{3,2,1,0:T(8,128)S(1)} %get-tuple-element.43.h_ref, f32[3,5,64,256]{3,2,1,0:T(8,128)S(1)} %get-tuple-element.37.em.e2_ref, f32[3,5,64,256]{3,2,1,0:T(8,128)S(1)} %get-tuple-element.38.hm, ...), custom_call_target="tpu_custom_call" | custom-call | flops 1 | bytes 1 | tf_op jit(solution)/shard_map/merge/pallas_call | solution.py:852
  37.4 0.5 %collective-permute-done.8 = f32[1,32,128]{2,1,0:T(8,128)S(1)} collective-permute-done((f32[1,32,128]{2,1,0:T(8,128)S(1)}, f32[1,32,128]{2,1,0:T(8,128)S(1)}, u32[]{:S(2)}, u32[]{:S(2)}) %collective-permute-start.8) | collective-permute-done | bytes 16416 | tf_op jit(solution)/shard_map/ppermute | solution.py:706
  37.9 0.9 %collective-permute-done.9 = f32[1,32,128]{2,1,0:T(8,128)S(1)} collective-permute-done((f32[1,32,128]{2,1,0:T(8,128)S(1)}, f32[1,32,128]{2,1,0:T(8,128)S(1)}, u32[]{:S(2)}, u32[]{:S(2)}) %collective-permute-start.9) | collective-permute-done | bytes 16416 | tf_op jit(solution)/shard_map/ppermute | solution.py:706
  38.8 0.6 %add_add_fusion = f32[1,32,128]{2,1,0:T(8,128)} fusion(f32[1,32,128]{2,1,0:T(8,128)S(1)} %collective-permute-done.10, f32[1,32,128]{2,1,0:T(8,128)S(1)} %collective-permute-done.9, f32[1,32,128]{2,1,0:T(8,128)S(1)} %get-tuple-element.67, f32[1,32,128]{2,1,0:T(8,128)S(1)} %collective-permute-done.8), kind=kLoop, calls=%fused_computation | loop fusion | flops 12288 | bytes 81920 | tf_op jit(solution)/shard_map/add | solution.py:871
  (27 shorter events, 0.2 us)
Async XLA Ops:
  0.6 6.2 %copy-start.5 = (f32[64,256]{1,0:T(8,128)S(1)}, f32[64,256]{1,0:T(8,128)}, u32[]{:S(2)}) copy-start(f32[64,256]{1,0:T(8,128)} %d_ref.5) | copy-start | bytes 196612
  0.6 6.2 %copy-start.2 = (s32[8,64,256]{2,1,0:T(8,128)S(1)}, s32[8,64,256]{2,1,0:T(8,128)}, u32[]{:S(2)}) copy-start(s32[8,64,256]{2,1,0:T(8,128)} %m_ref.7) | copy-start | bytes 1572868
  0.7 6.2 %copy-start = (f32[3,8,64,256]{3,2,1,0:T(8,128)S(1)}, f32[3,8,64,256]{3,2,1,0:T(8,128)}, u32[]{:S(2)}) copy-start(f32[3,8,64,256]{3,2,1,0:T(8,128)} %e_ref.7) | copy-start | bytes 4718596
  0.7 6.2 %copy-start.1 = (f32[3,8,64,256]{3,2,1,0:T(8,128)S(1)}, f32[3,8,64,256]{3,2,1,0:T(8,128)}, u32[]{:S(2)}) copy-start(f32[3,8,64,256]{3,2,1,0:T(8,128)} %h_ref.7) | copy-start | bytes 4718596
  0.7 6.2 %copy-start.7 = (s32[1,4]{1,0:T(1,128)S(1)}, s32[1,4]{1,0:T(1,128)}, u32[]{:S(2)}) copy-start(s32[1,4]{1,0:T(1,128)} %map_ref.3) | copy-start | bytes 52
  3.0 7.4 %collective-permute-start = (f32[15,8,256]{2,1,0:T(8,128)}, f32[15,8,256]{2,1,0:T(8,128)S(1)}, u32[]{:S(2)}, u32[]{:S(2)}) collective-permute-start(f32[15,8,256]{2,1,0:T(8,128)} %get-tuple-element.44), channel_id=1, source_target_pairs={{0,4},{1,5},{2,6},{3,7},{4,0},{5,1},{6,2},{7,3},{8,12},{9,13},{10,... | collective-permute-start | bytes 368648 | tf_op jit(solution)/shard_map/ppermute | solution.py:706
  6.0 2.6 %copy-start.6 = (f32[4]{0:T(128)S(1)}, f32[4]{0:T(128)}, u32[]{:S(2)}) copy-start(f32[4]{0:T(128)} %table.7) | copy-start | bytes 52
  6.0 4.4 %collective-permute-start.1 = (f32[15,8,256]{2,1,0:T(8,128)}, f32[15,8,256]{2,1,0:T(8,128)S(1)}, u32[]{:S(2)}, u32[]{:S(2)}) collective-permute-start(f32[15,8,256]{2,1,0:T(8,128)} %get-tuple-element.45), channel_id=1, source_target_pairs={{4,8},{5,9},{6,10},{7,11},{8,4},{9,5},{10,6},{11,7},{12,16},{13,17... | collective-permute-start | bytes 368648 | tf_op jit(solution)/shard_map/ppermute | solution.py:706
  6.8 4.6 %copy-start.4 = (bf16[4,2,3,2,64,256]{5,4,3,2,1,0:T(8,128)(2,1)S(1)}, bf16[4,2,3,2,64,256]{5,4,3,2,1,0:T(8,128)(2,1)}, u32[]{:S(2)}) copy-start(bf16[4,2,3,2,64,256]{5,4,3,2,1,0:T(8,128)(2,1)} %fwd_ref.1) | copy-start | bytes 4718596
  8.6 2.8 %copy-start.3 = (f32[4,2,3,2,64,256]{5,4,3,2,1,0:T(8,128)S(1)}, f32[4,2,3,2,64,256]{5,4,3,2,1,0:T(8,128)}, u32[]{:S(2)}) copy-start(f32[4,2,3,2,64,256]{5,4,3,2,1,0:T(8,128)} %adj_ref.1) | copy-start | bytes 9437188
  10.7 3.2 %collective-permute-start.2 = (f32[72,128]{1,0:T(8,128)S(1)}, f32[72,128]{1,0:T(8,128)S(1)}, u32[]{:S(2)}, u32[]{:S(2)}) collective-permute-start(f32[72,128]{1,0:T(8,128)S(1)} %get-tuple-element.50), channel_id=1, source_target_pairs={{0,1},{1,0},{2,3},{3,2},{4,5},{5,4},{6,7},{7,6},{8,9},{9,8},{10,11... | collective-permute-start | bytes 110600 | tf_op jit(solution)/shard_map/ppermute | solution.py:706
  10.8 3.1 %collective-permute-start.3 = (f32[72,128]{1,0:T(8,128)S(1)}, f32[72,128]{1,0:T(8,128)S(1)}, u32[]{:S(2)}, u32[]{:S(2)}) collective-permute-start(f32[72,128]{1,0:T(8,128)S(1)} %get-tuple-element.51), channel_id=1, source_target_pairs={{1,2},{2,1},{5,6},{6,5},{9,10},{10,9},{13,14},{14,13},{17,18},{18,... | collective-permute-start | bytes 110600 | tf_op jit(solution)/shard_map/ppermute | solution.py:706
  15.7 4.1 %collective-permute-start.4 = (f32[16,32,128]{2,1,0:T(8,128)S(1)}, f32[16,32,128]{2,1,0:T(8,128)S(1)}, u32[]{:S(2)}, u32[]{:S(2)}) collective-permute-start(f32[16,32,128]{2,1,0:T(8,128)S(1)} %slice.3), channel_id=1, source_target_pairs={{0,1},{1,0},{2,3},{3,2},{4,5},{5,4},{6,7},{7,6},{8,9},{9,8},{10,11... | collective-permute-start | bytes 786440 | tf_op jit(solution)/shard_map/ppermute | solution.py:706
  19.9 7.9 %collective-permute-start.5 = (f32[4,32,128]{2,1,0:T(8,128)S(1)}, f32[4,32,128]{2,1,0:T(8,128)S(1)}, u32[]{:S(2)}, u32[]{:S(2)}) collective-permute-start(f32[4,32,128]{2,1,0:T(8,128)S(1)} %get-tuple-element.63), channel_id=1, source_target_pairs={{0,4},{1,5},{2,6},{3,7},{4,0},{5,1},{6,2},{7,3},{8,12},{9,13},{10,... | collective-permute-start | bytes 196616 | tf_op jit(solution)/shard_map/ppermute | solution.py:706
  24.2 4.8 %collective-permute-start.6 = (f32[4,32,128]{2,1,0:T(8,128)S(1)}, f32[4,32,128]{2,1,0:T(8,128)S(1)}, u32[]{:S(2)}, u32[]{:S(2)}) collective-permute-start(f32[4,32,128]{2,1,0:T(8,128)S(1)} %get-tuple-element.64), channel_id=1, source_target_pairs={{0,2},{1,3},{2,0},{3,1},{4,6},{5,7},{6,4},{7,5},{8,10},{9,11},{10,... | collective-permute-start | bytes 196616 | tf_op jit(solution)/shard_map/ppermute | solution.py:706
  25.3 5.2 %collective-permute-start.7 = (f32[4,32,128]{2,1,0:T(8,128)S(1)}, f32[4,32,128]{2,1,0:T(8,128)S(1)}, u32[]{:S(2)}, u32[]{:S(2)}) collective-permute-start(f32[4,32,128]{2,1,0:T(8,128)S(1)} %get-tuple-element.65), channel_id=1, source_target_pairs={{0,6},{1,7},{2,4},{3,5},{4,2},{5,3},{6,0},{7,1},{8,14},{9,15},{10,... | collective-permute-start | bytes 196616 | tf_op jit(solution)/shard_map/ppermute | solution.py:706
  30.5 6.9 %collective-permute-start.10 = (f32[1,32,128]{2,1,0:T(8,128)S(1)}, f32[1,32,128]{2,1,0:T(8,128)S(1)}, u32[]{:S(2)}, u32[]{:S(2)}) collective-permute-start(f32[1,32,128]{2,1,0:T(8,128)S(1)} %get-tuple-element.70), channel_id=1, source_target_pairs={{0,24},{1,25},{2,26},{3,27},{4,28},{5,29},{6,30},{7,31},{8,16},{9,... | collective-permute-start | bytes 49160 | tf_op jit(solution)/shard_map/ppermute | solution.py:706
  34.2 3.7 %collective-permute-start.8 = (f32[1,32,128]{2,1,0:T(8,128)S(1)}, f32[1,32,128]{2,1,0:T(8,128)S(1)}, u32[]{:S(2)}, u32[]{:S(2)}) collective-permute-start(f32[1,32,128]{2,1,0:T(8,128)S(1)} %get-tuple-element.68), channel_id=1, source_target_pairs={{0,8},{1,9},{2,10},{3,11},{4,12},{5,13},{6,14},{7,15},{8,0},{9,1},... | collective-permute-start | bytes 49160 | tf_op jit(solution)/shard_map/ppermute | solution.py:706
  34.2 4.6 %collective-permute-start.9 = (f32[1,32,128]{2,1,0:T(8,128)S(1)}, f32[1,32,128]{2,1,0:T(8,128)S(1)}, u32[]{:S(2)}, u32[]{:S(2)}) collective-permute-start(f32[1,32,128]{2,1,0:T(8,128)S(1)} %get-tuple-element.69), channel_id=1, source_target_pairs={{0,16},{1,17},{2,18},{3,19},{4,20},{5,21},{6,22},{7,23},{8,24},{9,... | collective-permute-start | bytes 49160 | tf_op jit(solution)/shard_map/ppermute | solution.py:706

commit v3 on v2

--- a/solution.py
+++ b/solution.py
@@ -110,123 +110,170 @@
     return out
 
 
-def n_faces(planes_z):
-    return 7 * planes_z + 1
-
-
-def edge_tile(q, start, e_ref, h_ref, m_ref, d_ref, ids=None):
-    planes_z = m_ref.shape[0]
-    field, z = divmod(q, planes_z)
-    rows = pl.ds(start, SUB)
-    if field < 3:
-        return e_ref[field, z, rows]
-    if field < 6:
-        return h_ref[field - 3, z, rows]
-    if field > 6:
-        return ids
-    return d_ref[rows] if in_design(z) else m_ref[z, rows].astype(F32)
+TILES = 10
+BEHIND = (0, 1, 2, 4, 5)
 
 
 def pack_x(e_in, h_in, m_in, d_in, map_in, a_ref, b_ref, eb, hb, mb, db, map_ref, sems):
     planes_z, size, width_y = m_in.shape
-    fields = ((e_in, eb), (h_in, hb), (m_in, mb))
+    span = 2 * SUB
+    tiles = width_y // LANES
+    views = [
+        (e_in, eb.reshape(tiles, 3, planes_z, span, LANES)),
+        (h_in, hb.reshape(tiles, 3, planes_z, span, LANES)),
+        (m_in, mb.reshape(tiles, planes_z, span, LANES)),
+    ]
     copies = []
     for k, start in enumerate((0, size - SUB)):
         here, there = pl.ds(start, SUB), pl.ds(k * SUB, SUB)
-        for n, (src, dst) in enumerate(fields):
-            source = src.at[:, here] if n == 2 else src.at[:, :, here]
-            target = dst.at[:, there] if n == 2 else dst.at[:, :, there]
-            copies.append(pltpu.make_async_copy(source, target, sems.at[4 * k + n]))
-        copies.append(pltpu.make_async_copy(d_in.at[here], db.at[there], sems.at[4 * k + 3]))
-    copies.append(pltpu.make_async_copy(map_in, map_ref, sems.at[8]))
+        for u in range(tiles):
+            lanes = pl.ds(u * LANES, LANES)
+            for n, (src, dst) in enumerate(views):
+                source = src.at[:, here, lanes] if n == 2 else src.at[:, :, here, lanes]
+                target = dst.at[u, :, there] if n == 2 else dst.at[u, :, :, there]
+                copies.append(pltpu.make_async_copy(source, target, sems.at[len(copies)]))
+        copies.append(pltpu.make_async_copy(d_in.at[here], db.at[there], sems.at[len(copies)]))
+    copies.append(pltpu.make_async_copy(map_in, map_ref, sems.at[len(copies)]))
     for copy in copies:
         copy.start()
-    even = lax.axis_index("gx") % 2 == 0
-    sub = iota((SUB, width_y), 0)
+    gx, gy = lax.axis_index("gx"), lax.axis_index("gy")
+    total_x, total_y = size * lax.axis_size("gx"), width_y * lax.axis_size("gy")
+    shape = (SUB, width_y)
+    sub = iota(shape, 0)
+    rows = jnp.full(shape, (gx + 1) * size - 2, jnp.int32).astype(F32)
+    cols = (iota(shape, 1) + gy * width_y).astype(F32)
+    damping, coef_h, _ = edge_coefs(rows, cols, total_x, total_y)
+    layer = (sub >= ZLO) & (sub < ZLO + PLANES)
     for copy in copies:
         copy.wait()
-    for group in range(a_ref.shape[0]):
-        low = jnp.zeros((SUB, width_y), F32)
-        high = low
-        for k in range(4):
-            q = 4 * group + k
-            if q >= n_faces(planes_z):
-                break
-            ids = [None, None]
-            if q == n_faces(planes_z) - 1:
-                ids = [id_row(map_ref, tx, (SUB, width_y)) for tx in (0, map_ref.shape[0] - 1)]
-            tiles = [edge_tile(q, n * SUB, eb, hb, mb, db, ids[n]) for n in range(2)]
-            low = jnp.where(sub // 2 == k, turn(tiles[0], 2 * k, 0), low)
-            high = jnp.where(sub // 2 == k, turn(tiles[1], 2 * k - 6, 0), high)
-        a_ref[group] = jnp.where(even, high, low)
-        b_ref[group] = jnp.where(even, low, high)
-
-
-def halo_rows(a_ref, b_ref, q, even):
-    group, k = divmod(q, 4)
-    a, b = a_ref[group], b_ref[group]
-    below = jnp.where(even, b, a)
-    above = jnp.where(even, a, b)
-    return turn(below, -2 * k, 0), turn(above, -2 * k, 0)
-
-
-def to_strip(values, z, acc):
-    lane = iota((values.shape[0], LANES), 1) - z * GROUP
-    half = GROUP // 2
-    low = turn(values[:, :LANES], z * GROUP + 2, 1)
-    high = turn(values[:, -LANES:], z * GROUP + half - (LANES - half + 2), 1)
-    acc = jnp.where((lane >= 2) & (lane < half), low, acc)
-    return jnp.where((lane >= half) & (lane < GROUP - 2), high, acc)
+
+    def row(ref, c, r):
+        rows = pl.ds(c * planes_z * span + r, planes_z, stride=span)
+        return jnp.concatenate([ref[u, rows] for u in range(tiles)], axis=1)
+
+    near, far = span - 1, span - 2
+    ex, ey, ez = (row(eb, c, far) for c in range(3))
+    up = jnp.where(sub == SUB - 1, 0.0, turn(ex, SUB - 1, 0))
+    curl_y = (up - ex) - (row(eb, 2, near) - ez)
+    curl_z = (row(eb, 1, near) - ey) - (turn(ex, width_y - 1, 1) - ex)
+    mag = [row(hb, c, far) for c in (1, 2)]
+    high = [row(eb, c, near) for c in range(3)] + [row(hb, c, near) for c in range(3)]
+    high += [damping * h - coef_h * curl for h, curl in zip(mag, (curl_y, curl_z))]
+    low = [row(eb, c, 0) for c in range(3)] + [row(hb, c, 0) for c in range(3)]
+    low += [row(eb, 1, 1), row(eb, 2, 1)]
+    for side, edge, further, tx in ((low, 0, 1, 0), (high, near, far, map_ref.shape[0] - 1)):
+        density = jnp.broadcast_to(db[edge : edge + 1], shape)
+        side.append(jnp.where(layer, density, row(mb, 0, edge).astype(F32)))
+        misc = jnp.broadcast_to(db[further : further + 1], shape)
+        side.append(jnp.where(sub == 1, id_row(map_ref, tx, shape), misc))
+    strips = [row_to_strip(v) for v in [ex, ey, ez] + mag]
+    strips.append(strips[-1])
+    for k in range(3):
+        pair_of = jnp.concatenate([strips[2 * k], strips[2 * k + 1]], axis=1)
+        high[-1] = jnp.where(sub == 2 + k, jnp.broadcast_to(pair_of, shape), high[-1])
+    even = gx % 2 == 0
+    for k in range(TILES):
+        a_ref[k] = jnp.where(even, high[k], low[k])
+        b_ref[k] = jnp.where(even, low[k], high[k])
+
+
+def neighbours(axis, from_a, from_b):
+    here = lax.axis_index(axis)
+    even = here % 2 == 0
+    before = jnp.where(here > 0, jnp.where(even, from_b, from_a), 0.0)
+    after = jnp.where(here < lax.axis_size(axis) - 1, jnp.where(even, from_a, from_b), 0.0)
+    return before, after
+
+
+def x_halos(xa_ref, xb_ref):
+    both = [neighbours("gx", xa_ref[k], xb_ref[k]) for k in range(TILES)]
+    return [t[0] for t in both], [t[1] for t in both]
+
+
+def ends(values):
+    lane = iota((values.shape[0], LANES), 1)
+    return jnp.where(lane < LANES // 2, values[:, :LANES], values[:, -LANES:])
+
+
+def row_to_strip(values):
+    shape = (SUB, LANES)
+    rolled = pltpu.roll(ends(values), GROUP // 2, 1, stride=GROUP, stride_axis=0)
+    rolled = jnp.where(iota(shape, 1) // GROUP == iota(shape, 0), rolled, 0.0)
+    return jnp.sum(rolled, axis=0, keepdims=True)
 
 
 def build_strips(e_ref, h_ref, m_ref, d_ref, map_ref, s_ref):
     planes_z, width_x, width_y = m_ref.shape
-    zero = jnp.zeros((width_x, LANES), F32)
+    group = iota((SUB, LANES), 1) // GROUP
+
+    def gather(get, here):
+        acc = jnp.zeros((SUB, LANES), F32)
+        for z in range(planes_z):
+            acc = jnp.where(group == z, turn(ends(get(z, here)), z * GROUP + GROUP // 2, 1), acc)
+        return acc
 
     def body(c, _):
         for base, ref in ((0, e_ref), (3, h_ref)):
-            acc = zero
-            for z in range(planes_z):
-                acc = to_strip(ref[c, z], z, acc)
-            s_ref[base + c] = acc
+            for start in range(0, width_x, SUB):
+                here = pl.ds(start, SUB)
+                s_ref[base + c, here] = gather(lambda z, here: ref[c, z, here], here)
         return 0
 
     lax.fori_loop(0, 3, body, 0)
-    acc = zero
-    for z in range(planes_z):
-        acc = to_strip(d_ref[...] if in_design(z) else m_ref[z].astype(F32), z, acc)
-    s_ref[6] = acc
-    for tx in range(width_x // TILE):
-        rows = pl.ds(tx * TILE, TILE)
-        row = id_row(map_ref, tx, (TILE, width_y))
-        s_ref[7, rows] = to_strip(row, 0, jnp.zeros((TILE, LANES), F32))
+
+    def source(z, here):
+        return d_ref[here] if in_design(z) else m_ref[z, here].astype(F32)
+
+    for start in range(0, width_x, SUB):
+        here = pl.ds(start, SUB)
+        s_ref[6, here] = gather(source, here)
+        row = id_row(map_ref, start // TILE, (SUB, width_y))
+        s_ref[7, here] = turn(ends(row), GROUP // 2, 1)
 
 
 def pack_y(s_ref, xa_ref, xb_ref, _after, t_ref, a_ref, b_ref):
-    planes_z = LANES // GROUP
     width_x = s_ref.shape[1]
-    width_y = xa_ref.shape[2]
-    even_x = lax.axis_index("gx") % 2 == 0
     even_y = lax.axis_index("gy") % 2 == 0
-    sub = iota((SUB, width_y), 0)
+    below, above = x_halos(xa_ref, xb_ref)
+    shape = (SUB, LANES)
+    sub = iota(shape, 0)
+
+    def row(tile, k):
+        return jnp.broadcast_to(tile[k : k + 1], tile.shape)
+
+    def wide(values):
+        return jnp.broadcast_to(values, shape)
+
+    zero = jnp.zeros(shape, F32)
     tails = []
     for f in range(8):
-        acc = jnp.zeros((SUB, LANES), F32)
-        for z in range(planes_z if f < 7 else 1):
-            below, above = halo_rows(xa_ref, xb_ref, f * planes_z + z, even_x)
-            halo = jnp.where(sub < 2, above, jnp.where(sub >= 6, turn(below, 6, 0), 0.0))
-            acc = to_strip(halo, z, acc)
-        t_ref[f] = acc
-        tails.append(acc)
+        if f < 7:
+            k = 8 if f == 6 else f
+            after_1, before_1 = (wide(row_to_strip(side[k])) for side in (above, below))
+        else:
+            after_1, before_1 = (wide(row_to_strip(row(side[9], 1))) for side in (above, below))
+        after_2, before_2 = zero, zero
+        if f in (1, 2):
+            after_2 = wide(row_to_strip(above[5 + f]))
+        if f in BEHIND:
+            k = BEHIND.index(f)
+            lanes = (k % 2) * LANES
+            before_2 = wide(below[9][2 + k // 2 : 3 + k // 2, lanes : lanes + LANES])
+        if f == 6:
+            after_2, before_2 = (wide(row_to_strip(row(side[9], 0))) for side in (above, below))
+        tail = jnp.where(sub == 0, after_1, jnp.where(sub == 1, after_2, 0.0))
+        tail = jnp.where(sub == 6, before_2, jnp.where(sub == 7, before_1, tail))
+        t_ref[f] = tail
+        tails.append(tail)
+    lane = iota(shape, 1) % GROUP
     for start in range(0, width_x + SUB, SUB):
-        lane = iota((SUB, LANES), 1) % GROUP
-        low = jnp.zeros((SUB, LANES), F32)
-        high = low
+        low = zero
+        high = zero
         for f in range(8):
             values = tails[f] if start == width_x else s_ref[f, pl.ds(start, SUB)]
             mask = lane // 2 == f
-            low = jnp.where(mask, turn(values, 2 * f - 2, 1), low)
-            high = jnp.where(mask, turn(values, 2 * f - (GROUP - 4), 1), high)
+            low = jnp.where(mask, turn(values, 2 * f - GROUP // 2, 1), low)
+            high = jnp.where(mask, turn(values, 2 * f - (GROUP // 2 - 2), 1), high)
         a_ref[pl.ds(start, SUB)] = jnp.where(even_y, high, low)
         b_ref[pl.ds(start, SUB)] = jnp.where(even_y, low, high)
 
@@ -387,7 +434,6 @@
     planes_z, width_x, width_y = m_ref.shape
     gx, gy = lax.axis_index("gx"), lax.axis_index("gy")
     total_x, total_y = width_x * lax.axis_size("gx"), width_y * lax.axis_size("gy")
-    even = gx % 2 == 0
     shape = (SUB, width_y)
     sub = iota(shape, 0)
     cols = (iota(shape, 1) + gy * width_y).astype(F32)
@@ -395,12 +441,23 @@
     zero = jnp.zeros(shape, F32)
     damps, chs = [], []
 
-    def strip(side, q):
-        below, above = halo_rows(xa_ref, xb_ref, q, even)
-        own = edge_tile(q, side * (width_x - SUB), e_ref, h_ref, m_ref, d_ref)
-        if side == 0:
-            return jnp.where(sub < 2, below, turn(own, 2, 0))
-        return jnp.where(sub >= 6, turn(above, 6, 0), turn(own, 6, 0))
+    below, above = x_halos(xa_ref, xb_ref)
+    edges = pl.ds(0, SUB), pl.ds(width_x - SUB, SUB)
+
+    def place(values, tile, z, at_sub):
+        return jnp.where(sub == at_sub, turn(tile, at_sub - z, 0), values)
+
+    def strip(side, own, near, far, z):
+        out = turn(own, 2 if side == 0 else 6, 0)
+        out = place(out, near, z, 1 if side == 0 else 6)
+        if far is None:
+            return jnp.where(sub == (0 if side == 0 else 7), 0.0, out)
+        return place(out, far[0], far[1], 0 if side == 0 else 7)
+
+    def source(side, z):
+        own = d_ref[edges[side]] if in_design(z) else m_ref[z, edges[side]].astype(F32)
+        halo = (below, above)[side]
+        return strip(side, own, halo[8], (halo[9], 0), z)
 
     for side in range(2):
         rows = (sub + gx * width_x + (-2 if side == 0 else width_x - 6)).astype(F32)
@@ -410,18 +467,20 @@
         chs.append(coef_h)
         for z in range(planes_z):
             for c in range(3):
-                xe[side, c, z] = strip(side, c * planes_z + z)
-                xh[side, c, z + 1] = strip(side, (3 + c) * planes_z + z)
+                halo = (below, above)[side]
+                far = (above[5 + c], z) if side and c else None
+                xe[side, c, z] = strip(side, e_ref[c, z, edges[side]], halo[c], far, z)
+                xh[side, c, z + 1] = strip(side, h_ref[c, z, edges[side]], halo[3 + c], None, z)
         for c in range(3):
             xe[side, c, planes_z] = zero
             xh[side, c, 0] = zero
-        design, slope = design_terms(blur(strip(side, 6 * planes_z + ZLO)))
+        design, slope = design_terms(blur(source(side, ZLO)))
         sl_ref[side] = turn(slope, 6 if side == 0 else 2, 0)
         for z in range(planes_z):
             if in_design(z):
                 ce[side, z] = design * inverse
             else:
-                ce[side, z] = pick(strip(side, 6 * planes_z + z), choices) * inverse
+                ce[side, z] = pick(source(side, z), choices) * inverse
 
     def mag(z):
         for side in range(2):
@@ -448,6 +507,10 @@
     back = (6, 2)
     for n in range(STEPS):
         loop(mag)
+        if n == 0:
+            for z in range(planes_z):
+                for c in (1, 2):
+                    xh[0, c, z + 1] = place(xh[0, c, z + 1], below[5 + c], z, 0)
         loop(elec)
         if n == 0:
             for side in range(2):
@@ -475,11 +538,10 @@
 
 def patch_cols(values, strip, z):
     lane = iota((values.shape[0], LANES), 1)
-    low = turn(strip, -(z * GROUP + 2), 1)
-    high = turn(strip, LANES - 2 - (z * GROUP + GROUP - 4), 1)
+    rolled = turn(strip, -(z * GROUP + GROUP // 2), 1)
     tiles = [values[:, k : k + LANES] for k in range(0, values.shape[1], LANES)]
-    tiles[0] = jnp.where(lane < 2, low, tiles[0])
-    tiles[-1] = jnp.where(lane >= LANES - 2, high, tiles[-1])
+    tiles[0] = jnp.where(lane < 2, rolled, tiles[0])
+    tiles[-1] = jnp.where(lane >= LANES - 2, rolled, tiles[-1])
     return jnp.concatenate(tiles, axis=1)
 
 
@@ -487,14 +549,12 @@
     gx, gy = lax.axis_index("gx"), lax.axis_index("gy")
     total_x, total_y = width_x * lax.axis_size("gx"), width_y * lax.axis_size("gy")
     planes_z = LANES // GROUP
-    even = gy % 2 == 0
     size = width_x + SUB
     shape = (size, LANES)
     lane = iota(shape, 1)
     col = lane % GROUP
     plane = lane // GROUP
-    from_low = jnp.where(even, yb_ref[...], ya_ref[...])
-    from_high = jnp.where(even, ya_ref[...], yb_ref[...])
+    from_low, from_high = neighbours("gy", ya_ref[...], yb_ref[...])
 
     def field(f):
         own = jnp.concatenate([s_ref[f], t_ref[f]], axis=0)
@@ -503,13 +563,27 @@
 
     row = iota(shape, 0)
     row = jnp.where(row >= width_x + 4, row - size, row)
-    place = jnp.where(col < GROUP // 2, col - 2, col + (width_y - GROUP + 2))
+    place = jnp.where(col < GROUP // 2, col + (width_y - GROUP // 2), col - GROUP // 2)
+    place = jnp.where(col < 2, col - 2, place)
+    place = jnp.where(col >= GROUP - 2, col + (width_y - GROUP + 2), place)
     rows = (row + gx * width_x).astype(F32)
     cols = (place + gy * width_y).astype(F32)
     inside = within(rows, cols, total_x, total_y)
     damping, coef_h, inverse = edge_coefs(rows, cols, total_x, total_y, inside)
     source = field(6)
-    design, slope = design_terms(blur(source))
+    half = GROUP // 2
+
+    def next_col(v):
+        jump = (col == 1) | (col == half - 1)
+        return jnp.where(jump, turn(v, 1 - half, 1), turn(v, -1, 1))
+
+    def prev_col(v):
+        jump = (col == half) | (col == GROUP - 2)
+        return jnp.where(jump, turn(v, half - 1, 1), turn(v, 1, 1))
+
+    filtered = turn(source, 1, 0) + 2.0 * source + turn(source, size - 1, 0)
+    filtered = (prev_col(filtered) + 2.0 * filtered + next_col(filtered)) / 16.0
+    design, slope = design_terms(filtered)
     choices = [jnp.tile(c, (size // SUB, 1)) for c in table_inverse(table, (SUB, LANES))]
     layer = (plane >= ZLO) & (plane < ZLO + PLANES)
     coef_e = jnp.where(layer, design, pick(source, choices)) * inverse
@@ -522,7 +596,7 @@
         return turn(v, size - 1, 0) - v
 
     def dyf(v):
-        return turn(v, LANES - 1, 1) - v
+        return next_col(v) - v
 
     def dzf(v):
         return jnp.where(top, 0.0, turn(v, LANES - GROUP, 1)) - v
@@ -531,7 +605,7 @@
         return v - turn(v, 1, 0)
 
     def dyb(v):
-        return v - turn(v, 1, 1)
+        return v - prev_col(v)
 
     def dzb(v):
         return v - jnp.where(bottom, 0.0, turn(v, GROUP, 1))
@@ -543,12 +617,7 @@
         curl = (dyb(h[2]) - dzb(h[1]), dzb(h[0]) - dxb(h[2]), dxb(h[1]) - dyb(h[0]))
         e = [damping * v + coef_e * c for v, c in zip(e, curl)]
         steps.append(e)
-    return steps, h, slope, field(7)
-
-
-def scalar_of(values, sub, lane):
-    here = (iota(values.shape, 0) == sub) & (iota(values.shape, 1) == lane)
-    return jnp.max(jnp.where(here, values, 0.0)).astype(jnp.int32)
+    return steps, h, slope
 
 
 def slot_of(param, rows_mine):
@@ -569,8 +638,23 @@
     sl_ref, xsl_ref, sum_ref, g_ref, buf_ref, ye_ref, yh_ref, ye1, lpad, vpad, gpad,
 ):
     width_x, width_y = sl_ref.shape
-    planes_z = LANES // GROUP
-    steps, h, slope_y, ids_y = strips_y(width_x, width_y, s_ref, t_ref, ya_ref, yb_ref, table)
+    tiles_x, tiles_y = width_x // TILE, width_y // TILE
+
+    def scalar(row, lane):
+        here = iota(row.shape, 1) == lane
+        return jnp.max(jnp.where(here, row, 0.0)).astype(jnp.int32)
+
+    id_x, id_y = {}, {}
+    for k, tile in enumerate(neighbours("gx", xa_ref[TILES - 1], xb_ref[TILES - 1])):
+        for t in range(tiles_y):
+            u = t * TILE // LANES * LANES
+            id_x[k, t] = scalar(tile[1:2, u : u + LANES], t * TILE - u)
+    for row in [tx * TILE for tx in range(tiles_x)] + [width_x, width_x + SUB - 1]:
+        first = row // SUB * SUB
+        here = pl.ds(first, SUB)
+        for k, tile in enumerate(neighbours("gy", ya_ref[here], yb_ref[here])):
+            id_y[k, row] = scalar(tile[row - first : row - first + 1], GROUP - 1 - k)
+    steps, h, slope_y = strips_y(width_x, width_y, s_ref, t_ref, ya_ref, yb_ref, table)
     for c in range(3):
         ye_ref[c] = steps[-1][c]
         yh_ref[c] = h[c]
@@ -607,7 +691,6 @@
 
     half = LANES // 2
     lines = TILE // 2
-    tiles_x, tiles_y = width_x // TILE, width_y // TILE
     devices = lax.axis_size("gx") * lax.axis_size("gy")
     rows_mine = buf_ref.shape[0] // devices
     lane = iota((lines, LANES), 1)
@@ -629,8 +712,6 @@
             odd = gpad[u, pl.ds(pad + tx * TILE + 1, lines, stride=2)]
             add_tile(map_ref[tx, 2 * u], jnp.where(lane < half, even, turn(odd, half, 1)))
             add_tile(map_ref[tx, 2 * u + 1], jnp.where(lane < half, turn(even, half, 1), odd))
-    even_x = lax.axis_index("gx") % 2 == 0
-    below, above = halo_rows(xa_ref, xb_ref, 7 * planes_z, even_x)
     before, after = pl.ds(pad - SUB, SUB), pl.ds(pad + width_x, SUB)
     for t in range(tiles_y):
         u, odd = divmod(t, 2)
@@ -638,47 +719,62 @@
         top = top if odd else turn(top, half, 1)
         low = turn(low, half, 1) if odd else low
         keep = (sub8 == SUB - 1) & (lane8 >= half)
-        add_rows(scalar_of(below, 0, t * TILE), lines - SUB, jnp.where(keep, top, 0.0))
+        add_rows(id_x[0, t], lines - SUB, jnp.where(keep, top, 0.0))
         keep = (sub8 == 0) & (lane8 < half)
-        add_rows(scalar_of(above, 0, t * TILE), 0, jnp.where(keep, low, 0.0))
+        add_rows(id_x[1, t], 0, jnp.where(keep, low, 0.0))
     end = width_y // LANES - 1
     for tx in range(tiles_x):
-        ids = ids_y[tx * TILE : tx * TILE + SUB]
         even, odd = (pl.ds(pad + tx * TILE + k, lines, stride=2) for k in (0, 1))
         left = jnp.where(lane == half - 1, turn(vpad[0, even], half - 1, 1), 0.0)
         left = jnp.where(lane == LANES - 1, turn(vpad[0, odd], LANES - 1, 1), left)
         right = jnp.where(lane == 0, turn(vpad[end, even], 1, 1), 0.0)
         right = jnp.where(lane == half, turn(vpad[end, odd], half + 1, 1), right)
-        for column, values in ((0, left), (GROUP - 1, right)):
-            ident = scalar_of(ids, 0, column)
-            add_tile(jnp.maximum(ident - 1, 0), jnp.where(ident > 0, values, 0.0))
-    tail = ids_y[width_x : width_x + SUB]
+        for ahead, values in ((False, left), (True, right)):
+            owner = id_y[ahead, tx * TILE]
+            add_tile(jnp.maximum(owner - 1, 0), jnp.where(owner > 0, values, 0.0))
+    tail = width_x + SUB - 1
     corners = (
-        (SUB - 1, 0, before, 0, lines - SUB, LANES - 1),
-        (SUB - 1, GROUP - 1, before, end, lines - SUB, half),
-        (0, 0, after, 0, 0, half - 1),
-        (0, GROUP - 1, after, end, 0, 0),
+        (SUB - 1, False, tail, before, lines - SUB, LANES - 1),
+        (SUB - 1, True, tail, before, lines - SUB, half),
+        (0, False, width_x, after, 0, half - 1),
+        (0, True, width_x, after, 0, 0),
     )
-    for sub, column, rows, u, start, target in corners:
-        source = LANES - 1 if u == end and column else 0
+    for sub, ahead, row, rows, start, target in corners:
         keep = (sub8 == sub) & (lane8 == target)
-        values = jnp.where(keep, turn(vpad[u, rows], target - source, 1), 0.0)
-        add_rows(scalar_of(tail, sub, column), start, values)
-
-
-def merge(e_ref, h_ref, em, hm, xe_ref, xh_ref, ye_ref, yh_ref, eo_ref, ho_ref):
+        values = vpad[end, rows] if ahead else vpad[0, rows]
+        values = turn(values, target - (LANES - 1 if ahead else 0), 1)
+        add_rows(id_y[ahead, row], start, jnp.where(keep, values, 0.0))
+
+
+def merge(e_ref, h_ref, em, hm, xe_ref, xh_ref, ye_ref, yh_ref, eo_ref, ho_ref, out, sems):
     _, planes_z, width_x, _ = e_ref.shape
     parts = (
         (e_ref, em, xe_ref, ye_ref, eo_ref, LO + 2, HI - 1),
         (h_ref, hm, xh_ref, yh_ref, ho_ref, LO + 1, HI - 1),
     )
-    for rest, mid, xs, ys, out, low, high in parts:
-        for z in range(planes_z):
-            src = mid.at[0, z - LO] if low <= z < high else rest.at[0, z]
-            for start in range(0, width_x, SUB):
-                here = pl.ds(start, SUB)
-                values = patch_rows(src[here], xs.at[0, z], start, width_x)
-                out[0, z, here] = patch_cols(values, ys[0, here], z)
+    half = planes_z // 2
+
+    def send(n, c, k):
+        rows = pl.ds(k * half, half)
+        return pltpu.make_async_copy(out.at[n, c, rows], parts[n][4].at[c, rows], sems.at[n, c, k])
+
+    def body(c, _):
+        for n, (rest, mid, xs, ys, _, low, high) in enumerate(parts):
+            for z in range(planes_z):
+                src = mid.at[c, z - LO] if low <= z < high else rest.at[c, z]
+                for start in range(0, width_x, SUB):
+                    here = pl.ds(start, SUB)
+                    values = patch_rows(src[here], xs.at[c, z], start, width_x)
+                    out[n, c, z, here] = patch_cols(values, ys[c, here], z)
+                if z % half == half - 1:
+                    send(n, c, z // half).start()
+        return 0
+
+    lax.fori_loop(0, 3, body, 0)
+    for n in range(2):
+        for c in range(3):
+            for k in range(2):
+                send(n, c, k).wait()
 
 
 def first_sum(parts, buf_ref, got_ref, *outs):
@@ -695,41 +791,46 @@
         out[...] = sum(ref[rows] for ref in ins[1:]) + ins[0][rows]
 
 
-def pair(block, partner):
+def pair(block, partner, spare=None):
     count_gx, count_gy = lax.axis_size("gx"), lax.axis_size("gy")
     route = []
     for i in range(count_gx):
         for j in range(count_gy):
             a, b = partner(i, j)
-            if 0 <= a < count_gx and 0 <= b < count_gy:
-                route.append((i * count_gy + j, a * count_gy + b))
+            if not (0 <= a < count_gx and 0 <= b < count_gy):
+                a, b = spare(i, j)
+            route.append((i * count_gy + j, a * count_gy + b))
     return lax.ppermute(block, ("gx", "gy"), route)
+
+
+def after(k):
+    return ((k + 1) ^ 1) - 1
 
 
 def on_device(e_adj, h_adj, density, material, eps_table, dft_adj, dft_fwd, tile_map):
     planes_z, width_x, width_y = material.shape
     count_gx, count_gy = lax.axis_size("gx"), lax.axis_size("gy")
     block = 4 * width_x * width_y
-    groups = -(-n_faces(planes_z) // 4)
-    face = struct(groups, SUB, width_y)
+    assert planes_z == SUB
+    face = struct(TILES, SUB, width_y)
     xa, xb = pl.pallas_call(
         pack_x,
         out_shape=(face, face),
         in_specs=[HBM] * 5,
         out_specs=(VMEM,) * 2,
         scratch_shapes=[
-            pltpu.VMEM((3, planes_z, 2 * SUB, width_y), F32),
-            pltpu.VMEM((3, planes_z, 2 * SUB, width_y), F32),
-            pltpu.VMEM((planes_z, 2 * SUB, width_y), jnp.int32),
+            pltpu.VMEM((width_y // LANES, 3 * planes_z * 2 * SUB, LANES), F32),
+            pltpu.VMEM((width_y // LANES, 3 * planes_z * 2 * SUB, LANES), F32),
+            pltpu.VMEM((width_y // LANES, planes_z * 2 * SUB, LANES), jnp.int32),
             pltpu.VMEM((2 * SUB, width_y), F32),
             pltpu.SMEM(tile_map.shape, jnp.int32),
-            pltpu.SemaphoreType.DMA((9,)),
+            pltpu.SemaphoreType.DMA((6 * width_y // LANES + 3,)),
         ],
-        compiler_params=params(62700000),
+        compiler_params=params(62300000),
         name="pack_x",
     )(e_adj, h_adj, material, density, tile_map)
     xa = pair(xa, lambda i, j: (i ^ 1, j))
-    xb = pair(xb, lambda i, j: (((i + 1) ^ 1) - 1, j))
+    xb = pair(xb, lambda i, j: (after(i), j), lambda i, j: (i, j ^ 1))
     strip = pl.pallas_call(
         build_strips,
         out_shape=struct(8, width_x, LANES),
@@ -789,7 +890,7 @@
         name="pack_y",
     )(strip, xa, xb, slope)
     ya = pair(ya, lambda i, j: (i, j ^ 1))
-    yb = pair(yb, lambda i, j: (i, ((j + 1) ^ 1) - 1))
+    yb = pair(yb, lambda i, j: (i, after(j)), lambda i, j: (i ^ 1, j))
     xe2, xh2, xe1, xslope = pl.pallas_call(
         strips_x,
         out_shape=(
@@ -845,16 +946,15 @@
     parts = [parts[0]] + [
         pair(parts[k], lambda i, j: (i ^ (k & 1), j ^ (k >> 1 << 1))) for k in range(1, count_gy)
     ]
-    core = pl.BlockSpec((1, HI - LO, width_x, width_y), lambda c: (c, 0, 0, 0))
-    whole = pl.BlockSpec((1, planes_z, width_x, width_y), lambda c: (c, 0, 0, 0))
-    edge = pl.BlockSpec((1, planes_z, 2, SUB, width_y), lambda c: (c, 0, 0, 0, 0))
-    side = pl.BlockSpec((1, width_x + SUB, LANES), lambda c: (c, 0, 0))
     e_out, h_out = pl.pallas_call(
         merge,
-        grid=(3,),
-        out_shape=(struct(3, planes_z, width_x, width_y),) * 2,
-        in_specs=[whole, whole, core, core, edge, edge, side, side],
-        out_specs=(whole, whole),
+        out_shape=(full,) * 2,
+        in_specs=[VMEM] * 8,
+        out_specs=(HBM,) * 2,
+        scratch_shapes=[
+            pltpu.VMEM((2, 3, planes_z, width_x, width_y), F32),
+            pltpu.SemaphoreType.DMA((2, 3, 2)),
+        ],
         compiler_params=params(),
         cost_estimate=cost(1, 1),
         name="merge",

time: 39.6 us -> 35.6 us (0.90)
  starting transfers between devices: 17.8 us -> 13.6 us
  waiting for transfers between devices: 5.31 us -> 6.68 us
  Pallas kernels: 14.8 us -> 13.6 us
    ppermute x11, starting transfers between devices: 17.8 us -> 13.6 us  [pair(): return lax.ppermute(block, ('gx', 'gy'), route)]
    ppermute x11, waiting for transfers between devices: 5.31 us -> 6.68 us  [pair(): return lax.ppermute(block, ('gx', 'gy'), route)]
    pallas_call x1, Pallas kernels: 2.44 us -> 1.86 us  [on_device(): pl.pallas_call(merge, out_shape=(full,) * 2, in_specs=[VMEM] * 8, out_spe...]
    pallas_call x1, Pallas kernels: 1.75 us -> 1.29 us  [on_device(): pl.pallas_call(build_strips, out_shape=struct(8, width_x, LANES), in_spec...]
  transfers between devices with their start and end apart: 11 -> 11, of which waited for: 5 -> 6; matrix products, arithmetic and copies ran while one was open for 0% -> 0% of each run, Pallas kernels for 26% -> 26%
where the time goes in v3:
time: 35.6 us; the launch traced here: 35.5 us
  Pallas kernels  13.6 us (38%)
  starting transfers between devices  13.6 us (38%)
  waiting for transfers between devices  6.68 us (19%)
  between operations  0.84 us (2%)
  other arithmetic  0.61 us (2%)
    ppermute x11, starting transfers between devices, pair(): return lax.ppermute(block, ('gx', 'gy'), route)  13.6 us
    ppermute x11, waiting for transfers between devices, pair(): return lax.ppermute(block, ('gx', 'gy'), route)  6.68 us
    pallas_call x1, Pallas kernels, on_device(): pl.pallas_call(pack_x, out_shape=(face, face), in_specs=[HBM] * 5, out_sp...  2.3 us
    pallas_call x1, Pallas kernels, on_device(): pl.pallas_call(interior_rest, out_shape=(full, full, struct(SUB, LANES)),...  1.98 us
    pallas_call x1, Pallas kernels, on_device(): pl.pallas_call(merge, out_shape=(full,) * 2, in_specs=[VMEM] * 8, out_spe...  1.86 us
    pallas_call x1, Pallas kernels, on_device(): pl.pallas_call(gradient, out_shape=(struct(devices * rows_mine, lines, LA...  1.74 us
    pallas_call x1, Pallas kernels, on_device(): pl.pallas_call(interior_first, out_shape=(middle, middle, struct(3, PLANE...  1.71 us
    pallas_call x1, Pallas kernels, on_device(): pl.pallas_call(build_strips, out_shape=struct(8, width_x, LANES), in_spec...  1.29 us
  transfers between devices with their start and end apart: 11, of which 6 were waited for; matrix products, arithmetic and copies ran while one was open for 0% of the time, Pallas kernels for 26%

profile of v3, /device:TPU:0, one launch (start us, length us, event | category | flops | bytes accessed | tf_op | source)
XLA Modules:
  0.0 35.5 jit_solution(6668329366219283442)
XLA Ops:
  0.7 2.3 %pack_x.1 = (f32[10,8,256]{2,1,0:T(8,128)}, f32[10,8,256]{2,1,0:T(8,128)}) custom-call(f32[3,8,64,256]{3,2,1,0:T(8,128)} %e_ref.7, f32[3,8,64,256]{3,2,1,0:T(8,128)} %h_ref.7, s32[8,64,256]{2,1,0:T(8,128)} %m_ref.7, f32[64,256]{1,0:T(8,128)} %d_ref.5, s32[1,4]{1,0:T(1,128)} %map_ref.3), custom_call_target="tpu_custom_call" | custom-call | tf_op jit(solution)/shard_map/pack_x/pallas_call | solution.py:816
  3.0 3.0 %collective-permute-start = (f32[10,8,256]{2,1,0:T(8,128)}, f32[10,8,256]{2,1,0:T(8,128)S(1)}, u32[]{:S(2)}, u32[]{:S(2)}) collective-permute-start(f32[10,8,256]{2,1,0:T(8,128)} %get-tuple-element.44), channel_id=1, source_target_pairs={{0,4},{1,5},{2,6},{3,7},{4,0},{5,1},{6,2},{7,3},{8,12},{9,13},{10,... | collective-permute-start | bytes 245768 | tf_op jit(solution)/shard_map/ppermute | solution.py:803
  6.1 1.3 %build_strips.1.s_ref = f32[8,64,128]{2,1,0:T(8,128)S(1)} custom-call(f32[3,8,64,256]{3,2,1,0:T(8,128)S(1)} %copy-done, f32[3,8,64,256]{3,2,1,0:T(8,128)S(1)} %copy-done.1, s32[8,64,256]{2,1,0:T(8,128)S(1)} %copy-done.2, f32[64,256]{1,0:T(8,128)S(1)} %copy-done.5, s32[1,4]{1,0:T(1,128)S(1)} %copy-done.7), custom_call_target="tpu_custom_call" | custom-call | flops 1 | bytes 1 | tf_op jit(solution)/shard_map/build_strips/pallas_call | solution.py:834
  7.4 1.7 %interior_first.1 = (f32[3,5,64,256]{3,2,1,0:T(8,128)S(1)}, f32[3,5,64,256]{3,2,1,0:T(8,128)S(1)}, f32[3,2,64,256]{3,2,1,0:T(8,128)S(1)}, f32[64,256]{1,0:T(8,12...) custom-call(f32[3,8,64,256]{3,2,1,0:T(8,128)S(1)} %copy-done, ...), custom_call_target="tpu_custom_call" | custom-call | flops 1 | bytes 1 | tf_op jit(solution)/shard_map/interior_first/pallas_call | solution.py:862
  9.1 0.9 %collective-permute-done.xa_ref = f32[10,8,256]{2,1,0:T(8,128)S(1)} collective-permute-done((f32[10,8,256]{2,1,0:T(8,128)}, f32[10,8,256]{2,1,0:T(8,128)S(1)}, u32[]{:S(2)}, u32[]{:S(2)}) %collective-permute-start) | collective-permute-done | bytes 81952 | tf_op jit(solution)/shard_map/ppermute | solution.py:803
  10.0 0.2 pack_y.1
  10.2 0.1 collective-permute-start.2
  10.3 2.4 %collective-permute-start.3 = (f32[72,128]{1,0:T(8,128)S(1)}, f32[72,128]{1,0:T(8,128)S(1)}, u32[]{:S(2)}, u32[]{:S(2)}) collective-permute-start(f32[72,128]{1,0:T(8,128)S(1)} %get-tuple-element.51), channel_id=1, source_target_pairs={{0,4},{1,2},{2,1},{3,7},{4,0},{5,6},{6,5},{7,3},{8,12},{9,10},{10,... | collective-permute-start | bytes 110600 | tf_op jit(solution)/shard_map/ppermute | solution.py:803
  12.7 1.2 %transform.1 = (f32[64,256]{1,0:T(8,128)S(1)}, f32[2,3,2,64,256]{4,3,2,1,0:T(8,128)S(1)}) custom-call(f32[4,2,3,2,64,256]{5,4,3,2,1,0:T(8,128)S(1)} %copy-done.3, bf16[4,2,3,2,64,256]{5,4,3,2,1,0:T(8,128)(2,1)S(1)} %copy-done.4), custom_call_target="tpu_custom_call" | custom-call | flops 1 | bytes 1 | tf_op jit(solution)/shard_map/transform/pallas_call | solution.py:846
  14.0 1.2 %strips_x.1 = (f32[3,8,2,8,256]{4,3,2,1,0:T(8,128)S(1)}, f32[3,8,2,8,256]{4,3,2,1,0:T(8,128)S(1)}, f32[3,2,2,8,256]{4,3,2,1,0:T(8,128)S(1)}, f32[2,8,256]{2,1,0:T(8,128)S(1)}) custom-call(f32[3,8,64,256]{3,2,1,0:T(8,128)S(1)} %copy-done, f32[3,8,64,256]{3,2,1,0:T(8,128)S(1)} %copy-done.1, s32[8,64,256]{2,1,0:T(8,128)S(1)} %copy-done.2, ...), custom_call_target="tpu_custom_call" | custom-call | flops 1 | bytes 1 | tf_op jit(solution)/shard_map/strips_x/pallas_call | solution.py:894
  15.2 1.7 %gradient.1 = (f32[32,32,128]{2,1,0:T(8,128)S(1)}, f32[3,72,128]{2,1,0:T(8,128)S(1)}, f32[3,72,128]{2,1,0:T(8,128)S(1)}) custom-call(f32[8,64,128]{2,1,0:T(8,128)S(1)} %build_strips.1.s_ref, f32[8,8,128]{2,1,0:T(8,128)S(1)} %get-tuple-element.49.t_ref, f32[72,128]{1,0:T(8,128)S(1)} %collective-permute-done.2.ya_ref, ...), custom_call_target="tpu_custom_call" | custom-call | flops 1 | bytes 1 | tf_op jit(solution)/shard_map/gradient/pallas_call | solution.py:918
  17.0 1.5 %collective-permute-done.4.refs_1_ = f32[16,32,128]{2,1,0:T(8,128)S(1)} collective-permute-done((f32[16,32,128]{2,1,0:T(8,128)S(1)}, f32[16,32,128]{2,1,0:T(8,128)S(1)}, u32[]{:S(2)}, u32[]{:S(2)}) %collective-permute-start.4) | collective-permute-done | bytes 262176 | tf_op jit(solution)/shard_map/ppermute | solution.py:803
  18.6 1.5 %collective-permute-start.5 = (f32[4,32,128]{2,1,0:T(8,128)S(1)}, f32[4,32,128]{2,1,0:T(8,128)S(1)}, u32[]{:S(2)}, u32[]{:S(2)}) collective-permute-start(f32[4,32,128]{2,1,0:T(8,128)S(1)} %get-tuple-element.63), channel_id=1, source_target_pairs={{0,4},{1,5},{2,6},{3,7},{4,0},{5,1},{6,2},{7,3},{8,12},{9,13},{10,... | collective-permute-start | bytes 196616 | tf_op jit(solution)/shard_map/ppermute | solution.py:803
  20.1 1.0 %collective-permute-start.6 = (f32[4,32,128]{2,1,0:T(8,128)S(1)}, f32[4,32,128]{2,1,0:T(8,128)S(1)}, u32[]{:S(2)}, u32[]{:S(2)}) collective-permute-start(f32[4,32,128]{2,1,0:T(8,128)S(1)} %get-tuple-element.64), channel_id=1, source_target_pairs={{0,2},{1,3},{2,0},{3,1},{4,6},{5,7},{6,4},{7,5},{8,10},{9,11},{10,... | collective-permute-start | bytes 196616 | tf_op jit(solution)/shard_map/ppermute | solution.py:803
  21.1 1.0 %collective-permute-start.7 = (f32[4,32,128]{2,1,0:T(8,128)S(1)}, f32[4,32,128]{2,1,0:T(8,128)S(1)}, u32[]{:S(2)}, u32[]{:S(2)}) collective-permute-start(f32[4,32,128]{2,1,0:T(8,128)S(1)} %get-tuple-element.65), channel_id=1, source_target_pairs={{0,6},{1,7},{2,4},{3,5},{4,2},{5,3},{6,0},{7,1},{8,14},{9,15},{10,... | collective-permute-start | bytes 196616 | tf_op jit(solution)/shard_map/ppermute | solution.py:803
  22.1 2.0 %interior_rest.1 = (f32[3,8,64,256]{3,2,1,0:T(8,128)S(1)}, f32[3,8,64,256]{3,2,1,0:T(8,128)S(1)}, f32[8,128]{1,0:T(8,128)S(1)}) custom-call(f32[3,8,64,256]{3,2,1,0:T(8,128)S(1)} %copy-done, f32[3,8,64,256]{3,2,1,0:T(8,128)S(1)} %copy-done.1, s32[8,64,256]{2,1,0:T(8,128)S(1)} %copy-done.2, f32[4]{0:T(128)S(1)} %copy-done.6, ...), custom_call_target="tpu_custom_call" | custom-call | flops 1 | bytes 1 | tf_op jit(solution)/shard_map/interior_rest/pallas_call | solution.py:873
  24.1 0.7 %collective-permute-done.6.refs_2_ = f32[4,32,128]{2,1,0:T(8,128)S(1)} collective-permute-done((f32[4,32,128]{2,1,0:T(8,128)S(1)}, f32[4,32,128]{2,1,0:T(8,128)S(1)}, u32[]{:S(2)}, u32[]{:S(2)}) %collective-permute-start.6) | collective-permute-done | bytes 65568 | tf_op jit(solution)/shard_map/ppermute | solution.py:803
  24.9 1.5 %collective-permute-done.7.refs_3_ = f32[4,32,128]{2,1,0:T(8,128)S(1)} collective-permute-done((f32[4,32,128]{2,1,0:T(8,128)S(1)}, f32[4,32,128]{2,1,0:T(8,128)S(1)}, u32[]{:S(2)}, u32[]{:S(2)}) %collective-permute-start.7) | collective-permute-done | bytes 65568 | tf_op jit(solution)/shard_map/ppermute | solution.py:803
  26.3 3.9 %collective-permute-start.10 = (f32[1,32,128]{2,1,0:T(8,128)S(1)}, f32[1,32,128]{2,1,0:T(8,128)S(1)}, u32[]{:S(2)}, u32[]{:S(2)}) collective-permute-start(f32[1,32,128]{2,1,0:T(8,128)S(1)} %get-tuple-element.70), channel_id=1, source_target_pairs={{0,24},{1,25},{2,26},{3,27},{4,28},{5,29},{6,30},{7,31},{8,16},{9,... | collective-permute-start | bytes 49160 | tf_op jit(solution)/shard_map/ppermute | solution.py:803
  30.2 0.6 %collective-permute-start.9 = (f32[1,32,128]{2,1,0:T(8,128)S(1)}, f32[1,32,128]{2,1,0:T(8,128)S(1)}, u32[]{:S(2)}, u32[]{:S(2)}) collective-permute-start(f32[1,32,128]{2,1,0:T(8,128)S(1)} %get-tuple-element.69), channel_id=1, source_target_pairs={{0,16},{1,17},{2,18},{3,19},{4,20},{5,21},{6,22},{7,23},{8,24},{9,... | collective-permute-start | bytes 49160 | tf_op jit(solution)/shard_map/ppermute | solution.py:803
  30.8 1.9 %merge.1 = (f32[3,8,64,256]{3,2,1,0:T(8,128)}, f32[3,8,64,256]{3,2,1,0:T(8,128)}) custom-call(f32[3,8,64,256]{3,2,1,0:T(8,128)S(1)} %get-tuple-element.42.e_ref, f32[3,8,64,256]{3,2,1,0:T(8,128)S(1)} %get-tuple-element.43.h_ref, f32[3,5,64,256]{3,2,1,0:T(8,128)S(1)} %get-tuple-element.37.em.e2_ref, f32[3,5,64,256]{3,2,1,0:T(8,128)S(1)} %get-tuple-element.38.hm, ...), custom_call_target="tpu_custom_call" | custom-call | flops 1 | bytes 1 | tf_op jit(solution)/shard_map/merge/pallas_call | solution.py:949
  32.7 1.2 %collective-permute-done.8 = f32[1,32,128]{2,1,0:T(8,128)S(1)} collective-permute-done((f32[1,32,128]{2,1,0:T(8,128)S(1)}, f32[1,32,128]{2,1,0:T(8,128)S(1)}, u32[]{:S(2)}, u32[]{:S(2)}) %collective-permute-start.8) | collective-permute-done | bytes 16416 | tf_op jit(solution)/shard_map/ppermute | solution.py:803
  33.9 0.9 %collective-permute-done.9 = f32[1,32,128]{2,1,0:T(8,128)S(1)} collective-permute-done((f32[1,32,128]{2,1,0:T(8,128)S(1)}, f32[1,32,128]{2,1,0:T(8,128)S(1)}, u32[]{:S(2)}, u32[]{:S(2)}) %collective-permute-start.9) | collective-permute-done | bytes 16416 | tf_op jit(solution)/shard_map/ppermute | solution.py:803
  34.8 0.6 %add_add_fusion = f32[1,32,128]{2,1,0:T(8,128)} fusion(f32[1,32,128]{2,1,0:T(8,128)S(1)} %collective-permute-done.10, f32[1,32,128]{2,1,0:T(8,128)S(1)} %collective-permute-done.9, f32[1,32,128]{2,1,0:T(8,128)S(1)} %get-tuple-element.67, f32[1,32,128]{2,1,0:T(8,128)S(1)} %collective-permute-done.8), kind=kLoop, calls=%fused_computation | loop fusion | flops 12288 | bytes 81920 | tf_op jit(solution)/shard_map/add | solution.py:971
  (27 shorter events, 0.2 us)
Async XLA Ops:
  0.6 5.4 %copy-start.5 = (f32[64,256]{1,0:T(8,128)S(1)}, f32[64,256]{1,0:T(8,128)}, u32[]{:S(2)}) copy-start(f32[64,256]{1,0:T(8,128)} %d_ref.5) | copy-start | bytes 196612
  0.6 5.4 %copy-start.2 = (s32[8,64,256]{2,1,0:T(8,128)S(1)}, s32[8,64,256]{2,1,0:T(8,128)}, u32[]{:S(2)}) copy-start(s32[8,64,256]{2,1,0:T(8,128)} %m_ref.7) | copy-start | bytes 1572868
  0.7 5.4 %copy-start = (f32[3,8,64,256]{3,2,1,0:T(8,128)S(1)}, f32[3,8,64,256]{3,2,1,0:T(8,128)}, u32[]{:S(2)}) copy-start(f32[3,8,64,256]{3,2,1,0:T(8,128)} %e_ref.7) | copy-start | bytes 4718596
  0.7 5.4 %copy-start.1 = (f32[3,8,64,256]{3,2,1,0:T(8,128)S(1)}, f32[3,8,64,256]{3,2,1,0:T(8,128)}, u32[]{:S(2)}) copy-start(f32[3,8,64,256]{3,2,1,0:T(8,128)} %h_ref.7) | copy-start | bytes 4718596
  0.7 5.4 %copy-start.7 = (s32[1,4]{1,0:T(1,128)S(1)}, s32[1,4]{1,0:T(1,128)}, u32[]{:S(2)}) copy-start(s32[1,4]{1,0:T(1,128)} %map_ref.3) | copy-start | bytes 52
  3.0 7.0 %collective-permute-start = (f32[10,8,256]{2,1,0:T(8,128)}, f32[10,8,256]{2,1,0:T(8,128)S(1)}, u32[]{:S(2)}, u32[]{:S(2)}) collective-permute-start(f32[10,8,256]{2,1,0:T(8,128)} %get-tuple-element.44), channel_id=1, source_target_pairs={{0,4},{1,5},{2,6},{3,7},{4,0},{5,1},{6,2},{7,3},{8,12},{9,13},{10,... | collective-permute-start | bytes 245768 | tf_op jit(solution)/shard_map/ppermute | solution.py:803
  6.0 1.4 %copy-start.6 = (f32[4]{0:T(128)S(1)}, f32[4]{0:T(128)}, u32[]{:S(2)}) copy-start(f32[4]{0:T(128)} %table.7) | copy-start | bytes 52
  6.0 3.9 %collective-permute-start.1 = (f32[10,8,256]{2,1,0:T(8,128)}, f32[10,8,256]{2,1,0:T(8,128)S(1)}, u32[]{:S(2)}, u32[]{:S(2)}) collective-permute-start(f32[10,8,256]{2,1,0:T(8,128)} %get-tuple-element.45), channel_id=1, source_target_pairs={{0,1},{1,0},{2,3},{3,2},{4,8},{5,9},{6,10},{7,11},{8,4},{9,5},{10,... | collective-permute-start | bytes 245768 | tf_op jit(solution)/shard_map/ppermute | solution.py:803
  6.1 6.6 %copy-start.4 = (bf16[4,2,3,2,64,256]{5,4,3,2,1,0:T(8,128)(2,1)S(1)}, bf16[4,2,3,2,64,256]{5,4,3,2,1,0:T(8,128)(2,1)}, u32[]{:S(2)}) copy-start(bf16[4,2,3,2,64,256]{5,4,3,2,1,0:T(8,128)(2,1)} %fwd_ref.1) | copy-start | bytes 4718596
  7.4 5.3 %copy-start.3 = (f32[4,2,3,2,64,256]{5,4,3,2,1,0:T(8,128)S(1)}, f32[4,2,3,2,64,256]{5,4,3,2,1,0:T(8,128)}, u32[]{:S(2)}) copy-start(f32[4,2,3,2,64,256]{5,4,3,2,1,0:T(8,128)} %adj_ref.1) | copy-start | bytes 9437188
  10.2 5.0 %collective-permute-start.2 = (f32[72,128]{1,0:T(8,128)S(1)}, f32[72,128]{1,0:T(8,128)S(1)}, u32[]{:S(2)}, u32[]{:S(2)}) collective-permute-start(f32[72,128]{1,0:T(8,128)S(1)} %get-tuple-element.50), channel_id=1, source_target_pairs={{0,1},{1,0},{2,3},{3,2},{4,5},{5,4},{6,7},{7,6},{8,9},{9,8},{10,11... | collective-permute-start | bytes 110600 | tf_op jit(solution)/shard_map/ppermute | solution.py:803
  10.3 4.9 %collective-permute-start.3 = (f32[72,128]{1,0:T(8,128)S(1)}, f32[72,128]{1,0:T(8,128)S(1)}, u32[]{:S(2)}, u32[]{:S(2)}) collective-permute-start(f32[72,128]{1,0:T(8,128)S(1)} %get-tuple-element.51), channel_id=1, source_target_pairs={{0,4},{1,2},{2,1},{3,7},{4,0},{5,6},{6,5},{7,3},{8,12},{9,10},{10,... | collective-permute-start | bytes 110600 | tf_op jit(solution)/shard_map/ppermute | solution.py:803
  17.0 1.6 %collective-permute-start.4 = (f32[16,32,128]{2,1,0:T(8,128)S(1)}, f32[16,32,128]{2,1,0:T(8,128)S(1)}, u32[]{:S(2)}, u32[]{:S(2)}) collective-permute-start(f32[16,32,128]{2,1,0:T(8,128)S(1)} %slice.3), channel_id=1, source_target_pairs={{0,1},{1,0},{2,3},{3,2},{4,5},{5,4},{6,7},{7,6},{8,9},{9,8},{10,11... | collective-permute-start | bytes 786440 | tf_op jit(solution)/shard_map/ppermute | solution.py:803
  18.6 5.5 %collective-permute-start.5 = (f32[4,32,128]{2,1,0:T(8,128)S(1)}, f32[4,32,128]{2,1,0:T(8,128)S(1)}, u32[]{:S(2)}, u32[]{:S(2)}) collective-permute-start(f32[4,32,128]{2,1,0:T(8,128)S(1)} %get-tuple-element.63), channel_id=1, source_target_pairs={{0,4},{1,5},{2,6},{3,7},{4,0},{5,1},{6,2},{7,3},{8,12},{9,13},{10,... | collective-permute-start | bytes 196616 | tf_op jit(solution)/shard_map/ppermute | solution.py:803
  20.1 4.7 %collective-permute-start.6 = (f32[4,32,128]{2,1,0:T(8,128)S(1)}, f32[4,32,128]{2,1,0:T(8,128)S(1)}, u32[]{:S(2)}, u32[]{:S(2)}) collective-permute-start(f32[4,32,128]{2,1,0:T(8,128)S(1)} %get-tuple-element.64), channel_id=1, source_target_pairs={{0,2},{1,3},{2,0},{3,1},{4,6},{5,7},{6,4},{7,5},{8,10},{9,11},{10,... | collective-permute-start | bytes 196616 | tf_op jit(solution)/shard_map/ppermute | solution.py:803
  21.1 5.2 %collective-permute-start.7 = (f32[4,32,128]{2,1,0:T(8,128)S(1)}, f32[4,32,128]{2,1,0:T(8,128)S(1)}, u32[]{:S(2)}, u32[]{:S(2)}) collective-permute-start(f32[4,32,128]{2,1,0:T(8,128)S(1)} %get-tuple-element.65), channel_id=1, source_target_pairs={{0,6},{1,7},{2,4},{3,5},{4,2},{5,3},{6,0},{7,1},{8,14},{9,15},{10,... | collective-permute-start | bytes 196616 | tf_op jit(solution)/shard_map/ppermute | solution.py:803
  26.3 6.4 %collective-permute-start.10 = (f32[1,32,128]{2,1,0:T(8,128)S(1)}, f32[1,32,128]{2,1,0:T(8,128)S(1)}, u32[]{:S(2)}, u32[]{:S(2)}) collective-permute-start(f32[1,32,128]{2,1,0:T(8,128)S(1)} %get-tuple-element.70), channel_id=1, source_target_pairs={{0,24},{1,25},{2,26},{3,27},{4,28},{5,29},{6,30},{7,31},{8,16},{9,... | collective-permute-start | bytes 49160 | tf_op jit(solution)/shard_map/ppermute | solution.py:803
  30.2 3.7 %collective-permute-start.8 = (f32[1,32,128]{2,1,0:T(8,128)S(1)}, f32[1,32,128]{2,1,0:T(8,128)S(1)}, u32[]{:S(2)}, u32[]{:S(2)}) collective-permute-start(f32[1,32,128]{2,1,0:T(8,128)S(1)} %get-tuple-element.68), channel_id=1, source_target_pairs={{0,8},{1,9},{2,10},{3,11},{4,12},{5,13},{6,14},{7,15},{8,0},{9,1},... | collective-permute-start | bytes 49160 | tf_op jit(solution)/shard_map/ppermute | solution.py:803
  30.2 4.6 %collective-permute-start.9 = (f32[1,32,128]{2,1,0:T(8,128)S(1)}, f32[1,32,128]{2,1,0:T(8,128)S(1)}, u32[]{:S(2)}, u32[]{:S(2)}) collective-permute-start(f32[1,32,128]{2,1,0:T(8,128)S(1)} %get-tuple-element.69), channel_id=1, source_target_pairs={{0,16},{1,17},{2,18},{3,19},{4,20},{5,21},{6,22},{7,23},{8,24},{9,... | collective-permute-start | bytes 49160 | tf_op jit(solution)/shard_map/ppermute | solution.py:803

commit v4 on v3

--- a/solution.py
+++ b/solution.py
@@ -77,8 +77,9 @@
     return (rows >= 0) & (rows < total_x) & (cols >= 0) & (cols < total_y)
 
 
-def table_inverse(table, shape):
-    return [courant / jnp.full(shape, table[k], F32) for k in range(table.shape[0])]
+def table_inverse(table, rows, cols):
+    tiles = [table[k * SUB : (k + 1) * SUB] for k in range(table.shape[0] // SUB)]
+    return [jnp.tile(tile, (rows // SUB, cols // LANES)) for tile in tiles]
 
 
 def pick(index, choices):
@@ -114,7 +115,10 @@
 BEHIND = (0, 1, 2, 4, 5)
 
 
-def pack_x(e_in, h_in, m_in, d_in, map_in, a_ref, b_ref, eb, hb, mb, db, map_ref, sems):
+def pack_x(
+    e_in, h_in, m_in, d_in, map_in, table_in,
+    a_ref, b_ref, id_ref, inverse_ref, eb, hb, mb, db, map_ref, table_ref, sems,
+):
     planes_z, size, width_y = m_in.shape
     span = 2 * SUB
     tiles = width_y // LANES
@@ -134,6 +138,7 @@
                 copies.append(pltpu.make_async_copy(source, target, sems.at[len(copies)]))
         copies.append(pltpu.make_async_copy(d_in.at[here], db.at[there], sems.at[len(copies)]))
     copies.append(pltpu.make_async_copy(map_in, map_ref, sems.at[len(copies)]))
+    copies.append(pltpu.make_async_copy(table_in, table_ref, sems.at[len(copies)]))
     for copy in copies:
         copy.start()
     gx, gy = lax.axis_index("gx"), lax.axis_index("gy")
@@ -175,6 +180,10 @@
     for k in range(TILES):
         a_ref[k] = jnp.where(even, high[k], low[k])
         b_ref[k] = jnp.where(even, low[k], high[k])
+    for tx in range(map_ref.shape[0]):
+        id_ref[pl.ds(tx * SUB, SUB)] = id_row(map_ref, tx, shape)
+    for k in range(table_ref.shape[0]):
+        inverse_ref[pl.ds(k * SUB, SUB)] = courant / jnp.full((SUB, LANES), table_ref[k], F32)
 
 
 def neighbours(axis, from_a, from_b):
@@ -202,7 +211,7 @@
     return jnp.sum(rolled, axis=0, keepdims=True)
 
 
-def build_strips(e_ref, h_ref, m_ref, d_ref, map_ref, s_ref):
+def build_strips(e_ref, h_ref, m_ref, d_ref, id_ref, s_ref):
     planes_z, width_x, width_y = m_ref.shape
     group = iota((SUB, LANES), 1) // GROUP
 
@@ -227,7 +236,7 @@
     for start in range(0, width_x, SUB):
         here = pl.ds(start, SUB)
         s_ref[6, here] = gather(source, here)
-        row = id_row(map_ref, start // TILE, (SUB, width_y))
+        row = id_ref[pl.ds(start // TILE * SUB, SUB)]
         s_ref[7, here] = turn(ends(row), GROUP // 2, 1)
 
 
@@ -279,24 +288,31 @@
 
 
 def transform(adj_ref, fwd_ref, s_ref, g_ref):
-    rows, cols = s_ref.shape
-    total = jnp.zeros((rows, cols), F32)
-    for c in range(3):
-        for p in range(PLANES):
-            parts = [None] * STEPS
-            for f in range(FREQ):
-                real = fwd_ref[f, 0, c, p].astype(F32)
-                imag = fwd_ref[f, 1, c, p].astype(F32)
-                total = total + (real * adj_ref[f, 0, c, p] - imag * adj_ref[f, 1, c, p])
+    rows = 2 * SUB
+
+    def body(k, _):
+        here = pl.ds(pl.multiple_of(k * rows, rows), rows)
+        total = None
+        for c in range(3):
+            for p in range(PLANES):
+                parts = [None] * STEPS
+                for f in range(FREQ):
+                    real = fwd_ref[f, 0, c, p, here].astype(F32)
+                    imag = fwd_ref[f, 1, c, p, here].astype(F32)
+                    term = real * adj_ref[f, 0, c, p, here] - imag * adj_ref[f, 1, c, p, here]
+                    total = term if total is None else total + term
+                    for n in range(STEPS):
+                        angle = (0.21 + 0.06 * f) * (n + 1)
+                        term = (dft_weight * math.cos(angle)) * real + (
+                            dft_weight * math.sin(angle)
+                        ) * imag
+                        parts[n] = term if parts[n] is None else parts[n] + term
                 for n in range(STEPS):
-                    angle = (0.21 + 0.06 * f) * (n + 1)
-                    term = (dft_weight * math.cos(angle)) * real + (
-                        dft_weight * math.sin(angle)
-                    ) * imag
-                    parts[n] = term if parts[n] is None else parts[n] + term
-            for n in range(STEPS):
-                g_ref[n, c, p] = parts[n]
-    s_ref[...] = total
+                    g_ref[n, c, p, here] = parts[n]
+        s_ref[here] = total
+        return 0
+
+    lax.fori_loop(0, s_ref.shape[0] // rows, body, 0)
 
 
 LO = ZLO - STEPS
@@ -365,7 +381,7 @@
     ch[...] = coef_h
     design, slope = design_terms(blur(d_ref[...]))
     sl_ref[...] = slope
-    choices = [jnp.tile(c, (1, width_y // LANES)) for c in table_inverse(table, (SUB, LANES))]
+    choices = table_inverse(table, SUB, width_y)
     for z in range(LO, HI):
         if in_design(z):
             ce[z - LO] = design * inverse
@@ -393,7 +409,7 @@
 
 def interior_rest(e_ref, h_ref, m_ref, table, em, hm, damp, ch, ce, e2, h2, done, ce2):
     planes_z, width_x, width_y = m_ref.shape
-    choices = [jnp.tile(c, (1, width_y // LANES)) for c in table_inverse(table, (SUB, LANES))]
+    choices = table_inverse(table, SUB, width_y)
     done[...] = jnp.zeros(done.shape, F32)
     rest = [z for z in range(planes_z) if not LO < z < HI]
     for z in rest:
@@ -437,7 +453,7 @@
     shape = (SUB, width_y)
     sub = iota(shape, 0)
     cols = (iota(shape, 1) + gy * width_y).astype(F32)
-    choices = [jnp.tile(c, (1, width_y // LANES)) for c in table_inverse(table, (SUB, LANES))]
+    choices = table_inverse(table, SUB, width_y)
     zero = jnp.zeros(shape, F32)
     damps, chs = [], []
 
@@ -545,31 +561,67 @@
     return jnp.concatenate(tiles, axis=1)
 
 
-def strips_y(width_x, width_y, s_ref, t_ref, ya_ref, yb_ref, table):
+def strip_columns(shape):
+    lane = iota(shape, 1)
+    return lane % GROUP, lane // GROUP
+
+
+def strip_coefs(width_x, width_y):
     gx, gy = lax.axis_index("gx"), lax.axis_index("gy")
     total_x, total_y = width_x * lax.axis_size("gx"), width_y * lax.axis_size("gy")
-    planes_z = LANES // GROUP
-    size = width_x + SUB
-    shape = (size, LANES)
-    lane = iota(shape, 1)
-    col = lane % GROUP
-    plane = lane // GROUP
-    from_low, from_high = neighbours("gy", ya_ref[...], yb_ref[...])
-
-    def field(f):
-        own = jnp.concatenate([s_ref[f], t_ref[f]], axis=0)
-        own = jnp.where(col < 2, turn(from_low, -2 * f, 1), own)
-        return jnp.where(col >= GROUP - 2, turn(from_high, GROUP - 2 - 2 * f, 1), own)
-
+    shape = (width_x + SUB, LANES)
+    col, _ = strip_columns(shape)
     row = iota(shape, 0)
-    row = jnp.where(row >= width_x + 4, row - size, row)
+    row = jnp.where(row >= width_x + 4, row - shape[0], row)
     place = jnp.where(col < GROUP // 2, col + (width_y - GROUP // 2), col - GROUP // 2)
     place = jnp.where(col < 2, col - 2, place)
     place = jnp.where(col >= GROUP - 2, col + (width_y - GROUP + 2), place)
     rows = (row + gx * width_x).astype(F32)
     cols = (place + gy * width_y).astype(F32)
-    inside = within(rows, cols, total_x, total_y)
-    damping, coef_h, inverse = edge_coefs(rows, cols, total_x, total_y, inside)
+    return edge_coefs(rows, cols, total_x, total_y, within(rows, cols, total_x, total_y))
+
+
+def design(
+    e1_ref, e2_ref, xe1_ref, xe2_ref, sl_ref, xsl_ref, sum_ref, g_ref,
+    l_ref, gs_ref, ss_ref, coef_ref,
+):
+    width_x, width_y = sl_ref.shape
+    for k, values in enumerate(strip_coefs(width_x, width_y)):
+        coef_ref[k] = values
+    group = iota((SUB, LANES), 1) // GROUP
+    for start in range(0, width_x, SUB):
+        here = pl.ds(start, SUB)
+        total = sum_ref[here]
+        ss_ref[here] = jnp.where(group == ZLO, turn(ends(total), ZLO * GROUP + GROUP // 2, 1), 0.0)
+        for c in range(3):
+            strips = [jnp.zeros((SUB, LANES), F32) for _ in range(STEPS)]
+            for p in range(PLANES):
+                z = ZLO + p
+                first = patch_rows(e1_ref[c, p, here], xe1_ref.at[c, p], start, width_x)
+                second = patch_rows(e2_ref[c, z - LO, here], xe2_ref.at[c, z], start, width_x)
+                weights = [g_ref[n, c, p, here] for n in range(STEPS)]
+                total = total + weights[0] * first + weights[1] * second
+                for n in range(STEPS):
+                    rolled = turn(ends(weights[n]), z * GROUP + GROUP // 2, 1)
+                    strips[n] = jnp.where(group == z, rolled, strips[n])
+            for n in range(STEPS):
+                gs_ref[n, c, here] = strips[n]
+        slope = patch_rows(sl_ref[here], xsl_ref, start, width_x)
+        l_ref[here] = (grad_scale * (eps_high - eps_low)) * slope * total
+
+
+def strips_y(s_ref, t_ref, ya_ref, yb_ref, table, coef_ref):
+    planes_z = LANES // GROUP
+    size = coef_ref.shape[1]
+    col, plane = strip_columns((size, LANES))
+    from_low, from_high = neighbours("gy", ya_ref[...], yb_ref[...])
+
+    def field(f):
+        own = jnp.concatenate([s_ref[f], t_ref[f]], axis=0)
+        own = jnp.where(col < 2, turn(from_low, -2 * f, 1), own)
+        return jnp.where(col >= GROUP - 2, turn(from_high, GROUP - 2 - 2 * f, 1), own)
+
+    damping, coef_h, inverse = coef_ref[0], coef_ref[1], coef_ref[2]
     source = field(6)
     half = GROUP // 2
 
@@ -584,7 +636,7 @@
     filtered = turn(source, 1, 0) + 2.0 * source + turn(source, size - 1, 0)
     filtered = (prev_col(filtered) + 2.0 * filtered + next_col(filtered)) / 16.0
     design, slope = design_terms(filtered)
-    choices = [jnp.tile(c, (size // SUB, 1)) for c in table_inverse(table, (SUB, LANES))]
+    choices = table_inverse(table, size, LANES)
     layer = (plane >= ZLO) & (plane < ZLO + PLANES)
     coef_e = jnp.where(layer, design, pick(source, choices)) * inverse
     e = [field(c) for c in range(3)]
@@ -634,17 +686,22 @@
 
 
 def gradient(
-    s_ref, t_ref, ya_ref, yb_ref, xa_ref, xb_ref, table, map_ref, e1_ref, e2_ref, xe1_ref, xe2_ref,
-    sl_ref, xsl_ref, sum_ref, g_ref, buf_ref, ye_ref, yh_ref, ye1, lpad, vpad, gpad,
+    s_ref, t_ref, ya_ref, yb_ref, xa_ref, xb_ref, table, own_ref, l_ref, gs_ref, ss_ref, coef_ref,
+    buf_ref, ye_ref, yh_ref, lpad, vpad, gpad,
 ):
-    width_x, width_y = sl_ref.shape
+    width_x, width_y = l_ref.shape
     tiles_x, tiles_y = width_x // TILE, width_y // TILE
 
     def scalar(row, lane):
         here = iota(row.shape, 1) == lane
         return jnp.max(jnp.where(here, row, 0.0)).astype(jnp.int32)
 
-    id_x, id_y = {}, {}
+    id_x, id_y, own = {}, {}, {}
+    for tx in range(tiles_x):
+        for t in range(tiles_y):
+            u = t * TILE // LANES * LANES
+            row = own_ref[pl.ds(tx * SUB, 1), pl.ds(u, LANES)]
+            own[tx, t] = scalar(row, t * TILE - u) - 1
     for k, tile in enumerate(neighbours("gx", xa_ref[TILES - 1], xb_ref[TILES - 1])):
         for t in range(tiles_y):
             u = t * TILE // LANES * LANES
@@ -654,30 +711,23 @@
         here = pl.ds(first, SUB)
         for k, tile in enumerate(neighbours("gy", ya_ref[here], yb_ref[here])):
             id_y[k, row] = scalar(tile[row - first : row - first + 1], GROUP - 1 - k)
-    steps, h, slope_y = strips_y(width_x, width_y, s_ref, t_ref, ya_ref, yb_ref, table)
+    steps, h, slope_y = strips_y(s_ref, t_ref, ya_ref, yb_ref, table, coef_ref)
     for c in range(3):
         ye_ref[c] = steps[-1][c]
         yh_ref[c] = h[c]
-        ye1[c] = steps[0][c]
-    ye1[3] = slope_y
     pad = 2 * SUB
     lpad[pl.ds(0, pad)] = jnp.zeros((pad, width_y), F32)
     lpad[pl.ds(pad + width_x, pad)] = jnp.zeros((pad, width_y), F32)
     buf_ref[...] = jnp.zeros(buf_ref.shape, F32)
     for start in range(0, width_x, SUB):
-        here = pl.ds(start, SUB)
-        total = sum_ref[here]
+        here, rows = pl.ds(start, SUB), slice(start, start + SUB)
+        total = ss_ref[here]
         for c in range(3):
-            for p in range(PLANES):
-                first = patch_rows(e1_ref[c, p, here], xe1_ref.at[c, p], start, width_x)
-                first = patch_cols(first, ye1[c, here], ZLO + p)
-                second = e2_ref[c, ZLO + p - LO, here]
-                second = patch_rows(second, xe2_ref.at[c, ZLO + p], start, width_x)
-                second = patch_cols(second, ye_ref[c, here], ZLO + p)
-                total = total + g_ref[0, c, p, here] * first + g_ref[1, c, p, here] * second
-        slope = patch_rows(sl_ref[here], xsl_ref, start, width_x)
-        slope = patch_cols(slope, ye1[3, here], ZLO)
-        lpad[pl.ds(pad + start, SUB)] = (grad_scale * (eps_high - eps_low)) * slope * total
+            for n in range(STEPS):
+                total = total + gs_ref[n, c, here] * steps[n][c][rows]
+        total = sum((turn(total, -p * GROUP, 1) for p in range(1, PLANES)), total)
+        total = (grad_scale * (eps_high - eps_low)) * slope_y[rows] * total
+        lpad[pl.ds(pad + start, SUB)] = patch_cols(l_ref[here], total, ZLO)
     lane = iota((SUB, width_y), 1)
     for start in range(SUB, pad + width_x + SUB, SUB):
         v = lpad[pl.ds(start - 1, SUB)] + 2.0 * lpad[pl.ds(start, SUB)] + lpad[pl.ds(start + 1, SUB)]
@@ -710,8 +760,8 @@
         for u in range(width_y // LANES):
             even = gpad[u, pl.ds(pad + tx * TILE, lines, stride=2)]
             odd = gpad[u, pl.ds(pad + tx * TILE + 1, lines, stride=2)]
-            add_tile(map_ref[tx, 2 * u], jnp.where(lane < half, even, turn(odd, half, 1)))
-            add_tile(map_ref[tx, 2 * u + 1], jnp.where(lane < half, turn(even, half, 1), odd))
+            add_tile(own[tx, 2 * u], jnp.where(lane < half, even, turn(odd, half, 1)))
+            add_tile(own[tx, 2 * u + 1], jnp.where(lane < half, turn(even, half, 1), odd))
     before, after = pl.ds(pad - SUB, SUB), pl.ds(pad + width_x, SUB)
     for t in range(tiles_y):
         u, odd = divmod(t, 2)
@@ -810,48 +860,55 @@
 def on_device(e_adj, h_adj, density, material, eps_table, dft_adj, dft_fwd, tile_map):
     planes_z, width_x, width_y = material.shape
     count_gx, count_gy = lax.axis_size("gx"), lax.axis_size("gy")
-    block = 4 * width_x * width_y
     assert planes_z == SUB
     face = struct(TILES, SUB, width_y)
-    xa, xb = pl.pallas_call(
+    xa, xb, own_ids, table = pl.pallas_call(
         pack_x,
-        out_shape=(face, face),
-        in_specs=[HBM] * 5,
-        out_specs=(VMEM,) * 2,
+        out_shape=(
+            pltpu.VMEM(face.shape, F32),
+            pltpu.VMEM(face.shape, F32),
+            pltpu.VMEM((width_x // TILE * SUB, width_y), F32),
+            pltpu.VMEM((eps_table.shape[0] * SUB, LANES), F32),
+        ),
+        in_specs=[HBM] * 6,
+        out_specs=(VMEM,) * 4,
         scratch_shapes=[
             pltpu.VMEM((width_y // LANES, 3 * planes_z * 2 * SUB, LANES), F32),
             pltpu.VMEM((width_y // LANES, 3 * planes_z * 2 * SUB, LANES), F32),
             pltpu.VMEM((width_y // LANES, planes_z * 2 * SUB, LANES), jnp.int32),
             pltpu.VMEM((2 * SUB, width_y), F32),
             pltpu.SMEM(tile_map.shape, jnp.int32),
-            pltpu.SemaphoreType.DMA((6 * width_y // LANES + 3,)),
+            pltpu.SMEM(eps_table.shape, F32),
+            pltpu.SemaphoreType.DMA((6 * width_y // LANES + 4,)),
         ],
-        compiler_params=params(62300000),
+        compiler_params=params(),
         name="pack_x",
-    )(e_adj, h_adj, material, density, tile_map)
+    )(
+        *(
+            pltpu.with_memory_space_constraint(x, pltpu.HBM)
+            for x in (e_adj, h_adj, material, density, tile_map, eps_table)
+        )
+    )
     xa = pair(xa, lambda i, j: (i ^ 1, j))
     xb = pair(xb, lambda i, j: (after(i), j), lambda i, j: (i, j ^ 1))
     strip = pl.pallas_call(
         build_strips,
         out_shape=struct(8, width_x, LANES),
-        in_specs=[VMEM] * 4 + [SMEM],
+        in_specs=[VMEM] * 5,
         out_specs=VMEM,
         compiler_params=params(),
         cost_estimate=cost(1, 1),
         name="build_strips",
-    )(e_adj, h_adj, material, density, tile_map)
-
-    rows = 2 * SUB
-    moved = struct(width_x, width_y), struct(STEPS, 3, PLANES, width_x, width_y)
+    )(e_adj, h_adj, material, density, own_ids)
+
     base, weight = pl.pallas_call(
         transform,
-        grid=(width_x // rows,),
-        out_shape=moved,
-        in_specs=[pl.BlockSpec((FREQ, 2, 3, PLANES, rows, width_y), lambda i: (0, 0, 0, 0, i, 0))] * 2,
-        out_specs=(
-            pl.BlockSpec((rows, width_y), lambda i: (i, 0)),
-            pl.BlockSpec((STEPS, 3, PLANES, rows, width_y), lambda i: (0, 0, 0, i, 0)),
+        out_shape=(
+            struct(width_x, width_y),
+            struct(STEPS, 3, PLANES, width_x, width_y),
         ),
+        in_specs=[VMEM] * 2,
+        out_specs=(VMEM,) * 2,
         compiler_params=params(),
         cost_estimate=cost(1, 1),
         name="transform",
@@ -864,22 +921,22 @@
         out_shape=(middle, middle, struct(3, PLANES, width_x, width_y))
         + (plane,) * 3
         + (struct(HI - LO, width_x, width_y),),
-        in_specs=[VMEM] * 4 + [SMEM],
+        in_specs=[VMEM] * 5,
         out_specs=(VMEM,) * 7,
         compiler_params=params(),
         cost_estimate=cost(1, 1),
         name="interior_first",
-    )(e_adj, h_adj, material, density, eps_table)
+    )(e_adj, h_adj, material, density, table)
     e2, h2, done = pl.pallas_call(
         interior_rest,
         out_shape=(full, full, struct(SUB, LANES)),
-        in_specs=[VMEM] * 3 + [SMEM] + [VMEM] * 5,
+        in_specs=[VMEM] * 9,
         out_specs=(VMEM,) * 3,
         scratch_shapes=[pltpu.VMEM((planes_z, width_x, width_y), F32)],
         compiler_params=params(),
         cost_estimate=cost(1, 1),
         name="interior_rest",
-    )(e_adj, h_adj, material, eps_table, em, hm, damp, ch, ce)
+    )(e_adj, h_adj, material, table, em, hm, damp, ch, ce)
 
     tails, ya, yb = pl.pallas_call(
         pack_y,
@@ -889,8 +946,8 @@
         compiler_params=params(),
         name="pack_y",
     )(strip, xa, xb, slope)
+    yb = pair(yb, lambda i, j: (i, after(j)), lambda i, j: (i ^ 1, j))
     ya = pair(ya, lambda i, j: (i, j ^ 1))
-    yb = pair(yb, lambda i, j: (i, after(j)), lambda i, j: (i ^ 1, j))
     xe2, xh2, xe1, xslope = pl.pallas_call(
         strips_x,
         out_shape=(
@@ -899,7 +956,7 @@
             struct(3, PLANES, 2, SUB, width_y),
             struct(2, SUB, width_y),
         ),
-        in_specs=[VMEM] * 4 + [SMEM] + [VMEM] * 2,
+        in_specs=[VMEM] * 7,
         out_specs=(VMEM,) * 4,
         scratch_shapes=[
             pltpu.VMEM((2, 3, planes_z + 1, SUB, width_y), F32),
@@ -909,20 +966,33 @@
         compiler_params=params(),
         cost_estimate=cost(1, 1),
         name="strips_x",
-    )(e_adj, h_adj, material, density, eps_table, xa, xb)
+    )(e_adj, h_adj, material, density, table, xa, xb)
 
     devices = count_gx * count_gy
     rows_mine = (width_x // TILE) * (width_y // TILE) // REPEAT
     lines = TILE // 2
     padded = width_x + 4 * SUB
+    local, weight_y, base_y, coef_y = pl.pallas_call(
+        design,
+        out_shape=(
+            plane,
+            struct(STEPS, 3, width_x, LANES),
+            struct(width_x, LANES),
+            struct(3, width_x + SUB, LANES),
+        ),
+        in_specs=[VMEM] * 8,
+        out_specs=(VMEM,) * 4,
+        compiler_params=params(),
+        cost_estimate=cost(1, 1),
+        name="design",
+    )(e1, em, xe1, xe2, slope, xslope, base, weight)
     buf, ye2, yh2 = pl.pallas_call(
         gradient,
         out_shape=(struct(devices * rows_mine, lines, LANES),)
         + (struct(3, width_x + SUB, LANES),) * 2,
-        in_specs=[VMEM] * 6 + [SMEM] * 2 + [VMEM] * 8,
+        in_specs=[VMEM] * 12,
         out_specs=(VMEM,) * 3,
         scratch_shapes=[
-            pltpu.VMEM((4, width_x + SUB, LANES), F32),
             pltpu.VMEM((padded, width_y), F32),
             pltpu.VMEM((width_y // LANES, padded, LANES), F32),
             pltpu.VMEM((width_y // LANES, padded, LANES), F32),
@@ -930,7 +1000,7 @@
         compiler_params=params(),
         cost_estimate=cost(1, 1),
         name="gradient",
-    )(strip, tails, ya, yb, xa, xb, eps_table, tile_map, e1, em, xe1, xe2, slope, xslope, base, weight)
+    )(strip, tails, ya, yb, xa, xb, table, own_ids, local, weight_y, base_y, coef_y)
 
     half = devices * rows_mine // 2
     far = count_gx // 2

time: 35.6 us -> 33.7 us (0.947)
  Pallas kernels: 13.6 us -> 9.79 us
  waiting for transfers between devices: 6.68 us -> 8.52 us
    ppermute x11, waiting for transfers between devices: 6.68 us -> 8.52 us  [pair(): return lax.ppermute(block, ('gx', 'gy'), route)]
    pallas_call x2 -> x3, Pallas kernels: 3.55 us -> 2.66 us  [the longest x1 1.68 us: on_device(): pl.pallas_call(pack_x, out_shape=(pltpu.VMEM(face.shape, F32), pltpu.VMEM...]
    pallas_call x1, Pallas kernels: 1.74 us -> 1.08 us  [on_device(): pl.pallas_call(gradient, out_shape=(struct(devices * rows_mine, lines, LA...]
    pallas_call x1, Pallas kernels: 1.98 us -> 1.36 us  [on_device(): pl.pallas_call(interior_rest, out_shape=(full, full, struct(SUB, LANES)),...]
    pallas_call x1, Pallas kernels: 1.21 us -> 0.65 us  [on_device(): pl.pallas_call(strips_x, out_shape=(struct(3, planes_z, 2, SUB, width_y),...]
    pallas_call x1, Pallas kernels: 1.71 us -> 1.15 us  [on_device(): pl.pallas_call(interior_first, out_shape=(middle, middle, struct(3, PLANE...]
    pallas_call x1, Pallas kernels: 1.29 us -> 0.75 us  [on_device(): pl.pallas_call(build_strips, out_shape=struct(8, width_x, LANES), in_spec...]
  transfers between devices with their start and end apart: 11 -> 11, of which waited for: 6 -> 7; matrix products, arithmetic and copies ran while one was open for 0% -> 0% of each run, Pallas kernels for 26% -> 20%
where the time goes in v4:
time: 33.7 us; the launch traced here: 33.5 us
  starting transfers between devices  13.8 us (41%)
  Pallas kernels  9.79 us (29%)
  waiting for transfers between devices  8.52 us (25%)
  between operations  0.81 us (2%)
  other arithmetic  0.61 us (2%)
    ppermute x11, starting transfers between devices, pair(): return lax.ppermute(block, ('gx', 'gy'), route)  13.8 us
    ppermute x11, waiting for transfers between devices, pair(): return lax.ppermute(block, ('gx', 'gy'), route)  8.52 us
    pallas_call x1, Pallas kernels, on_device(): pl.pallas_call(merge, out_shape=(full,) * 2, in_specs=[VMEM] * 8, out_spe...  1.85 us
    pallas_call x1, Pallas kernels, on_device(): pl.pallas_call(pack_x, out_shape=(pltpu.VMEM(face.shape, F32), pltpu.VMEM...  1.68 us
    pallas_call x1, Pallas kernels, on_device(): pl.pallas_call(interior_rest, out_shape=(full, full, struct(SUB, LANES)),...  1.36 us
    pallas_call x1, Pallas kernels, on_device(): pl.pallas_call(interior_first, out_shape=(middle, middle, struct(3, PLANE...  1.15 us
    pallas_call x1, Pallas kernels, on_device(): pl.pallas_call(gradient, out_shape=(struct(devices * rows_mine, lines, LA...  1.08 us
    pallas_call x1, Pallas kernels, on_device(): pl.pallas_call(build_strips, out_shape=struct(8, width_x, LANES), in_spec...  0.75 us
  transfers between devices with their start and end apart: 11, of which 7 were waited for; matrix products, arithmetic and copies ran while one was open for 0% of the time, Pallas kernels for 20%

profile of v4, /device:TPU:0, one launch (start us, length us, event | category | flops | bytes accessed | tf_op | source)
XLA Modules:
  0.0 33.5 jit_solution(9075334781314112753)
XLA Ops:
  0.7 1.7 %pack_x.1 = (f32[10,8,256]{2,1,0:T(8,128)S(1)}, f32[10,8,256]{2,1,0:T(8,128)S(1)}, f32[8,256]{1,0:T(8,128)S(1)}, f32[32,128]{1,0:T(8,128)S(1)}) custom-call(f32[3,8,64,256]{3,2,1,0:T(8,128)} %e_ref.7, f32[3,8,64,256]{3,2,1,0:T(8,128)} %h_ref.7, s32[8,64,256]{2,1,0:T(8,128)} %m_ref.7, f32[64,256]{1,0:T(8,128)} %d_ref.5, s32[1,4]{1,0:T(1,128)} %map_in.1, ...), custom_call_target="tpu_custom_call" | custom-call | tf_op jit(solution)/shard_map/pack_x/pallas_call | solution.py:865
  2.4 3.0 %collective-permute-start = (f32[10,8,256]{2,1,0:T(8,128)S(1)}, f32[10,8,256]{2,1,0:T(8,128)S(1)}, u32[]{:S(2)}, u32[]{:S(2)}) collective-permute-start(f32[10,8,256]{2,1,0:T(8,128)S(1)} %get-tuple-element.51), channel_id=1, source_target_pairs={{0,4},{1,5},{2,6},{3,7},{4,0},{5,1},{6,2},{7,3},{8,12},{9,13},{10,... | collective-permute-start | bytes 245768 | tf_op jit(solution)/shard_map/ppermute | solution.py:853
  5.4 1.2 %interior_first.1 = (f32[3,5,64,256]{3,2,1,0:T(8,128)S(1)}, f32[3,5,64,256]{3,2,1,0:T(8,128)S(1)}, f32[3,2,64,256]{3,2,1,0:T(8,128)S(1)}, f32[64,256]{1,0:T(8,12...) custom-call(f32[3,8,64,256]{3,2,1,0:T(8,128)S(1)} %copy-done, ...), custom_call_target="tpu_custom_call" | custom-call | flops 1 | bytes 1 | tf_op jit(solution)/shard_map/interior_first/pallas_call | solution.py:919
  6.6 0.8 %build_strips.1.s_ref = f32[8,64,128]{2,1,0:T(8,128)S(1)} custom-call(f32[3,8,64,256]{3,2,1,0:T(8,128)S(1)} %copy-done, f32[3,8,64,256]{3,2,1,0:T(8,128)S(1)} %copy-done.1, s32[8,64,256]{2,1,0:T(8,128)S(1)} %copy-done.2, f32[64,256]{1,0:T(8,128)S(1)} %copy-done.5, f32[8,256]{1,0:T(8,128)S(1)} %get-tuple-element.55.id_ref.own_ref), custom_call_target="tpu_custom_call" | custom-call | flops 1 | bytes 1 | tf_op jit(solution)/shard_map/build_strips/pallas_call | solution.py:894
  7.4 1.7 %collective-permute-done.xa_ref = f32[10,8,256]{2,1,0:T(8,128)S(1)} collective-permute-done((f32[10,8,256]{2,1,0:T(8,128)S(1)}, f32[10,8,256]{2,1,0:T(8,128)S(1)}, u32[]{:S(2)}, u32[]{:S(2)}) %collective-permute-start) | collective-permute-done | bytes 81952 | tf_op jit(solution)/shard_map/ppermute | solution.py:853
  9.3 2.5 %collective-permute-start.3 = (f32[72,128]{1,0:T(8,128)S(1)}, f32[72,128]{1,0:T(8,128)S(1)}, u32[]{:S(2)}, u32[]{:S(2)}) collective-permute-start(f32[72,128]{1,0:T(8,128)S(1)} %get-tuple-element.59), channel_id=1, source_target_pairs={{0,4},{1,2},{2,1},{3,7},{4,0},{5,6},{6,5},{7,3},{8,12},{9,10},{10,... | collective-permute-start | bytes 110600 | tf_op jit(solution)/shard_map/ppermute | solution.py:853
  11.9 0.7 %transform.1 = (f32[64,256]{1,0:T(8,128)S(1)}, f32[2,3,2,64,256]{4,3,2,1,0:T(8,128)S(1)}) custom-call(f32[4,2,3,2,64,256]{5,4,3,2,1,0:T(8,128)S(1)} %copy-done.3, bf16[4,2,3,2,64,256]{5,4,3,2,1,0:T(8,128)(2,1)S(1)} %copy-done.4), custom_call_target="tpu_custom_call" | custom-call | flops 1 | bytes 1 | tf_op jit(solution)/shard_map/transform/pallas_call | solution.py:904
  12.6 0.7 %strips_x.1 = (f32[3,8,2,8,256]{4,3,2,1,0:T(8,128)S(1)}, f32[3,8,2,8,256]{4,3,2,1,0:T(8,128)S(1)}, f32[3,2,2,8,256]{4,3,2,1,0:T(8,128)S(1)}, f32[2,8,256]{2,1,0:T(8,128)S(1)}) custom-call(f32[3,8,64,256]{3,2,1,0:T(8,128)S(1)} %copy-done, f32[3,8,64,256]{3,2,1,0:T(8,128)S(1)} %copy-done.1, s32[8,64,256]{2,1,0:T(8,128)S(1)} %copy-done.2, ...), custom_call_target="tpu_custom_call" | custom-call | flops 1 | bytes 1 | tf_op jit(solution)/shard_map/strips_x/pallas_call | solution.py:951
  13.3 0.2 design.1
  13.5 0.3 collective-permute-done.3.yb_ref
  13.8 1.1 %gradient.1 = (f32[32,32,128]{2,1,0:T(8,128)S(1)}, f32[3,72,128]{2,1,0:T(8,128)S(1)}, f32[3,72,128]{2,1,0:T(8,128)S(1)}) custom-call(f32[8,64,128]{2,1,0:T(8,128)S(1)} %build_strips.1.s_ref, f32[8,8,128]{2,1,0:T(8,128)S(1)} %get-tuple-element.57.t_ref, f32[72,128]{1,0:T(8,128)S(1)} %collective-permute-done.2.ya_ref, ...), custom_call_target="tpu_custom_call" | custom-call | flops 1 | bytes 1 | tf_op jit(solution)/shard_map/gradient/pallas_call | solution.py:989
  15.0 1.5 %collective-permute-done.4.refs_1_ = f32[16,32,128]{2,1,0:T(8,128)S(1)} collective-permute-done((f32[16,32,128]{2,1,0:T(8,128)S(1)}, f32[16,32,128]{2,1,0:T(8,128)S(1)}, u32[]{:S(2)}, u32[]{:S(2)}) %collective-permute-start.4) | collective-permute-done | bytes 262176 | tf_op jit(solution)/shard_map/ppermute | solution.py:853
  16.5 2.1 %collective-permute-start.5 = (f32[4,32,128]{2,1,0:T(8,128)S(1)}, f32[4,32,128]{2,1,0:T(8,128)S(1)}, u32[]{:S(2)}, u32[]{:S(2)}) collective-permute-start(f32[4,32,128]{2,1,0:T(8,128)S(1)} %get-tuple-element.75), channel_id=1, source_target_pairs={{0,4},{1,5},{2,6},{3,7},{4,0},{5,1},{6,2},{7,3},{8,12},{9,13},{10,... | collective-permute-start | bytes 196616 | tf_op jit(solution)/shard_map/ppermute | solution.py:853
  18.6 1.0 %collective-permute-start.6 = (f32[4,32,128]{2,1,0:T(8,128)S(1)}, f32[4,32,128]{2,1,0:T(8,128)S(1)}, u32[]{:S(2)}, u32[]{:S(2)}) collective-permute-start(f32[4,32,128]{2,1,0:T(8,128)S(1)} %get-tuple-element.76), channel_id=1, source_target_pairs={{0,2},{1,3},{2,0},{3,1},{4,6},{5,7},{6,4},{7,5},{8,10},{9,11},{10,... | collective-permute-start | bytes 196616 | tf_op jit(solution)/shard_map/ppermute | solution.py:853
  19.7 0.5 %collective-permute-start.7 = (f32[4,32,128]{2,1,0:T(8,128)S(1)}, f32[4,32,128]{2,1,0:T(8,128)S(1)}, u32[]{:S(2)}, u32[]{:S(2)}) collective-permute-start(f32[4,32,128]{2,1,0:T(8,128)S(1)} %get-tuple-element.77), channel_id=1, source_target_pairs={{0,6},{1,7},{2,4},{3,5},{4,2},{5,3},{6,0},{7,1},{8,14},{9,15},{10,... | collective-permute-start | bytes 196616 | tf_op jit(solution)/shard_map/ppermute | solution.py:853
  20.2 1.4 %interior_rest.1 = (f32[3,8,64,256]{3,2,1,0:T(8,128)S(1)}, f32[3,8,64,256]{3,2,1,0:T(8,128)S(1)}, f32[8,128]{1,0:T(8,128)S(1)}) custom-call(f32[3,8,64,256]{3,2,1,0:T(8,128)S(1)} %copy-done, f32[3,8,64,256]{3,2,1,0:T(8,128)S(1)} %copy-done.1, s32[8,64,256]{2,1,0:T(8,128)S(1)} %copy-done.2, f32[32,128]{1,0:T(8,128)S(1)} %get-tuple-element.43.table, ...), custom_call_target="tpu_custom_call" | custom-call | flops 1 | bytes 1 | tf_op jit(solution)/shard_map/interior_rest/pallas_call | solution.py:930
  21.5 1.6 %collective-permute-done.6.refs_2_ = f32[4,32,128]{2,1,0:T(8,128)S(1)} collective-permute-done((f32[4,32,128]{2,1,0:T(8,128)S(1)}, f32[4,32,128]{2,1,0:T(8,128)S(1)}, u32[]{:S(2)}, u32[]{:S(2)}) %collective-permute-start.6) | collective-permute-done | bytes 65568 | tf_op jit(solution)/shard_map/ppermute | solution.py:853
  23.2 1.6 %collective-permute-done.7.refs_3_ = f32[4,32,128]{2,1,0:T(8,128)S(1)} collective-permute-done((f32[4,32,128]{2,1,0:T(8,128)S(1)}, f32[4,32,128]{2,1,0:T(8,128)S(1)}, u32[]{:S(2)}, u32[]{:S(2)}) %collective-permute-start.7) | collective-permute-done | bytes 65568 | tf_op jit(solution)/shard_map/ppermute | solution.py:853
  24.8 3.5 %collective-permute-start.10 = (f32[1,32,128]{2,1,0:T(8,128)S(1)}, f32[1,32,128]{2,1,0:T(8,128)S(1)}, u32[]{:S(2)}, u32[]{:S(2)}) collective-permute-start(f32[1,32,128]{2,1,0:T(8,128)S(1)} %get-tuple-element.82), channel_id=1, source_target_pairs={{0,24},{1,25},{2,26},{3,27},{4,28},{5,29},{6,30},{7,31},{8,16},{9,... | collective-permute-start | bytes 49160 | tf_op jit(solution)/shard_map/ppermute | solution.py:853
  28.3 1.0 %collective-permute-start.9 = (f32[1,32,128]{2,1,0:T(8,128)S(1)}, f32[1,32,128]{2,1,0:T(8,128)S(1)}, u32[]{:S(2)}, u32[]{:S(2)}) collective-permute-start(f32[1,32,128]{2,1,0:T(8,128)S(1)} %get-tuple-element.81), channel_id=1, source_target_pairs={{0,16},{1,17},{2,18},{3,19},{4,20},{5,21},{6,22},{7,23},{8,24},{9,... | collective-permute-start | bytes 49160 | tf_op jit(solution)/shard_map/ppermute | solution.py:853
  29.3 1.9 %merge.1 = (f32[3,8,64,256]{3,2,1,0:T(8,128)}, f32[3,8,64,256]{3,2,1,0:T(8,128)}) custom-call(f32[3,8,64,256]{3,2,1,0:T(8,128)S(1)} %get-tuple-element.49.e_ref, f32[3,8,64,256]{3,2,1,0:T(8,128)S(1)} %get-tuple-element.50.h_ref, f32[3,5,64,256]{3,2,1,0:T(8,128)S(1)} %get-tuple-element.44.em.e2_ref, f32[3,5,64,256]{3,2,1,0:T(8,128)S(1)} %get-tuple-element.45.hm, ...), custom_call_target="tpu_custom_call" | custom-call | flops 1 | bytes 1 | tf_op jit(solution)/shard_map/merge/pallas_call | solution.py:1019
  31.2 0.9 %collective-permute-done.8 = f32[1,32,128]{2,1,0:T(8,128)S(1)} collective-permute-done((f32[1,32,128]{2,1,0:T(8,128)S(1)}, f32[1,32,128]{2,1,0:T(8,128)S(1)}, u32[]{:S(2)}, u32[]{:S(2)}) %collective-permute-start.8) | collective-permute-done | bytes 16416 | tf_op jit(solution)/shard_map/ppermute | solution.py:853
  32.0 0.9 %collective-permute-done.9 = f32[1,32,128]{2,1,0:T(8,128)S(1)} collective-permute-done((f32[1,32,128]{2,1,0:T(8,128)S(1)}, f32[1,32,128]{2,1,0:T(8,128)S(1)}, u32[]{:S(2)}, u32[]{:S(2)}) %collective-permute-start.9) | collective-permute-done | bytes 16416 | tf_op jit(solution)/shard_map/ppermute | solution.py:853
  32.9 0.6 %add_add_fusion = f32[1,32,128]{2,1,0:T(8,128)} fusion(f32[1,32,128]{2,1,0:T(8,128)S(1)} %collective-permute-done.10, f32[1,32,128]{2,1,0:T(8,128)S(1)} %collective-permute-done.9, f32[1,32,128]{2,1,0:T(8,128)S(1)} %get-tuple-element.79, f32[1,32,128]{2,1,0:T(8,128)S(1)} %collective-permute-done.8), kind=kLoop, calls=%fused_computation | loop fusion | flops 12288 | bytes 81920 | tf_op jit(solution)/shard_map/add | solution.py:1041
  (24 shorter events, 0.5 us)
Async XLA Ops:
  0.6 4.8 %copy-start.5 = (f32[64,256]{1,0:T(8,128)S(1)}, f32[64,256]{1,0:T(8,128)}, u32[]{:S(2)}) copy-start(f32[64,256]{1,0:T(8,128)} %d_ref.5) | copy-start | bytes 196612
  0.6 4.8 %copy-start.2 = (s32[8,64,256]{2,1,0:T(8,128)S(1)}, s32[8,64,256]{2,1,0:T(8,128)}, u32[]{:S(2)}) copy-start(s32[8,64,256]{2,1,0:T(8,128)} %m_ref.7) | copy-start | bytes 1572868
  0.7 4.8 %copy-start = (f32[3,8,64,256]{3,2,1,0:T(8,128)S(1)}, f32[3,8,64,256]{3,2,1,0:T(8,128)}, u32[]{:S(2)}) copy-start(f32[3,8,64,256]{3,2,1,0:T(8,128)} %e_ref.7) | copy-start | bytes 4718596
  0.7 4.8 %copy-start.1 = (f32[3,8,64,256]{3,2,1,0:T(8,128)S(1)}, f32[3,8,64,256]{3,2,1,0:T(8,128)}, u32[]{:S(2)}) copy-start(f32[3,8,64,256]{3,2,1,0:T(8,128)} %h_ref.7) | copy-start | bytes 4718596
  2.4 6.7 %collective-permute-start = (f32[10,8,256]{2,1,0:T(8,128)S(1)}, f32[10,8,256]{2,1,0:T(8,128)S(1)}, u32[]{:S(2)}, u32[]{:S(2)}) collective-permute-start(f32[10,8,256]{2,1,0:T(8,128)S(1)} %get-tuple-element.51), channel_id=1, source_target_pairs={{0,4},{1,5},{2,6},{3,7},{4,0},{5,1},{6,2},{7,3},{8,12},{9,13},{10,... | collective-permute-start | bytes 245768 | tf_op jit(solution)/shard_map/ppermute | solution.py:853
  5.4 3.6 %collective-permute-start.1 = (f32[10,8,256]{2,1,0:T(8,128)S(1)}, f32[10,8,256]{2,1,0:T(8,128)S(1)}, u32[]{:S(2)}, u32[]{:S(2)}) collective-permute-start(f32[10,8,256]{2,1,0:T(8,128)S(1)} %get-tuple-element.52), channel_id=1, source_target_pairs={{0,1},{1,0},{2,3},{3,2},{4,8},{5,9},{6,10},{7,11},{8,4},{9,5},{10,... | collective-permute-start | bytes 245768 | tf_op jit(solution)/shard_map/ppermute | solution.py:853
  5.4 6.4 %copy-start.4 = (bf16[4,2,3,2,64,256]{5,4,3,2,1,0:T(8,128)(2,1)S(1)}, bf16[4,2,3,2,64,256]{5,4,3,2,1,0:T(8,128)(2,1)}, u32[]{:S(2)}) copy-start(bf16[4,2,3,2,64,256]{5,4,3,2,1,0:T(8,128)(2,1)} %fwd_ref.1) | copy-start | bytes 4718596
  6.6 5.3 %copy-start.3 = (f32[4,2,3,2,64,256]{5,4,3,2,1,0:T(8,128)S(1)}, f32[4,2,3,2,64,256]{5,4,3,2,1,0:T(8,128)}, u32[]{:S(2)}) copy-start(f32[4,2,3,2,64,256]{5,4,3,2,1,0:T(8,128)} %adj_ref.1) | copy-start | bytes 9437188
  9.3 4.2 %collective-permute-start.2 = (f32[72,128]{1,0:T(8,128)S(1)}, f32[72,128]{1,0:T(8,128)S(1)}, u32[]{:S(2)}, u32[]{:S(2)}) collective-permute-start(f32[72,128]{1,0:T(8,128)S(1)} %get-tuple-element.58), channel_id=1, source_target_pairs={{0,1},{1,0},{2,3},{3,2},{4,5},{5,4},{6,7},{7,6},{8,9},{9,8},{10,11... | collective-permute-start | bytes 110600 | tf_op jit(solution)/shard_map/ppermute | solution.py:853
  9.3 4.5 %collective-permute-start.3 = (f32[72,128]{1,0:T(8,128)S(1)}, f32[72,128]{1,0:T(8,128)S(1)}, u32[]{:S(2)}, u32[]{:S(2)}) collective-permute-start(f32[72,128]{1,0:T(8,128)S(1)} %get-tuple-element.59), channel_id=1, source_target_pairs={{0,4},{1,2},{2,1},{3,7},{4,0},{5,6},{6,5},{7,3},{8,12},{9,10},{10,... | collective-permute-start | bytes 110600 | tf_op jit(solution)/shard_map/ppermute | solution.py:853
  14.9 1.6 %collective-permute-start.4 = (f32[16,32,128]{2,1,0:T(8,128)S(1)}, f32[16,32,128]{2,1,0:T(8,128)S(1)}, u32[]{:S(2)}, u32[]{:S(2)}) collective-permute-start(f32[16,32,128]{2,1,0:T(8,128)S(1)} %slice.3), channel_id=1, source_target_pairs={{0,1},{1,0},{2,3},{3,2},{4,5},{5,4},{6,7},{7,6},{8,9},{9,8},{10,11... | collective-permute-start | bytes 786440 | tf_op jit(solution)/shard_map/ppermute | solution.py:853
  16.5 5.0 %collective-permute-start.5 = (f32[4,32,128]{2,1,0:T(8,128)S(1)}, f32[4,32,128]{2,1,0:T(8,128)S(1)}, u32[]{:S(2)}, u32[]{:S(2)}) collective-permute-start(f32[4,32,128]{2,1,0:T(8,128)S(1)} %get-tuple-element.75), channel_id=1, source_target_pairs={{0,4},{1,5},{2,6},{3,7},{4,0},{5,1},{6,2},{7,3},{8,12},{9,13},{10,... | collective-permute-start | bytes 196616 | tf_op jit(solution)/shard_map/ppermute | solution.py:853
  18.6 4.6 %collective-permute-start.6 = (f32[4,32,128]{2,1,0:T(8,128)S(1)}, f32[4,32,128]{2,1,0:T(8,128)S(1)}, u32[]{:S(2)}, u32[]{:S(2)}) collective-permute-start(f32[4,32,128]{2,1,0:T(8,128)S(1)} %get-tuple-element.76), channel_id=1, source_target_pairs={{0,2},{1,3},{2,0},{3,1},{4,6},{5,7},{6,4},{7,5},{8,10},{9,11},{10,... | collective-permute-start | bytes 196616 | tf_op jit(solution)/shard_map/ppermute | solution.py:853
  19.7 5.2 %collective-permute-start.7 = (f32[4,32,128]{2,1,0:T(8,128)S(1)}, f32[4,32,128]{2,1,0:T(8,128)S(1)}, u32[]{:S(2)}, u32[]{:S(2)}) collective-permute-start(f32[4,32,128]{2,1,0:T(8,128)S(1)} %get-tuple-element.77), channel_id=1, source_target_pairs={{0,6},{1,7},{2,4},{3,5},{4,2},{5,3},{6,0},{7,1},{8,14},{9,15},{10,... | collective-permute-start | bytes 196616 | tf_op jit(solution)/shard_map/ppermute | solution.py:853
  24.8 6.3 %collective-permute-start.10 = (f32[1,32,128]{2,1,0:T(8,128)S(1)}, f32[1,32,128]{2,1,0:T(8,128)S(1)}, u32[]{:S(2)}, u32[]{:S(2)}) collective-permute-start(f32[1,32,128]{2,1,0:T(8,128)S(1)} %get-tuple-element.82), channel_id=1, source_target_pairs={{0,24},{1,25},{2,26},{3,27},{4,28},{5,29},{6,30},{7,31},{8,16},{9,... | collective-permute-start | bytes 49160 | tf_op jit(solution)/shard_map/ppermute | solution.py:853
  28.3 3.7 %collective-permute-start.8 = (f32[1,32,128]{2,1,0:T(8,128)S(1)}, f32[1,32,128]{2,1,0:T(8,128)S(1)}, u32[]{:S(2)}, u32[]{:S(2)}) collective-permute-start(f32[1,32,128]{2,1,0:T(8,128)S(1)} %get-tuple-element.80), channel_id=1, source_target_pairs={{0,8},{1,9},{2,10},{3,11},{4,12},{5,13},{6,14},{7,15},{8,0},{9,1},... | collective-permute-start | bytes 49160 | tf_op jit(solution)/shard_map/ppermute | solution.py:853
  28.3 4.6 %collective-permute-start.9 = (f32[1,32,128]{2,1,0:T(8,128)S(1)}, f32[1,32,128]{2,1,0:T(8,128)S(1)}, u32[]{:S(2)}, u32[]{:S(2)}) collective-permute-start(f32[1,32,128]{2,1,0:T(8,128)S(1)} %get-tuple-element.81), channel_id=1, source_target_pairs={{0,16},{1,17},{2,18},{3,19},{4,20},{5,21},{6,22},{7,23},{8,24},{9,... | collective-permute-start | bytes 49160 | tf_op jit(solution)/shard_map/ppermute | solution.py:853

commit v5 on v4

--- a/solution.py
+++ b/solution.py
@@ -686,7 +686,7 @@
 
 
 def gradient(
-    s_ref, t_ref, ya_ref, yb_ref, xa_ref, xb_ref, table, own_ref, l_ref, gs_ref, ss_ref, coef_ref,
+    s_ref, t_ref, yb_ref, ya_ref, xa_ref, xb_ref, table, own_ref, l_ref, gs_ref, ss_ref, coef_ref,
     buf_ref, ye_ref, yh_ref, lpad, vpad, gpad,
 ):
     width_x, width_y = l_ref.shape
@@ -1000,7 +1000,7 @@
         compiler_params=params(),
         cost_estimate=cost(1, 1),
         name="gradient",
-    )(strip, tails, ya, yb, xa, xb, table, own_ids, local, weight_y, base_y, coef_y)
+    )(strip, tails, yb, ya, xa, xb, table, own_ids, local, weight_y, base_y, coef_y)
 
     half = devices * rows_mine // 2
     far = count_gx // 2
@@ -1014,7 +1014,7 @@
         name="first_sum",
     )(buf, got)
     parts = [parts[0]] + [
-        pair(parts[k], lambda i, j: (i ^ (k & 1), j ^ (k >> 1 << 1))) for k in range(1, count_gy)
+        pair(parts[k], lambda i, j: (i ^ (k & 1), j ^ (k >> 1 << 1))) for k in range(count_gy - 1, 0, -1)
     ]
     e_out, h_out = pl.pallas_call(
         merge,

time: 33.7 us -> 33.3 us (0.988)
  waiting for transfers between devices: 8.52 us -> 8.09 us
    ppermute x11, waiting for transfers between devices: 8.52 us -> 8.09 us  [pair(): return lax.ppermute(block, ('gx', 'gy'), route)]
  transfers between devices with their start and end apart: 11 -> 11, of which waited for: 7 -> 8; matrix products, arithmetic and copies ran while one was open for 0% -> 0% of each run, Pallas kernels for 20% -> 20%
where the time goes in v5:
time: 33.3 us; the launch traced here: 33.2 us
  starting transfers between devices  13.9 us (42%)
  Pallas kernels  9.79 us (29%)
  waiting for transfers between devices  8.09 us (24%)
  between operations  0.79 us (2%)
  other arithmetic  0.61 us (2%)
    ppermute x11, starting transfers between devices, pair(): return lax.ppermute(block, ('gx', 'gy'), route)  13.9 us
    ppermute x11, waiting for transfers between devices, pair(): return lax.ppermute(block, ('gx', 'gy'), route)  8.09 us
    pallas_call x1, Pallas kernels, on_device(): pl.pallas_call(merge, out_shape=(full,) * 2, in_specs=[VMEM] * 8, out_spe...  1.85 us
    pallas_call x1, Pallas kernels, on_device(): pl.pallas_call(pack_x, out_shape=(pltpu.VMEM(face.shape, F32), pltpu.VMEM...  1.68 us
    pallas_call x1, Pallas kernels, on_device(): pl.pallas_call(interior_rest, out_shape=(full, full, struct(SUB, LANES)),...  1.36 us
    pallas_call x1, Pallas kernels, on_device(): pl.pallas_call(interior_first, out_shape=(middle, middle, struct(3, PLANE...  1.15 us
    pallas_call x1, Pallas kernels, on_device(): pl.pallas_call(gradient, out_shape=(struct(devices * rows_mine, lines, LA...  1.08 us
    pallas_call x1, Pallas kernels, on_device(): pl.pallas_call(build_strips, out_shape=struct(8, width_x, LANES), in_spec...  0.75 us
  transfers between devices with their start and end apart: 11, of which 8 were waited for; matrix products, arithmetic and copies ran while one was open for 0% of the time, Pallas kernels for 20%

profile of v5, /device:TPU:0, one launch (start us, length us, event | category | flops | bytes accessed | tf_op | source)
XLA Modules:
  0.0 33.2 jit_solution(17446124674342426879)
XLA Ops:
  0.7 1.7 %pack_x.1 = (f32[10,8,256]{2,1,0:T(8,128)S(1)}, f32[10,8,256]{2,1,0:T(8,128)S(1)}, f32[8,256]{1,0:T(8,128)S(1)}, f32[32,128]{1,0:T(8,128)S(1)}) custom-call(f32[3,8,64,256]{3,2,1,0:T(8,128)} %e_ref.7, f32[3,8,64,256]{3,2,1,0:T(8,128)} %h_ref.7, s32[8,64,256]{2,1,0:T(8,128)} %m_ref.7, f32[64,256]{1,0:T(8,128)} %d_ref.5, s32[1,4]{1,0:T(1,128)} %map_in.1, ...), custom_call_target="tpu_custom_call" | custom-call | tf_op jit(solution)/shard_map/pack_x/pallas_call | solution.py:865
  2.4 3.0 %collective-permute-start = (f32[10,8,256]{2,1,0:T(8,128)S(1)}, f32[10,8,256]{2,1,0:T(8,128)S(1)}, u32[]{:S(2)}, u32[]{:S(2)}) collective-permute-start(f32[10,8,256]{2,1,0:T(8,128)S(1)} %get-tuple-element.51), channel_id=1, source_target_pairs={{0,4},{1,5},{2,6},{3,7},{4,0},{5,1},{6,2},{7,3},{8,12},{9,13},{10,... | collective-permute-start | bytes 245768 | tf_op jit(solution)/shard_map/ppermute | solution.py:853
  5.4 1.2 %interior_first.1 = (f32[3,5,64,256]{3,2,1,0:T(8,128)S(1)}, f32[3,5,64,256]{3,2,1,0:T(8,128)S(1)}, f32[3,2,64,256]{3,2,1,0:T(8,128)S(1)}, f32[64,256]{1,0:T(8,12...) custom-call(f32[3,8,64,256]{3,2,1,0:T(8,128)S(1)} %copy-done, ...), custom_call_target="tpu_custom_call" | custom-call | flops 1 | bytes 1 | tf_op jit(solution)/shard_map/interior_first/pallas_call | solution.py:919
  6.6 0.8 %build_strips.1.s_ref = f32[8,64,128]{2,1,0:T(8,128)S(1)} custom-call(f32[3,8,64,256]{3,2,1,0:T(8,128)S(1)} %copy-done, f32[3,8,64,256]{3,2,1,0:T(8,128)S(1)} %copy-done.1, s32[8,64,256]{2,1,0:T(8,128)S(1)} %copy-done.2, f32[64,256]{1,0:T(8,128)S(1)} %copy-done.5, f32[8,256]{1,0:T(8,128)S(1)} %get-tuple-element.55.id_ref.own_ref), custom_call_target="tpu_custom_call" | custom-call | flops 1 | bytes 1 | tf_op jit(solution)/shard_map/build_strips/pallas_call | solution.py:894
  7.4 1.7 %collective-permute-done.xa_ref = f32[10,8,256]{2,1,0:T(8,128)S(1)} collective-permute-done((f32[10,8,256]{2,1,0:T(8,128)S(1)}, f32[10,8,256]{2,1,0:T(8,128)S(1)}, u32[]{:S(2)}, u32[]{:S(2)}) %collective-permute-start) | collective-permute-done | bytes 81952 | tf_op jit(solution)/shard_map/ppermute | solution.py:853
  9.3 2.5 %collective-permute-start.2 = (f32[72,128]{1,0:T(8,128)S(1)}, f32[72,128]{1,0:T(8,128)S(1)}, u32[]{:S(2)}, u32[]{:S(2)}) collective-permute-start(f32[72,128]{1,0:T(8,128)S(1)} %get-tuple-element.58), channel_id=1, source_target_pairs={{0,4},{1,2},{2,1},{3,7},{4,0},{5,6},{6,5},{7,3},{8,12},{9,10},{10,... | collective-permute-start | bytes 110600 | tf_op jit(solution)/shard_map/ppermute | solution.py:853
  11.8 0.7 %transform.1 = (f32[64,256]{1,0:T(8,128)S(1)}, f32[2,3,2,64,256]{4,3,2,1,0:T(8,128)S(1)}) custom-call(f32[4,2,3,2,64,256]{5,4,3,2,1,0:T(8,128)S(1)} %copy-done.3, bf16[4,2,3,2,64,256]{5,4,3,2,1,0:T(8,128)(2,1)S(1)} %copy-done.4), custom_call_target="tpu_custom_call" | custom-call | flops 1 | bytes 1 | tf_op jit(solution)/shard_map/transform/pallas_call | solution.py:904
  12.5 0.7 %strips_x.1 = (f32[3,8,2,8,256]{4,3,2,1,0:T(8,128)S(1)}, f32[3,8,2,8,256]{4,3,2,1,0:T(8,128)S(1)}, f32[3,2,2,8,256]{4,3,2,1,0:T(8,128)S(1)}, f32[2,8,256]{2,1,0:T(8,128)S(1)}) custom-call(f32[3,8,64,256]{3,2,1,0:T(8,128)S(1)} %copy-done, f32[3,8,64,256]{3,2,1,0:T(8,128)S(1)} %copy-done.1, s32[8,64,256]{2,1,0:T(8,128)S(1)} %copy-done.2, ...), custom_call_target="tpu_custom_call" | custom-call | flops 1 | bytes 1 | tf_op jit(solution)/shard_map/strips_x/pallas_call | solution.py:951
  13.4 0.3 collective-permute-done.2.yb_ref
  13.7 1.1 %gradient.1 = (f32[32,32,128]{2,1,0:T(8,128)S(1)}, f32[3,72,128]{2,1,0:T(8,128)S(1)}, f32[3,72,128]{2,1,0:T(8,128)S(1)}) custom-call(f32[8,64,128]{2,1,0:T(8,128)S(1)} %build_strips.1.s_ref, f32[8,8,128]{2,1,0:T(8,128)S(1)} %get-tuple-element.57.t_ref, f32[72,128]{1,0:T(8,128)S(1)} %collective-permute-done.2.yb_ref, ...), custom_call_target="tpu_custom_call" | custom-call | flops 1 | bytes 1 | tf_op jit(solution)/shard_map/gradient/pallas_call | solution.py:989
  14.8 0.3 collective-permute-start.4
  15.1 1.3 %collective-permute-done.4.refs_1_ = f32[16,32,128]{2,1,0:T(8,128)S(1)} collective-permute-done((f32[16,32,128]{2,1,0:T(8,128)S(1)}, f32[16,32,128]{2,1,0:T(8,128)S(1)}, u32[]{:S(2)}, u32[]{:S(2)}) %collective-permute-start.4) | collective-permute-done | bytes 262176 | tf_op jit(solution)/shard_map/ppermute | solution.py:853
  16.5 2.5 %collective-permute-start.5 = (f32[4,32,128]{2,1,0:T(8,128)S(1)}, f32[4,32,128]{2,1,0:T(8,128)S(1)}, u32[]{:S(2)}, u32[]{:S(2)}) collective-permute-start(f32[4,32,128]{2,1,0:T(8,128)S(1)} %get-tuple-element.75), channel_id=1, source_target_pairs={{0,6},{1,7},{2,4},{3,5},{4,2},{5,3},{6,0},{7,1},{8,14},{9,15},{10,... | collective-permute-start | bytes 196616 | tf_op jit(solution)/shard_map/ppermute | solution.py:853
  19.0 1.0 %collective-permute-start.6 = (f32[4,32,128]{2,1,0:T(8,128)S(1)}, f32[4,32,128]{2,1,0:T(8,128)S(1)}, u32[]{:S(2)}, u32[]{:S(2)}) collective-permute-start(f32[4,32,128]{2,1,0:T(8,128)S(1)} %get-tuple-element.76), channel_id=1, source_target_pairs={{0,2},{1,3},{2,0},{3,1},{4,6},{5,7},{6,4},{7,5},{8,10},{9,11},{10,... | collective-permute-start | bytes 196616 | tf_op jit(solution)/shard_map/ppermute | solution.py:853
  20.0 1.4 %interior_rest.1 = (f32[3,8,64,256]{3,2,1,0:T(8,128)S(1)}, f32[3,8,64,256]{3,2,1,0:T(8,128)S(1)}, f32[8,128]{1,0:T(8,128)S(1)}) custom-call(f32[3,8,64,256]{3,2,1,0:T(8,128)S(1)} %copy-done, f32[3,8,64,256]{3,2,1,0:T(8,128)S(1)} %copy-done.1, s32[8,64,256]{2,1,0:T(8,128)S(1)} %copy-done.2, f32[32,128]{1,0:T(8,128)S(1)} %get-tuple-element.43.table, ...), custom_call_target="tpu_custom_call" | custom-call | flops 1 | bytes 1 | tf_op jit(solution)/shard_map/interior_rest/pallas_call | solution.py:930
  21.4 1.0 %collective-permute-done.5.refs_1_ = f32[4,32,128]{2,1,0:T(8,128)S(1)} collective-permute-done((f32[4,32,128]{2,1,0:T(8,128)S(1)}, f32[4,32,128]{2,1,0:T(8,128)S(1)}, u32[]{:S(2)}, u32[]{:S(2)}) %collective-permute-start.5) | collective-permute-done | bytes 65568 | tf_op jit(solution)/shard_map/ppermute | solution.py:853
  22.4 1.2 %collective-permute-done.6.refs_2_ = f32[4,32,128]{2,1,0:T(8,128)S(1)} collective-permute-done((f32[4,32,128]{2,1,0:T(8,128)S(1)}, f32[4,32,128]{2,1,0:T(8,128)S(1)}, u32[]{:S(2)}, u32[]{:S(2)}) %collective-permute-start.6) | collective-permute-done | bytes 65568 | tf_op jit(solution)/shard_map/ppermute | solution.py:853
  23.6 0.7 %collective-permute-done.7.refs_3_ = f32[4,32,128]{2,1,0:T(8,128)S(1)} collective-permute-done((f32[4,32,128]{2,1,0:T(8,128)S(1)}, f32[4,32,128]{2,1,0:T(8,128)S(1)}, u32[]{:S(2)}, u32[]{:S(2)}) %collective-permute-start.7) | collective-permute-done | bytes 65568 | tf_op jit(solution)/shard_map/ppermute | solution.py:853
  24.3 3.6 %collective-permute-start.10 = (f32[1,32,128]{2,1,0:T(8,128)S(1)}, f32[1,32,128]{2,1,0:T(8,128)S(1)}, u32[]{:S(2)}, u32[]{:S(2)}) collective-permute-start(f32[1,32,128]{2,1,0:T(8,128)S(1)} %get-tuple-element.82), channel_id=1, source_target_pairs={{0,24},{1,25},{2,26},{3,27},{4,28},{5,29},{6,30},{7,31},{8,16},{9,... | collective-permute-start | bytes 49160 | tf_op jit(solution)/shard_map/ppermute | solution.py:853
  27.9 0.8 %collective-permute-start.9 = (f32[1,32,128]{2,1,0:T(8,128)S(1)}, f32[1,32,128]{2,1,0:T(8,128)S(1)}, u32[]{:S(2)}, u32[]{:S(2)}) collective-permute-start(f32[1,32,128]{2,1,0:T(8,128)S(1)} %get-tuple-element.81), channel_id=1, source_target_pairs={{0,16},{1,17},{2,18},{3,19},{4,20},{5,21},{6,22},{7,23},{8,24},{9,... | collective-permute-start | bytes 49160 | tf_op jit(solution)/shard_map/ppermute | solution.py:853
  28.8 1.9 %merge.1 = (f32[3,8,64,256]{3,2,1,0:T(8,128)}, f32[3,8,64,256]{3,2,1,0:T(8,128)}) custom-call(f32[3,8,64,256]{3,2,1,0:T(8,128)S(1)} %get-tuple-element.49.e_ref, f32[3,8,64,256]{3,2,1,0:T(8,128)S(1)} %get-tuple-element.50.h_ref, f32[3,5,64,256]{3,2,1,0:T(8,128)S(1)} %get-tuple-element.44.em.e2_ref, f32[3,5,64,256]{3,2,1,0:T(8,128)S(1)} %get-tuple-element.45.hm, ...), custom_call_target="tpu_custom_call" | custom-call | flops 1 | bytes 1 | tf_op jit(solution)/shard_map/merge/pallas_call | solution.py:1019
  30.6 1.0 %collective-permute-done.8 = f32[1,32,128]{2,1,0:T(8,128)S(1)} collective-permute-done((f32[1,32,128]{2,1,0:T(8,128)S(1)}, f32[1,32,128]{2,1,0:T(8,128)S(1)}, u32[]{:S(2)}, u32[]{:S(2)}) %collective-permute-start.8) | collective-permute-done | bytes 16416 | tf_op jit(solution)/shard_map/ppermute | solution.py:853
  31.7 0.9 %collective-permute-done.9 = f32[1,32,128]{2,1,0:T(8,128)S(1)} collective-permute-done((f32[1,32,128]{2,1,0:T(8,128)S(1)}, f32[1,32,128]{2,1,0:T(8,128)S(1)}, u32[]{:S(2)}, u32[]{:S(2)}) %collective-permute-start.9) | collective-permute-done | bytes 16416 | tf_op jit(solution)/shard_map/ppermute | solution.py:853
  32.6 0.6 %add_add_fusion = f32[1,32,128]{2,1,0:T(8,128)} fusion(f32[1,32,128]{2,1,0:T(8,128)S(1)} %collective-permute-done.10, f32[1,32,128]{2,1,0:T(8,128)S(1)} %collective-permute-done.9, f32[1,32,128]{2,1,0:T(8,128)S(1)} %get-tuple-element.79, f32[1,32,128]{2,1,0:T(8,128)S(1)} %collective-permute-done.8), kind=kLoop, calls=%fused_computation | loop fusion | flops 12288 | bytes 81920 | tf_op jit(solution)/shard_map/add | solution.py:1041
  (24 shorter events, 0.6 us)
Async XLA Ops:
  0.6 4.8 %copy-start.5 = (f32[64,256]{1,0:T(8,128)S(1)}, f32[64,256]{1,0:T(8,128)}, u32[]{:S(2)}) copy-start(f32[64,256]{1,0:T(8,128)} %d_ref.5) | copy-start | bytes 196612
  0.6 4.8 %copy-start.2 = (s32[8,64,256]{2,1,0:T(8,128)S(1)}, s32[8,64,256]{2,1,0:T(8,128)}, u32[]{:S(2)}) copy-start(s32[8,64,256]{2,1,0:T(8,128)} %m_ref.7) | copy-start | bytes 1572868
  0.7 4.8 %copy-start = (f32[3,8,64,256]{3,2,1,0:T(8,128)S(1)}, f32[3,8,64,256]{3,2,1,0:T(8,128)}, u32[]{:S(2)}) copy-start(f32[3,8,64,256]{3,2,1,0:T(8,128)} %e_ref.7) | copy-start | bytes 4718596
  0.7 4.8 %copy-start.1 = (f32[3,8,64,256]{3,2,1,0:T(8,128)S(1)}, f32[3,8,64,256]{3,2,1,0:T(8,128)}, u32[]{:S(2)}) copy-start(f32[3,8,64,256]{3,2,1,0:T(8,128)} %h_ref.7) | copy-start | bytes 4718596
  2.4 6.7 %collective-permute-start = (f32[10,8,256]{2,1,0:T(8,128)S(1)}, f32[10,8,256]{2,1,0:T(8,128)S(1)}, u32[]{:S(2)}, u32[]{:S(2)}) collective-permute-start(f32[10,8,256]{2,1,0:T(8,128)S(1)} %get-tuple-element.51), channel_id=1, source_target_pairs={{0,4},{1,5},{2,6},{3,7},{4,0},{5,1},{6,2},{7,3},{8,12},{9,13},{10,... | collective-permute-start | bytes 245768 | tf_op jit(solution)/shard_map/ppermute | solution.py:853
  5.4 3.6 %collective-permute-start.1 = (f32[10,8,256]{2,1,0:T(8,128)S(1)}, f32[10,8,256]{2,1,0:T(8,128)S(1)}, u32[]{:S(2)}, u32[]{:S(2)}) collective-permute-start(f32[10,8,256]{2,1,0:T(8,128)S(1)} %get-tuple-element.52), channel_id=1, source_target_pairs={{0,1},{1,0},{2,3},{3,2},{4,8},{5,9},{6,10},{7,11},{8,4},{9,5},{10,... | collective-permute-start | bytes 245768 | tf_op jit(solution)/shard_map/ppermute | solution.py:853
  5.4 6.4 %copy-start.4 = (bf16[4,2,3,2,64,256]{5,4,3,2,1,0:T(8,128)(2,1)S(1)}, bf16[4,2,3,2,64,256]{5,4,3,2,1,0:T(8,128)(2,1)}, u32[]{:S(2)}) copy-start(bf16[4,2,3,2,64,256]{5,4,3,2,1,0:T(8,128)(2,1)} %fwd_ref.1) | copy-start | bytes 4718596
  6.6 5.2 %copy-start.3 = (f32[4,2,3,2,64,256]{5,4,3,2,1,0:T(8,128)S(1)}, f32[4,2,3,2,64,256]{5,4,3,2,1,0:T(8,128)}, u32[]{:S(2)}) copy-start(f32[4,2,3,2,64,256]{5,4,3,2,1,0:T(8,128)} %adj_ref.1) | copy-start | bytes 9437188
  9.3 4.5 %collective-permute-start.2 = (f32[72,128]{1,0:T(8,128)S(1)}, f32[72,128]{1,0:T(8,128)S(1)}, u32[]{:S(2)}, u32[]{:S(2)}) collective-permute-start(f32[72,128]{1,0:T(8,128)S(1)} %get-tuple-element.58), channel_id=1, source_target_pairs={{0,4},{1,2},{2,1},{3,7},{4,0},{5,6},{6,5},{7,3},{8,12},{9,10},{10,... | collective-permute-start | bytes 110600 | tf_op jit(solution)/shard_map/ppermute | solution.py:853
  11.8 1.9 %collective-permute-start.3 = (f32[72,128]{1,0:T(8,128)S(1)}, f32[72,128]{1,0:T(8,128)S(1)}, u32[]{:S(2)}, u32[]{:S(2)}) collective-permute-start(f32[72,128]{1,0:T(8,128)S(1)} %get-tuple-element.59), channel_id=1, source_target_pairs={{0,1},{1,0},{2,3},{3,2},{4,5},{5,4},{6,7},{7,6},{8,9},{9,8},{10,11... | collective-permute-start | bytes 110600 | tf_op jit(solution)/shard_map/ppermute | solution.py:853
  14.8 1.6 %collective-permute-start.4 = (f32[16,32,128]{2,1,0:T(8,128)S(1)}, f32[16,32,128]{2,1,0:T(8,128)S(1)}, u32[]{:S(2)}, u32[]{:S(2)}) collective-permute-start(f32[16,32,128]{2,1,0:T(8,128)S(1)} %slice.3), channel_id=1, source_target_pairs={{0,1},{1,0},{2,3},{3,2},{4,5},{5,4},{6,7},{7,6},{8,9},{9,8},{10,11... | collective-permute-start | bytes 786440 | tf_op jit(solution)/shard_map/ppermute | solution.py:853
  16.5 5.9 %collective-permute-start.5 = (f32[4,32,128]{2,1,0:T(8,128)S(1)}, f32[4,32,128]{2,1,0:T(8,128)S(1)}, u32[]{:S(2)}, u32[]{:S(2)}) collective-permute-start(f32[4,32,128]{2,1,0:T(8,128)S(1)} %get-tuple-element.75), channel_id=1, source_target_pairs={{0,6},{1,7},{2,4},{3,5},{4,2},{5,3},{6,0},{7,1},{8,14},{9,15},{10,... | collective-permute-start | bytes 196616 | tf_op jit(solution)/shard_map/ppermute | solution.py:853
  19.0 4.6 %collective-permute-start.6 = (f32[4,32,128]{2,1,0:T(8,128)S(1)}, f32[4,32,128]{2,1,0:T(8,128)S(1)}, u32[]{:S(2)}, u32[]{:S(2)}) collective-permute-start(f32[4,32,128]{2,1,0:T(8,128)S(1)} %get-tuple-element.76), channel_id=1, source_target_pairs={{0,2},{1,3},{2,0},{3,1},{4,6},{5,7},{6,4},{7,5},{8,10},{9,11},{10,... | collective-permute-start | bytes 196616 | tf_op jit(solution)/shard_map/ppermute | solution.py:853
  20.0 4.3 %collective-permute-start.7 = (f32[4,32,128]{2,1,0:T(8,128)S(1)}, f32[4,32,128]{2,1,0:T(8,128)S(1)}, u32[]{:S(2)}, u32[]{:S(2)}) collective-permute-start(f32[4,32,128]{2,1,0:T(8,128)S(1)} %get-tuple-element.77), channel_id=1, source_target_pairs={{0,4},{1,5},{2,6},{3,7},{4,0},{5,1},{6,2},{7,3},{8,12},{9,13},{10,... | collective-permute-start | bytes 196616 | tf_op jit(solution)/shard_map/ppermute | solution.py:853
  24.3 6.3 %collective-permute-start.10 = (f32[1,32,128]{2,1,0:T(8,128)S(1)}, f32[1,32,128]{2,1,0:T(8,128)S(1)}, u32[]{:S(2)}, u32[]{:S(2)}) collective-permute-start(f32[1,32,128]{2,1,0:T(8,128)S(1)} %get-tuple-element.82), channel_id=1, source_target_pairs={{0,24},{1,25},{2,26},{3,27},{4,28},{5,29},{6,30},{7,31},{8,16},{9,... | collective-permute-start | bytes 49160 | tf_op jit(solution)/shard_map/ppermute | solution.py:853
  27.9 3.7 %collective-permute-start.8 = (f32[1,32,128]{2,1,0:T(8,128)S(1)}, f32[1,32,128]{2,1,0:T(8,128)S(1)}, u32[]{:S(2)}, u32[]{:S(2)}) collective-permute-start(f32[1,32,128]{2,1,0:T(8,128)S(1)} %get-tuple-element.80), channel_id=1, source_target_pairs={{0,8},{1,9},{2,10},{3,11},{4,12},{5,13},{6,14},{7,15},{8,0},{9,1},... | collective-permute-start | bytes 49160 | tf_op jit(solution)/shard_map/ppermute | solution.py:853
  27.9 4.6 %collective-permute-start.9 = (f32[1,32,128]{2,1,0:T(8,128)S(1)}, f32[1,32,128]{2,1,0:T(8,128)S(1)}, u32[]{:S(2)}, u32[]{:S(2)}) collective-permute-start(f32[1,32,128]{2,1,0:T(8,128)S(1)} %get-tuple-element.81), channel_id=1, source_target_pairs={{0,16},{1,17},{2,18},{3,19},{4,20},{5,21},{6,22},{7,23},{8,24},{9,... | collective-permute-start | bytes 49160 | tf_op jit(solution)/shard_map/ppermute | solution.py:853

commit v6 on v5

--- a/solution.py
+++ b/solution.py
@@ -834,10 +834,18 @@
         outs[k][...] = buf_ref[rows] + got_ref[rows]
 
 
+def rounds(count):
+    if count == 4:
+        return [(0, 1, 2, 3), (1, 3, 0, 2), (3, 2, 1, 0), (2, 0, 3, 1)]
+    return [tuple(k ^ n for k in range(count)) for n in range(count)]
+
+
 def second_sum(parts, rows_mine, *refs):
     ins, outs = refs[:parts], refs[parts + 1 :]
-    for k, out in enumerate(outs):
-        rows = pl.ds(k * rows_mine, rows_mine)
+    here = lax.axis_index("gx") >> 1
+    for out, targets in zip(outs, rounds(len(outs))):
+        slot = sum(jnp.where(here == k, k ^ to, 0) for k, to in enumerate(targets))
+        rows = pl.ds(slot * rows_mine, rows_mine)
         out[...] = sum(ref[rows] for ref in ins[1:]) + ins[0][rows]
 
 
@@ -1037,7 +1045,10 @@
         compiler_params=params(),
         name="second_sum",
     )(*parts, done)
-    parts = [parts[0]] + [pair(parts[k], lambda i, j: (i ^ (k << 1), j)) for k in range(1, far)]
+    parts = [parts[0]] + [
+        pair(part, lambda i, j: (2 * targets[i >> 1] + i % 2, j))
+        for part, targets in zip(parts[1:], rounds(far)[1:])
+    ]
     param_grad = sum(parts[1:], parts[0]).reshape(rows_mine, TILE * TILE)
 
     return e_out, h_out, param_grad

time: 33.3 us -> 33.4 us (level)
  starting transfers between devices: 13.9 us -> 15.1 us
  waiting for transfers between devices: 8.09 us -> 6.9 us
    ppermute x11, starting transfers between devices: 13.9 us -> 15.1 us  [pair(): return lax.ppermute(block, ('gx', 'gy'), route)]
    ppermute x11, waiting for transfers between devices: 8.09 us -> 6.9 us  [pair(): return lax.ppermute(block, ('gx', 'gy'), route)]
  transfers between devices with their start and end apart: 11 -> 11, of which waited for: 8 -> 7; matrix products, arithmetic and copies ran while one was open for 0% -> 0% of each run, Pallas kernels for 20% -> 20%
where the time goes in v6:
time: 33.4 us; the launch traced here: 33.2 us
  starting transfers between devices  15.1 us (45%)
  Pallas kernels  9.8 us (29%)
  waiting for transfers between devices  6.9 us (21%)
  between operations  0.79 us (2%)
  other arithmetic  0.61 us (2%)
    ppermute x11, starting transfers between devices, pair(): return lax.ppermute(block, ('gx', 'gy'), route)  15.1 us
    ppermute x11, waiting for transfers between devices, pair(): return lax.ppermute(block, ('gx', 'gy'), route)  6.9 us
    pallas_call x1, Pallas kernels, on_device(): pl.pallas_call(merge, out_shape=(full,) * 2, in_specs=[VMEM] * 8, out_spe...  1.85 us
    pallas_call x1, Pallas kernels, on_device(): pl.pallas_call(pack_x, out_shape=(pltpu.VMEM(face.shape, F32), pltpu.VMEM...  1.68 us
    pallas_call x1, Pallas kernels, on_device(): pl.pallas_call(interior_rest, out_shape=(full, full, struct(SUB, LANES)),...  1.36 us
    pallas_call x1, Pallas kernels, on_device(): pl.pallas_call(interior_first, out_shape=(middle, middle, struct(3, PLANE...  1.15 us
    pallas_call x1, Pallas kernels, on_device(): pl.pallas_call(gradient, out_shape=(struct(devices * rows_mine, lines, LA...  1.08 us
    pallas_call x1, Pallas kernels, on_device(): pl.pallas_call(build_strips, out_shape=struct(8, width_x, LANES), in_spec...  0.75 us
  transfers between devices with their start and end apart: 11, of which 7 were waited for; matrix products, arithmetic and copies ran while one was open for 0% of the time, Pallas kernels for 20%

profile of v6, /device:TPU:0, one launch (start us, length us, event | category | flops | bytes accessed | tf_op | source)
XLA Modules:
  0.0 33.2 jit_solution(1376339418410272216)
XLA Ops:
  0.7 1.7 %pack_x.1 = (f32[10,8,256]{2,1,0:T(8,128)S(1)}, f32[10,8,256]{2,1,0:T(8,128)S(1)}, f32[8,256]{1,0:T(8,128)S(1)}, f32[32,128]{1,0:T(8,128)S(1)}) custom-call(f32[3,8,64,256]{3,2,1,0:T(8,128)} %e_ref.7, f32[3,8,64,256]{3,2,1,0:T(8,128)} %h_ref.7, s32[8,64,256]{2,1,0:T(8,128)} %m_ref.7, f32[64,256]{1,0:T(8,128)} %d_ref.5, s32[1,4]{1,0:T(1,128)} %map_in.1, ...), custom_call_target="tpu_custom_call" | custom-call | tf_op jit(solution)/shard_map/pack_x/pallas_call | solution.py:873
  2.4 3.0 %collective-permute-start = (f32[10,8,256]{2,1,0:T(8,128)S(1)}, f32[10,8,256]{2,1,0:T(8,128)S(1)}, u32[]{:S(2)}, u32[]{:S(2)}) collective-permute-start(f32[10,8,256]{2,1,0:T(8,128)S(1)} %get-tuple-element.51), channel_id=1, source_target_pairs={{0,4},{1,5},{2,6},{3,7},{4,0},{5,1},{6,2},{7,3},{8,12},{9,13},{10,... | collective-permute-start | bytes 245768 | tf_op jit(solution)/shard_map/ppermute | solution.py:861
  5.4 1.2 %interior_first.1 = (f32[3,5,64,256]{3,2,1,0:T(8,128)S(1)}, f32[3,5,64,256]{3,2,1,0:T(8,128)S(1)}, f32[3,2,64,256]{3,2,1,0:T(8,128)S(1)}, f32[64,256]{1,0:T(8,12...) custom-call(f32[3,8,64,256]{3,2,1,0:T(8,128)S(1)} %copy-done, ...), custom_call_target="tpu_custom_call" | custom-call | flops 1 | bytes 1 | tf_op jit(solution)/shard_map/interior_first/pallas_call | solution.py:927
  6.6 0.8 %build_strips.1.s_ref = f32[8,64,128]{2,1,0:T(8,128)S(1)} custom-call(f32[3,8,64,256]{3,2,1,0:T(8,128)S(1)} %copy-done, f32[3,8,64,256]{3,2,1,0:T(8,128)S(1)} %copy-done.1, s32[8,64,256]{2,1,0:T(8,128)S(1)} %copy-done.2, f32[64,256]{1,0:T(8,128)S(1)} %copy-done.5, f32[8,256]{1,0:T(8,128)S(1)} %get-tuple-element.55.id_ref.own_ref), custom_call_target="tpu_custom_call" | custom-call | flops 1 | bytes 1 | tf_op jit(solution)/shard_map/build_strips/pallas_call | solution.py:902
  7.4 1.7 %collective-permute-done.xa_ref = f32[10,8,256]{2,1,0:T(8,128)S(1)} collective-permute-done((f32[10,8,256]{2,1,0:T(8,128)S(1)}, f32[10,8,256]{2,1,0:T(8,128)S(1)}, u32[]{:S(2)}, u32[]{:S(2)}) %collective-permute-start) | collective-permute-done | bytes 81952 | tf_op jit(solution)/shard_map/ppermute | solution.py:861
  9.3 2.5 %collective-permute-start.2 = (f32[72,128]{1,0:T(8,128)S(1)}, f32[72,128]{1,0:T(8,128)S(1)}, u32[]{:S(2)}, u32[]{:S(2)}) collective-permute-start(f32[72,128]{1,0:T(8,128)S(1)} %get-tuple-element.58), channel_id=1, source_target_pairs={{0,4},{1,2},{2,1},{3,7},{4,0},{5,6},{6,5},{7,3},{8,12},{9,10},{10,... | collective-permute-start | bytes 110600 | tf_op jit(solution)/shard_map/ppermute | solution.py:861
  11.8 0.7 %transform.1 = (f32[64,256]{1,0:T(8,128)S(1)}, f32[2,3,2,64,256]{4,3,2,1,0:T(8,128)S(1)}) custom-call(f32[4,2,3,2,64,256]{5,4,3,2,1,0:T(8,128)S(1)} %copy-done.3, bf16[4,2,3,2,64,256]{5,4,3,2,1,0:T(8,128)(2,1)S(1)} %copy-done.4), custom_call_target="tpu_custom_call" | custom-call | flops 1 | bytes 1 | tf_op jit(solution)/shard_map/transform/pallas_call | solution.py:912
  12.5 0.7 %strips_x.1 = (f32[3,8,2,8,256]{4,3,2,1,0:T(8,128)S(1)}, f32[3,8,2,8,256]{4,3,2,1,0:T(8,128)S(1)}, f32[3,2,2,8,256]{4,3,2,1,0:T(8,128)S(1)}, f32[2,8,256]{2,1,0:T(8,128)S(1)}) custom-call(f32[3,8,64,256]{3,2,1,0:T(8,128)S(1)} %copy-done, f32[3,8,64,256]{3,2,1,0:T(8,128)S(1)} %copy-done.1, s32[8,64,256]{2,1,0:T(8,128)S(1)} %copy-done.2, ...), custom_call_target="tpu_custom_call" | custom-call | flops 1 | bytes 1 | tf_op jit(solution)/shard_map/strips_x/pallas_call | solution.py:959
  13.2 0.2 design.1
  13.4 0.3 collective-permute-done.2.yb_ref
  13.7 1.1 %gradient.1 = (f32[32,32,128]{2,1,0:T(8,128)S(1)}, f32[3,72,128]{2,1,0:T(8,128)S(1)}, f32[3,72,128]{2,1,0:T(8,128)S(1)}) custom-call(f32[8,64,128]{2,1,0:T(8,128)S(1)} %build_strips.1.s_ref, f32[8,8,128]{2,1,0:T(8,128)S(1)} %get-tuple-element.57.t_ref, f32[72,128]{1,0:T(8,128)S(1)} %collective-permute-done.2.yb_ref, ...), custom_call_target="tpu_custom_call" | custom-call | flops 1 | bytes 1 | tf_op jit(solution)/shard_map/gradient/pallas_call | solution.py:997
  14.8 0.3 collective-permute-start.4
  15.1 1.3 %collective-permute-done.4.refs_1_ = f32[16,32,128]{2,1,0:T(8,128)S(1)} collective-permute-done((f32[16,32,128]{2,1,0:T(8,128)S(1)}, f32[16,32,128]{2,1,0:T(8,128)S(1)}, u32[]{:S(2)}, u32[]{:S(2)}) %collective-permute-start.4) | collective-permute-done | bytes 262176 | tf_op jit(solution)/shard_map/ppermute | solution.py:861
  16.5 2.5 %collective-permute-start.5 = (f32[4,32,128]{2,1,0:T(8,128)S(1)}, f32[4,32,128]{2,1,0:T(8,128)S(1)}, u32[]{:S(2)}, u32[]{:S(2)}) collective-permute-start(f32[4,32,128]{2,1,0:T(8,128)S(1)} %get-tuple-element.75), channel_id=1, source_target_pairs={{0,6},{1,7},{2,4},{3,5},{4,2},{5,3},{6,0},{7,1},{8,14},{9,15},{10,... | collective-permute-start | bytes 196616 | tf_op jit(solution)/shard_map/ppermute | solution.py:861
  19.0 1.0 %collective-permute-start.6 = (f32[4,32,128]{2,1,0:T(8,128)S(1)}, f32[4,32,128]{2,1,0:T(8,128)S(1)}, u32[]{:S(2)}, u32[]{:S(2)}) collective-permute-start(f32[4,32,128]{2,1,0:T(8,128)S(1)} %get-tuple-element.76), channel_id=1, source_target_pairs={{0,2},{1,3},{2,0},{3,1},{4,6},{5,7},{6,4},{7,5},{8,10},{9,11},{10,... | collective-permute-start | bytes 196616 | tf_op jit(solution)/shard_map/ppermute | solution.py:861
  20.0 1.4 %interior_rest.1 = (f32[3,8,64,256]{3,2,1,0:T(8,128)S(1)}, f32[3,8,64,256]{3,2,1,0:T(8,128)S(1)}, f32[8,128]{1,0:T(8,128)S(1)}) custom-call(f32[3,8,64,256]{3,2,1,0:T(8,128)S(1)} %copy-done, f32[3,8,64,256]{3,2,1,0:T(8,128)S(1)} %copy-done.1, s32[8,64,256]{2,1,0:T(8,128)S(1)} %copy-done.2, f32[32,128]{1,0:T(8,128)S(1)} %get-tuple-element.43.table, ...), custom_call_target="tpu_custom_call" | custom-call | flops 1 | bytes 1 | tf_op jit(solution)/shard_map/interior_rest/pallas_call | solution.py:938
  21.4 1.0 %collective-permute-done.5.refs_1_ = f32[4,32,128]{2,1,0:T(8,128)S(1)} collective-permute-done((f32[4,32,128]{2,1,0:T(8,128)S(1)}, f32[4,32,128]{2,1,0:T(8,128)S(1)}, u32[]{:S(2)}, u32[]{:S(2)}) %collective-permute-start.5) | collective-permute-done | bytes 65568 | tf_op jit(solution)/shard_map/ppermute | solution.py:861
  22.4 1.2 %collective-permute-done.6.refs_2_ = f32[4,32,128]{2,1,0:T(8,128)S(1)} collective-permute-done((f32[4,32,128]{2,1,0:T(8,128)S(1)}, f32[4,32,128]{2,1,0:T(8,128)S(1)}, u32[]{:S(2)}, u32[]{:S(2)}) %collective-permute-start.6) | collective-permute-done | bytes 65568 | tf_op jit(solution)/shard_map/ppermute | solution.py:861
  23.6 0.7 %collective-permute-done.7.refs_3_ = f32[4,32,128]{2,1,0:T(8,128)S(1)} collective-permute-done((f32[4,32,128]{2,1,0:T(8,128)S(1)}, f32[4,32,128]{2,1,0:T(8,128)S(1)}, u32[]{:S(2)}, u32[]{:S(2)}) %collective-permute-start.7) | collective-permute-done | bytes 65568 | tf_op jit(solution)/shard_map/ppermute | solution.py:861
  24.3 2.8 %collective-permute-start.10 = (f32[1,32,128]{2,1,0:T(8,128)S(1)}, f32[1,32,128]{2,1,0:T(8,128)S(1)}, u32[]{:S(2)}, u32[]{:S(2)}) collective-permute-start(f32[1,32,128]{2,1,0:T(8,128)S(1)} %get-tuple-element.82), channel_id=1, source_target_pairs={{0,16},{1,17},{2,18},{3,19},{4,20},{5,21},{6,22},{7,23},{8,0},{9,1... | collective-permute-start | bytes 49160 | tf_op jit(solution)/shard_map/ppermute | solution.py:861
  27.1 2.9 %collective-permute-start.9 = (f32[1,32,128]{2,1,0:T(8,128)S(1)}, f32[1,32,128]{2,1,0:T(8,128)S(1)}, u32[]{:S(2)}, u32[]{:S(2)}) collective-permute-start(f32[1,32,128]{2,1,0:T(8,128)S(1)} %get-tuple-element.81), channel_id=1, source_target_pairs={{0,24},{1,25},{2,26},{3,27},{4,28},{5,29},{6,30},{7,31},{8,16},{9,... | collective-permute-start | bytes 49160 | tf_op jit(solution)/shard_map/ppermute | solution.py:861
  30.0 1.9 %merge.1 = (f32[3,8,64,256]{3,2,1,0:T(8,128)}, f32[3,8,64,256]{3,2,1,0:T(8,128)}) custom-call(f32[3,8,64,256]{3,2,1,0:T(8,128)S(1)} %get-tuple-element.49.e_ref, f32[3,8,64,256]{3,2,1,0:T(8,128)S(1)} %get-tuple-element.50.h_ref, f32[3,5,64,256]{3,2,1,0:T(8,128)S(1)} %get-tuple-element.44.em.e2_ref, f32[3,5,64,256]{3,2,1,0:T(8,128)S(1)} %get-tuple-element.45.hm, ...), custom_call_target="tpu_custom_call" | custom-call | flops 1 | bytes 1 | tf_op jit(solution)/shard_map/merge/pallas_call | solution.py:1027
  31.8 0.8 %collective-permute-done.9 = f32[1,32,128]{2,1,0:T(8,128)S(1)} collective-permute-done((f32[1,32,128]{2,1,0:T(8,128)S(1)}, f32[1,32,128]{2,1,0:T(8,128)S(1)}, u32[]{:S(2)}, u32[]{:S(2)}) %collective-permute-start.9) | collective-permute-done | bytes 16416 | tf_op jit(solution)/shard_map/ppermute | solution.py:861
  32.6 0.6 %add_add_fusion = f32[1,32,128]{2,1,0:T(8,128)} fusion(f32[1,32,128]{2,1,0:T(8,128)S(1)} %collective-permute-done.10, f32[1,32,128]{2,1,0:T(8,128)S(1)} %collective-permute-done.9, f32[1,32,128]{2,1,0:T(8,128)S(1)} %get-tuple-element.79, f32[1,32,128]{2,1,0:T(8,128)S(1)} %collective-permute-done.8), kind=kLoop, calls=%fused_computation | loop fusion | flops 12288 | bytes 81920 | tf_op jit(solution)/shard_map/add | solution.py:1052
  (24 shorter events, 0.4 us)
Async XLA Ops:
  0.6 4.8 %copy-start.5 = (f32[64,256]{1,0:T(8,128)S(1)}, f32[64,256]{1,0:T(8,128)}, u32[]{:S(2)}) copy-start(f32[64,256]{1,0:T(8,128)} %d_ref.5) | copy-start | bytes 196612
  0.6 4.8 %copy-start.2 = (s32[8,64,256]{2,1,0:T(8,128)S(1)}, s32[8,64,256]{2,1,0:T(8,128)}, u32[]{:S(2)}) copy-start(s32[8,64,256]{2,1,0:T(8,128)} %m_ref.7) | copy-start | bytes 1572868
  0.7 4.8 %copy-start = (f32[3,8,64,256]{3,2,1,0:T(8,128)S(1)}, f32[3,8,64,256]{3,2,1,0:T(8,128)}, u32[]{:S(2)}) copy-start(f32[3,8,64,256]{3,2,1,0:T(8,128)} %e_ref.7) | copy-start | bytes 4718596
  0.7 4.8 %copy-start.1 = (f32[3,8,64,256]{3,2,1,0:T(8,128)S(1)}, f32[3,8,64,256]{3,2,1,0:T(8,128)}, u32[]{:S(2)}) copy-start(f32[3,8,64,256]{3,2,1,0:T(8,128)} %h_ref.7) | copy-start | bytes 4718596
  2.4 6.7 %collective-permute-start = (f32[10,8,256]{2,1,0:T(8,128)S(1)}, f32[10,8,256]{2,1,0:T(8,128)S(1)}, u32[]{:S(2)}, u32[]{:S(2)}) collective-permute-start(f32[10,8,256]{2,1,0:T(8,128)S(1)} %get-tuple-element.51), channel_id=1, source_target_pairs={{0,4},{1,5},{2,6},{3,7},{4,0},{5,1},{6,2},{7,3},{8,12},{9,13},{10,... | collective-permute-start | bytes 245768 | tf_op jit(solution)/shard_map/ppermute | solution.py:861
  5.4 3.6 %collective-permute-start.1 = (f32[10,8,256]{2,1,0:T(8,128)S(1)}, f32[10,8,256]{2,1,0:T(8,128)S(1)}, u32[]{:S(2)}, u32[]{:S(2)}) collective-permute-start(f32[10,8,256]{2,1,0:T(8,128)S(1)} %get-tuple-element.52), channel_id=1, source_target_pairs={{0,1},{1,0},{2,3},{3,2},{4,8},{5,9},{6,10},{7,11},{8,4},{9,5},{10,... | collective-permute-start | bytes 245768 | tf_op jit(solution)/shard_map/ppermute | solution.py:861
  5.4 6.4 %copy-start.4 = (bf16[4,2,3,2,64,256]{5,4,3,2,1,0:T(8,128)(2,1)S(1)}, bf16[4,2,3,2,64,256]{5,4,3,2,1,0:T(8,128)(2,1)}, u32[]{:S(2)}) copy-start(bf16[4,2,3,2,64,256]{5,4,3,2,1,0:T(8,128)(2,1)} %fwd_ref.1) | copy-start | bytes 4718596
  6.6 5.2 %copy-start.3 = (f32[4,2,3,2,64,256]{5,4,3,2,1,0:T(8,128)S(1)}, f32[4,2,3,2,64,256]{5,4,3,2,1,0:T(8,128)}, u32[]{:S(2)}) copy-start(f32[4,2,3,2,64,256]{5,4,3,2,1,0:T(8,128)} %adj_ref.1) | copy-start | bytes 9437188
  9.3 4.5 %collective-permute-start.2 = (f32[72,128]{1,0:T(8,128)S(1)}, f32[72,128]{1,0:T(8,128)S(1)}, u32[]{:S(2)}, u32[]{:S(2)}) collective-permute-start(f32[72,128]{1,0:T(8,128)S(1)} %get-tuple-element.58), channel_id=1, source_target_pairs={{0,4},{1,2},{2,1},{3,7},{4,0},{5,6},{6,5},{7,3},{8,12},{9,10},{10,... | collective-permute-start | bytes 110600 | tf_op jit(solution)/shard_map/ppermute | solution.py:861
  11.8 1.9 %collective-permute-start.3 = (f32[72,128]{1,0:T(8,128)S(1)}, f32[72,128]{1,0:T(8,128)S(1)}, u32[]{:S(2)}, u32[]{:S(2)}) collective-permute-start(f32[72,128]{1,0:T(8,128)S(1)} %get-tuple-element.59), channel_id=1, source_target_pairs={{0,1},{1,0},{2,3},{3,2},{4,5},{5,4},{6,7},{7,6},{8,9},{9,8},{10,11... | collective-permute-start | bytes 110600 | tf_op jit(solution)/shard_map/ppermute | solution.py:861
  14.8 1.6 %collective-permute-start.4 = (f32[16,32,128]{2,1,0:T(8,128)S(1)}, f32[16,32,128]{2,1,0:T(8,128)S(1)}, u32[]{:S(2)}, u32[]{:S(2)}) collective-permute-start(f32[16,32,128]{2,1,0:T(8,128)S(1)} %slice.3), channel_id=1, source_target_pairs={{0,1},{1,0},{2,3},{3,2},{4,5},{5,4},{6,7},{7,6},{8,9},{9,8},{10,11... | collective-permute-start | bytes 786440 | tf_op jit(solution)/shard_map/ppermute | solution.py:861
  16.5 5.9 %collective-permute-start.5 = (f32[4,32,128]{2,1,0:T(8,128)S(1)}, f32[4,32,128]{2,1,0:T(8,128)S(1)}, u32[]{:S(2)}, u32[]{:S(2)}) collective-permute-start(f32[4,32,128]{2,1,0:T(8,128)S(1)} %get-tuple-element.75), channel_id=1, source_target_pairs={{0,6},{1,7},{2,4},{3,5},{4,2},{5,3},{6,0},{7,1},{8,14},{9,15},{10,... | collective-permute-start | bytes 196616 | tf_op jit(solution)/shard_map/ppermute | solution.py:861
  19.0 4.6 %collective-permute-start.6 = (f32[4,32,128]{2,1,0:T(8,128)S(1)}, f32[4,32,128]{2,1,0:T(8,128)S(1)}, u32[]{:S(2)}, u32[]{:S(2)}) collective-permute-start(f32[4,32,128]{2,1,0:T(8,128)S(1)} %get-tuple-element.76), channel_id=1, source_target_pairs={{0,2},{1,3},{2,0},{3,1},{4,6},{5,7},{6,4},{7,5},{8,10},{9,11},{10,... | collective-permute-start | bytes 196616 | tf_op jit(solution)/shard_map/ppermute | solution.py:861
  20.0 4.3 %collective-permute-start.7 = (f32[4,32,128]{2,1,0:T(8,128)S(1)}, f32[4,32,128]{2,1,0:T(8,128)S(1)}, u32[]{:S(2)}, u32[]{:S(2)}) collective-permute-start(f32[4,32,128]{2,1,0:T(8,128)S(1)} %get-tuple-element.77), channel_id=1, source_target_pairs={{0,4},{1,5},{2,6},{3,7},{4,0},{5,1},{6,2},{7,3},{8,12},{9,13},{10,... | collective-permute-start | bytes 196616 | tf_op jit(solution)/shard_map/ppermute | solution.py:861
  24.3 7.5 %collective-permute-start.10 = (f32[1,32,128]{2,1,0:T(8,128)S(1)}, f32[1,32,128]{2,1,0:T(8,128)S(1)}, u32[]{:S(2)}, u32[]{:S(2)}) collective-permute-start(f32[1,32,128]{2,1,0:T(8,128)S(1)} %get-tuple-element.82), channel_id=1, source_target_pairs={{0,16},{1,17},{2,18},{3,19},{4,20},{5,21},{6,22},{7,23},{8,0},{9,1... | collective-permute-start | bytes 49160 | tf_op jit(solution)/shard_map/ppermute | solution.py:861
  27.1 4.8 %collective-permute-start.8 = (f32[1,32,128]{2,1,0:T(8,128)S(1)}, f32[1,32,128]{2,1,0:T(8,128)S(1)}, u32[]{:S(2)}, u32[]{:S(2)}) collective-permute-start(f32[1,32,128]{2,1,0:T(8,128)S(1)} %get-tuple-element.80), channel_id=1, source_target_pairs={{0,8},{1,9},{2,10},{3,11},{4,12},{5,13},{6,14},{7,15},{8,24},{9,25... | collective-permute-start | bytes 49160 | tf_op jit(solution)/shard_map/ppermute | solution.py:861
  27.1 5.5 %collective-permute-start.9 = (f32[1,32,128]{2,1,0:T(8,128)S(1)}, f32[1,32,128]{2,1,0:T(8,128)S(1)}, u32[]{:S(2)}, u32[]{:S(2)}) collective-permute-start(f32[1,32,128]{2,1,0:T(8,128)S(1)} %get-tuple-element.81), channel_id=1, source_target_pairs={{0,24},{1,25},{2,26},{3,27},{4,28},{5,29},{6,30},{7,31},{8,16},{9,... | collective-permute-start | bytes 49160 | tf_op jit(solution)/shard_map/ppermute | solution.py:861

commit v7 on v6

--- a/solution.py
+++ b/solution.py
@@ -127,20 +127,29 @@
         (h_in, hb.reshape(tiles, 3, planes_z, span, LANES)),
         (m_in, mb.reshape(tiles, planes_z, span, LANES)),
     ]
-    copies = []
-    for k, start in enumerate((0, size - SUB)):
-        here, there = pl.ds(start, SUB), pl.ds(k * SUB, SUB)
-        for u in range(tiles):
-            lanes = pl.ds(u * LANES, LANES)
-            for n, (src, dst) in enumerate(views):
-                source = src.at[:, here, lanes] if n == 2 else src.at[:, :, here, lanes]
-                target = dst.at[u, :, there] if n == 2 else dst.at[u, :, :, there]
-                copies.append(pltpu.make_async_copy(source, target, sems.at[len(copies)]))
-        copies.append(pltpu.make_async_copy(d_in.at[here], db.at[there], sems.at[len(copies)]))
-    copies.append(pltpu.make_async_copy(map_in, map_ref, sems.at[len(copies)]))
-    copies.append(pltpu.make_async_copy(table_in, table_ref, sems.at[len(copies)]))
-    for copy in copies:
-        copy.start()
+    copies = [], [], []
+    count = 0
+
+    def fetch(n, source, target):
+        nonlocal count
+        copies[n].append(pltpu.make_async_copy(source, target, sems.at[count]))
+        copies[n][-1].start()
+        count += 1
+
+    for n, (src, dst) in enumerate(views):
+        for k, start in enumerate((0, size - SUB)):
+            here, there = pl.ds(start, SUB), pl.ds(k * SUB, SUB)
+            for u in range(tiles):
+                lanes = pl.ds(u * LANES, LANES)
+                if n == 2:
+                    fetch(n, src.at[:, here, lanes], dst.at[u, :, there])
+                    continue
+                for c in range(3):
+                    fetch(n, src.at[c, :, here, lanes], dst.at[u, c, :, there])
+            if n == 2:
+                fetch(n, d_in.at[here], db.at[there])
+    fetch(2, map_in, map_ref)
+    fetch(2, table_in, table_ref)
     gx, gy = lax.axis_index("gx"), lax.axis_index("gy")
     total_x, total_y = size * lax.axis_size("gx"), width_y * lax.axis_size("gy")
     shape = (SUB, width_y)
@@ -149,29 +158,37 @@
     cols = (iota(shape, 1) + gy * width_y).astype(F32)
     damping, coef_h, _ = edge_coefs(rows, cols, total_x, total_y)
     layer = (sub >= ZLO) & (sub < ZLO + PLANES)
-    for copy in copies:
-        copy.wait()
+
+    def wait(n):
+        for copy in copies[n]:
+            copy.wait()
 
     def row(ref, c, r):
         rows = pl.ds(c * planes_z * span + r, planes_z, stride=span)
         return jnp.concatenate([ref[u, rows] for u in range(tiles)], axis=1)
 
     near, far = span - 1, span - 2
+    wait(0)
     ex, ey, ez = (row(eb, c, far) for c in range(3))
     up = jnp.where(sub == SUB - 1, 0.0, turn(ex, SUB - 1, 0))
     curl_y = (up - ex) - (row(eb, 2, near) - ez)
     curl_z = (row(eb, 1, near) - ey) - (turn(ex, width_y - 1, 1) - ex)
+    high = [row(eb, c, near) for c in range(3)]
+    low = [row(eb, c, 0) for c in range(3)]
+    beyond = [row(eb, 1, 1), row(eb, 2, 1)]
+    strips = [row_to_strip(v) for v in (ex, ey, ez)]
+    wait(1)
     mag = [row(hb, c, far) for c in (1, 2)]
-    high = [row(eb, c, near) for c in range(3)] + [row(hb, c, near) for c in range(3)]
+    strips += [row_to_strip(v) for v in mag]
+    high += [row(hb, c, near) for c in range(3)]
     high += [damping * h - coef_h * curl for h, curl in zip(mag, (curl_y, curl_z))]
-    low = [row(eb, c, 0) for c in range(3)] + [row(hb, c, 0) for c in range(3)]
-    low += [row(eb, 1, 1), row(eb, 2, 1)]
+    low += [row(hb, c, 0) for c in range(3)] + beyond
+    wait(2)
     for side, edge, further, tx in ((low, 0, 1, 0), (high, near, far, map_ref.shape[0] - 1)):
         density = jnp.broadcast_to(db[edge : edge + 1], shape)
         side.append(jnp.where(layer, density, row(mb, 0, edge).astype(F32)))
         misc = jnp.broadcast_to(db[further : further + 1], shape)
         side.append(jnp.where(sub == 1, id_row(map_ref, tx, shape), misc))
-    strips = [row_to_strip(v) for v in [ex, ey, ez] + mag]
     strips.append(strips[-1])
     for k in range(3):
         pair_of = jnp.concatenate([strips[2 * k], strips[2 * k + 1]], axis=1)
@@ -887,7 +904,7 @@
             pltpu.VMEM((2 * SUB, width_y), F32),
             pltpu.SMEM(tile_map.shape, jnp.int32),
             pltpu.SMEM(eps_table.shape, F32),
-            pltpu.SemaphoreType.DMA((6 * width_y // LANES + 4,)),
+            pltpu.SemaphoreType.DMA((14 * width_y // LANES + 4,)),
         ],
         compiler_params=params(),
         name="pack_x",

time: 33.4 us -> 33.3 us (level)
  no operation moved by 1% of the time
where the time goes in v7:
time: 33.3 us; the launch traced here: 33.2 us
  starting transfers between devices  15.1 us (45%)
  Pallas kernels  9.78 us (29%)
  waiting for transfers between devices  6.9 us (21%)
  between operations  0.79 us (2%)
  other arithmetic  0.61 us (2%)
    ppermute x11, starting transfers between devices, pair(): return lax.ppermute(block, ('gx', 'gy'), route)  15.1 us
    ppermute x11, waiting for transfers between devices, pair(): return lax.ppermute(block, ('gx', 'gy'), route)  6.9 us
    pallas_call x1, Pallas kernels, on_device(): pl.pallas_call(merge, out_shape=(full,) * 2, in_specs=[VMEM] * 8, out_spe...  1.85 us
    pallas_call x1, Pallas kernels, on_device(): pl.pallas_call(pack_x, out_shape=(pltpu.VMEM(face.shape, F32), pltpu.VMEM...  1.67 us
    pallas_call x1, Pallas kernels, on_device(): pl.pallas_call(interior_rest, out_shape=(full, full, struct(SUB, LANES)),...  1.36 us
    pallas_call x1, Pallas kernels, on_device(): pl.pallas_call(interior_first, out_shape=(middle, middle, struct(3, PLANE...  1.15 us
    pallas_call x1, Pallas kernels, on_device(): pl.pallas_call(gradient, out_shape=(struct(devices * rows_mine, lines, LA...  1.08 us
    pallas_call x1, Pallas kernels, on_device(): pl.pallas_call(build_strips, out_shape=struct(8, width_x, LANES), in_spec...  0.75 us
  transfers between devices with their start and end apart: 11, of which 7 were waited for; matrix products, arithmetic and copies ran while one was open for 0% of the time, Pallas kernels for 20%

profile of v7, /device:TPU:0, one launch (start us, length us, event | category | flops | bytes accessed | tf_op | source)
XLA Modules:
  0.0 33.2 jit_solution(14446280936946571602)
XLA Ops:
  0.7 1.7 %pack_x.1 = (f32[10,8,256]{2,1,0:T(8,128)S(1)}, f32[10,8,256]{2,1,0:T(8,128)S(1)}, f32[8,256]{1,0:T(8,128)S(1)}, f32[32,128]{1,0:T(8,128)S(1)}) custom-call(f32[3,8,64,256]{3,2,1,0:T(8,128)} %e_ref.7, f32[3,8,64,256]{3,2,1,0:T(8,128)} %h_ref.7, s32[8,64,256]{2,1,0:T(8,128)} %m_ref.7, f32[64,256]{1,0:T(8,128)} %d_ref.5, s32[1,4]{1,0:T(1,128)} %map_in.1, ...), custom_call_target="tpu_custom_call" | custom-call | tf_op jit(solution)/shard_map/pack_x/pallas_call | solution.py:890
  2.3 3.0 %collective-permute-start = (f32[10,8,256]{2,1,0:T(8,128)S(1)}, f32[10,8,256]{2,1,0:T(8,128)S(1)}, u32[]{:S(2)}, u32[]{:S(2)}) collective-permute-start(f32[10,8,256]{2,1,0:T(8,128)S(1)} %get-tuple-element.51), channel_id=1, source_target_pairs={{0,4},{1,5},{2,6},{3,7},{4,0},{5,1},{6,2},{7,3},{8,12},{9,13},{10,... | collective-permute-start | bytes 245768 | tf_op jit(solution)/shard_map/ppermute | solution.py:878
  5.4 1.2 %interior_first.1 = (f32[3,5,64,256]{3,2,1,0:T(8,128)S(1)}, f32[3,5,64,256]{3,2,1,0:T(8,128)S(1)}, f32[3,2,64,256]{3,2,1,0:T(8,128)S(1)}, f32[64,256]{1,0:T(8,12...) custom-call(f32[3,8,64,256]{3,2,1,0:T(8,128)S(1)} %copy-done, ...), custom_call_target="tpu_custom_call" | custom-call | flops 1 | bytes 1 | tf_op jit(solution)/shard_map/interior_first/pallas_call | solution.py:944
  6.6 0.8 %build_strips.1.s_ref = f32[8,64,128]{2,1,0:T(8,128)S(1)} custom-call(f32[3,8,64,256]{3,2,1,0:T(8,128)S(1)} %copy-done, f32[3,8,64,256]{3,2,1,0:T(8,128)S(1)} %copy-done.1, s32[8,64,256]{2,1,0:T(8,128)S(1)} %copy-done.2, f32[64,256]{1,0:T(8,128)S(1)} %copy-done.5, f32[8,256]{1,0:T(8,128)S(1)} %get-tuple-element.55.id_ref.own_ref), custom_call_target="tpu_custom_call" | custom-call | flops 1 | bytes 1 | tf_op jit(solution)/shard_map/build_strips/pallas_call | solution.py:919
  7.3 1.7 %collective-permute-done.xa_ref = f32[10,8,256]{2,1,0:T(8,128)S(1)} collective-permute-done((f32[10,8,256]{2,1,0:T(8,128)S(1)}, f32[10,8,256]{2,1,0:T(8,128)S(1)}, u32[]{:S(2)}, u32[]{:S(2)}) %collective-permute-start) | collective-permute-done | bytes 81952 | tf_op jit(solution)/shard_map/ppermute | solution.py:878
  9.3 2.5 %collective-permute-start.2 = (f32[72,128]{1,0:T(8,128)S(1)}, f32[72,128]{1,0:T(8,128)S(1)}, u32[]{:S(2)}, u32[]{:S(2)}) collective-permute-start(f32[72,128]{1,0:T(8,128)S(1)} %get-tuple-element.58), channel_id=1, source_target_pairs={{0,4},{1,2},{2,1},{3,7},{4,0},{5,6},{6,5},{7,3},{8,12},{9,10},{10,... | collective-permute-start | bytes 110600 | tf_op jit(solution)/shard_map/ppermute | solution.py:878
  11.8 0.7 %transform.1 = (f32[64,256]{1,0:T(8,128)S(1)}, f32[2,3,2,64,256]{4,3,2,1,0:T(8,128)S(1)}) custom-call(f32[4,2,3,2,64,256]{5,4,3,2,1,0:T(8,128)S(1)} %copy-done.3, bf16[4,2,3,2,64,256]{5,4,3,2,1,0:T(8,128)(2,1)S(1)} %copy-done.4), custom_call_target="tpu_custom_call" | custom-call | flops 1 | bytes 1 | tf_op jit(solution)/shard_map/transform/pallas_call | solution.py:929
  12.5 0.7 %strips_x.1 = (f32[3,8,2,8,256]{4,3,2,1,0:T(8,128)S(1)}, f32[3,8,2,8,256]{4,3,2,1,0:T(8,128)S(1)}, f32[3,2,2,8,256]{4,3,2,1,0:T(8,128)S(1)}, f32[2,8,256]{2,1,0:T(8,128)S(1)}) custom-call(f32[3,8,64,256]{3,2,1,0:T(8,128)S(1)} %copy-done, f32[3,8,64,256]{3,2,1,0:T(8,128)S(1)} %copy-done.1, s32[8,64,256]{2,1,0:T(8,128)S(1)} %copy-done.2, ...), custom_call_target="tpu_custom_call" | custom-call | flops 1 | bytes 1 | tf_op jit(solution)/shard_map/strips_x/pallas_call | solution.py:976
  13.2 0.2 design.1
  13.4 0.3 collective-permute-done.2.yb_ref
  13.7 1.1 %gradient.1 = (f32[32,32,128]{2,1,0:T(8,128)S(1)}, f32[3,72,128]{2,1,0:T(8,128)S(1)}, f32[3,72,128]{2,1,0:T(8,128)S(1)}) custom-call(f32[8,64,128]{2,1,0:T(8,128)S(1)} %build_strips.1.s_ref, f32[8,8,128]{2,1,0:T(8,128)S(1)} %get-tuple-element.57.t_ref, f32[72,128]{1,0:T(8,128)S(1)} %collective-permute-done.2.yb_ref, ...), custom_call_target="tpu_custom_call" | custom-call | flops 1 | bytes 1 | tf_op jit(solution)/shard_map/gradient/pallas_call | solution.py:1014
  14.8 0.3 collective-permute-start.4
  15.1 1.3 %collective-permute-done.4.refs_1_ = f32[16,32,128]{2,1,0:T(8,128)S(1)} collective-permute-done((f32[16,32,128]{2,1,0:T(8,128)S(1)}, f32[16,32,128]{2,1,0:T(8,128)S(1)}, u32[]{:S(2)}, u32[]{:S(2)}) %collective-permute-start.4) | collective-permute-done | bytes 262176 | tf_op jit(solution)/shard_map/ppermute | solution.py:878
  16.4 2.5 %collective-permute-start.5 = (f32[4,32,128]{2,1,0:T(8,128)S(1)}, f32[4,32,128]{2,1,0:T(8,128)S(1)}, u32[]{:S(2)}, u32[]{:S(2)}) collective-permute-start(f32[4,32,128]{2,1,0:T(8,128)S(1)} %get-tuple-element.75), channel_id=1, source_target_pairs={{0,6},{1,7},{2,4},{3,5},{4,2},{5,3},{6,0},{7,1},{8,14},{9,15},{10,... | collective-permute-start | bytes 196616 | tf_op jit(solution)/shard_map/ppermute | solution.py:878
  19.0 1.0 %collective-permute-start.6 = (f32[4,32,128]{2,1,0:T(8,128)S(1)}, f32[4,32,128]{2,1,0:T(8,128)S(1)}, u32[]{:S(2)}, u32[]{:S(2)}) collective-permute-start(f32[4,32,128]{2,1,0:T(8,128)S(1)} %get-tuple-element.76), channel_id=1, source_target_pairs={{0,2},{1,3},{2,0},{3,1},{4,6},{5,7},{6,4},{7,5},{8,10},{9,11},{10,... | collective-permute-start | bytes 196616 | tf_op jit(solution)/shard_map/ppermute | solution.py:878
  20.0 1.4 %interior_rest.1 = (f32[3,8,64,256]{3,2,1,0:T(8,128)S(1)}, f32[3,8,64,256]{3,2,1,0:T(8,128)S(1)}, f32[8,128]{1,0:T(8,128)S(1)}) custom-call(f32[3,8,64,256]{3,2,1,0:T(8,128)S(1)} %copy-done, f32[3,8,64,256]{3,2,1,0:T(8,128)S(1)} %copy-done.1, s32[8,64,256]{2,1,0:T(8,128)S(1)} %copy-done.2, f32[32,128]{1,0:T(8,128)S(1)} %get-tuple-element.43.table, ...), custom_call_target="tpu_custom_call" | custom-call | flops 1 | bytes 1 | tf_op jit(solution)/shard_map/interior_rest/pallas_call | solution.py:955
  21.4 1.0 %collective-permute-done.5.refs_1_ = f32[4,32,128]{2,1,0:T(8,128)S(1)} collective-permute-done((f32[4,32,128]{2,1,0:T(8,128)S(1)}, f32[4,32,128]{2,1,0:T(8,128)S(1)}, u32[]{:S(2)}, u32[]{:S(2)}) %collective-permute-start.5) | collective-permute-done | bytes 65568 | tf_op jit(solution)/shard_map/ppermute | solution.py:878
  22.3 1.2 %collective-permute-done.6.refs_2_ = f32[4,32,128]{2,1,0:T(8,128)S(1)} collective-permute-done((f32[4,32,128]{2,1,0:T(8,128)S(1)}, f32[4,32,128]{2,1,0:T(8,128)S(1)}, u32[]{:S(2)}, u32[]{:S(2)}) %collective-permute-start.6) | collective-permute-done | bytes 65568 | tf_op jit(solution)/shard_map/ppermute | solution.py:878
  23.6 0.7 %collective-permute-done.7.refs_3_ = f32[4,32,128]{2,1,0:T(8,128)S(1)} collective-permute-done((f32[4,32,128]{2,1,0:T(8,128)S(1)}, f32[4,32,128]{2,1,0:T(8,128)S(1)}, u32[]{:S(2)}, u32[]{:S(2)}) %collective-permute-start.7) | collective-permute-done | bytes 65568 | tf_op jit(solution)/shard_map/ppermute | solution.py:878
  24.3 2.8 %collective-permute-start.10 = (f32[1,32,128]{2,1,0:T(8,128)S(1)}, f32[1,32,128]{2,1,0:T(8,128)S(1)}, u32[]{:S(2)}, u32[]{:S(2)}) collective-permute-start(f32[1,32,128]{2,1,0:T(8,128)S(1)} %get-tuple-element.82), channel_id=1, source_target_pairs={{0,16},{1,17},{2,18},{3,19},{4,20},{5,21},{6,22},{7,23},{8,0},{9,1... | collective-permute-start | bytes 49160 | tf_op jit(solution)/shard_map/ppermute | solution.py:878
  27.0 2.9 %collective-permute-start.9 = (f32[1,32,128]{2,1,0:T(8,128)S(1)}, f32[1,32,128]{2,1,0:T(8,128)S(1)}, u32[]{:S(2)}, u32[]{:S(2)}) collective-permute-start(f32[1,32,128]{2,1,0:T(8,128)S(1)} %get-tuple-element.81), channel_id=1, source_target_pairs={{0,24},{1,25},{2,26},{3,27},{4,28},{5,29},{6,30},{7,31},{8,16},{9,... | collective-permute-start | bytes 49160 | tf_op jit(solution)/shard_map/ppermute | solution.py:878
  29.9 1.9 %merge.1 = (f32[3,8,64,256]{3,2,1,0:T(8,128)}, f32[3,8,64,256]{3,2,1,0:T(8,128)}) custom-call(f32[3,8,64,256]{3,2,1,0:T(8,128)S(1)} %get-tuple-element.49.e_ref, f32[3,8,64,256]{3,2,1,0:T(8,128)S(1)} %get-tuple-element.50.h_ref, f32[3,5,64,256]{3,2,1,0:T(8,128)S(1)} %get-tuple-element.44.em.e2_ref, f32[3,5,64,256]{3,2,1,0:T(8,128)S(1)} %get-tuple-element.45.hm, ...), custom_call_target="tpu_custom_call" | custom-call | flops 1 | bytes 1 | tf_op jit(solution)/shard_map/merge/pallas_call | solution.py:1044
  31.8 0.8 %collective-permute-done.9 = f32[1,32,128]{2,1,0:T(8,128)S(1)} collective-permute-done((f32[1,32,128]{2,1,0:T(8,128)S(1)}, f32[1,32,128]{2,1,0:T(8,128)S(1)}, u32[]{:S(2)}, u32[]{:S(2)}) %collective-permute-start.9) | collective-permute-done | bytes 16416 | tf_op jit(solution)/shard_map/ppermute | solution.py:878
  32.6 0.6 %add_add_fusion = f32[1,32,128]{2,1,0:T(8,128)} fusion(f32[1,32,128]{2,1,0:T(8,128)S(1)} %collective-permute-done.10, f32[1,32,128]{2,1,0:T(8,128)S(1)} %collective-permute-done.9, f32[1,32,128]{2,1,0:T(8,128)S(1)} %get-tuple-element.79, f32[1,32,128]{2,1,0:T(8,128)S(1)} %collective-permute-done.8), kind=kLoop, calls=%fused_computation | loop fusion | flops 12288 | bytes 81920 | tf_op jit(solution)/shard_map/add | solution.py:1069
  (24 shorter events, 0.4 us)
Async XLA Ops:
  0.6 4.8 %copy-start.5 = (f32[64,256]{1,0:T(8,128)S(1)}, f32[64,256]{1,0:T(8,128)}, u32[]{:S(2)}) copy-start(f32[64,256]{1,0:T(8,128)} %d_ref.5) | copy-start | bytes 196612
  0.6 4.7 %copy-start.2 = (s32[8,64,256]{2,1,0:T(8,128)S(1)}, s32[8,64,256]{2,1,0:T(8,128)}, u32[]{:S(2)}) copy-start(s32[8,64,256]{2,1,0:T(8,128)} %m_ref.7) | copy-start | bytes 1572868
  0.7 4.7 %copy-start = (f32[3,8,64,256]{3,2,1,0:T(8,128)S(1)}, f32[3,8,64,256]{3,2,1,0:T(8,128)}, u32[]{:S(2)}) copy-start(f32[3,8,64,256]{3,2,1,0:T(8,128)} %e_ref.7) | copy-start | bytes 4718596
  0.7 4.7 %copy-start.1 = (f32[3,8,64,256]{3,2,1,0:T(8,128)S(1)}, f32[3,8,64,256]{3,2,1,0:T(8,128)}, u32[]{:S(2)}) copy-start(f32[3,8,64,256]{3,2,1,0:T(8,128)} %h_ref.7) | copy-start | bytes 4718596
  2.3 6.7 %collective-permute-start = (f32[10,8,256]{2,1,0:T(8,128)S(1)}, f32[10,8,256]{2,1,0:T(8,128)S(1)}, u32[]{:S(2)}, u32[]{:S(2)}) collective-permute-start(f32[10,8,256]{2,1,0:T(8,128)S(1)} %get-tuple-element.51), channel_id=1, source_target_pairs={{0,4},{1,5},{2,6},{3,7},{4,0},{5,1},{6,2},{7,3},{8,12},{9,13},{10,... | collective-permute-start | bytes 245768 | tf_op jit(solution)/shard_map/ppermute | solution.py:878
  5.4 3.6 %collective-permute-start.1 = (f32[10,8,256]{2,1,0:T(8,128)S(1)}, f32[10,8,256]{2,1,0:T(8,128)S(1)}, u32[]{:S(2)}, u32[]{:S(2)}) collective-permute-start(f32[10,8,256]{2,1,0:T(8,128)S(1)} %get-tuple-element.52), channel_id=1, source_target_pairs={{0,1},{1,0},{2,3},{3,2},{4,8},{5,9},{6,10},{7,11},{8,4},{9,5},{10,... | collective-permute-start | bytes 245768 | tf_op jit(solution)/shard_map/ppermute | solution.py:878
  5.4 6.4 %copy-start.4 = (bf16[4,2,3,2,64,256]{5,4,3,2,1,0:T(8,128)(2,1)S(1)}, bf16[4,2,3,2,64,256]{5,4,3,2,1,0:T(8,128)(2,1)}, u32[]{:S(2)}) copy-start(bf16[4,2,3,2,64,256]{5,4,3,2,1,0:T(8,128)(2,1)} %fwd_ref.1) | copy-start | bytes 4718596
  6.6 5.2 %copy-start.3 = (f32[4,2,3,2,64,256]{5,4,3,2,1,0:T(8,128)S(1)}, f32[4,2,3,2,64,256]{5,4,3,2,1,0:T(8,128)}, u32[]{:S(2)}) copy-start(f32[4,2,3,2,64,256]{5,4,3,2,1,0:T(8,128)} %adj_ref.1) | copy-start | bytes 9437188
  9.3 4.5 %collective-permute-start.2 = (f32[72,128]{1,0:T(8,128)S(1)}, f32[72,128]{1,0:T(8,128)S(1)}, u32[]{:S(2)}, u32[]{:S(2)}) collective-permute-start(f32[72,128]{1,0:T(8,128)S(1)} %get-tuple-element.58), channel_id=1, source_target_pairs={{0,4},{1,2},{2,1},{3,7},{4,0},{5,6},{6,5},{7,3},{8,12},{9,10},{10,... | collective-permute-start | bytes 110600 | tf_op jit(solution)/shard_map/ppermute | solution.py:878
  11.8 1.9 %collective-permute-start.3 = (f32[72,128]{1,0:T(8,128)S(1)}, f32[72,128]{1,0:T(8,128)S(1)}, u32[]{:S(2)}, u32[]{:S(2)}) collective-permute-start(f32[72,128]{1,0:T(8,128)S(1)} %get-tuple-element.59), channel_id=1, source_target_pairs={{0,1},{1,0},{2,3},{3,2},{4,5},{5,4},{6,7},{7,6},{8,9},{9,8},{10,11... | collective-permute-start | bytes 110600 | tf_op jit(solution)/shard_map/ppermute | solution.py:878
  14.8 1.6 %collective-permute-start.4 = (f32[16,32,128]{2,1,0:T(8,128)S(1)}, f32[16,32,128]{2,1,0:T(8,128)S(1)}, u32[]{:S(2)}, u32[]{:S(2)}) collective-permute-start(f32[16,32,128]{2,1,0:T(8,128)S(1)} %slice.3), channel_id=1, source_target_pairs={{0,1},{1,0},{2,3},{3,2},{4,5},{5,4},{6,7},{7,6},{8,9},{9,8},{10,11... | collective-permute-start | bytes 786440 | tf_op jit(solution)/shard_map/ppermute | solution.py:878
  16.4 5.9 %collective-permute-start.5 = (f32[4,32,128]{2,1,0:T(8,128)S(1)}, f32[4,32,128]{2,1,0:T(8,128)S(1)}, u32[]{:S(2)}, u32[]{:S(2)}) collective-permute-start(f32[4,32,128]{2,1,0:T(8,128)S(1)} %get-tuple-element.75), channel_id=1, source_target_pairs={{0,6},{1,7},{2,4},{3,5},{4,2},{5,3},{6,0},{7,1},{8,14},{9,15},{10,... | collective-permute-start | bytes 196616 | tf_op jit(solution)/shard_map/ppermute | solution.py:878
  19.0 4.6 %collective-permute-start.6 = (f32[4,32,128]{2,1,0:T(8,128)S(1)}, f32[4,32,128]{2,1,0:T(8,128)S(1)}, u32[]{:S(2)}, u32[]{:S(2)}) collective-permute-start(f32[4,32,128]{2,1,0:T(8,128)S(1)} %get-tuple-element.76), channel_id=1, source_target_pairs={{0,2},{1,3},{2,0},{3,1},{4,6},{5,7},{6,4},{7,5},{8,10},{9,11},{10,... | collective-permute-start | bytes 196616 | tf_op jit(solution)/shard_map/ppermute | solution.py:878
  20.0 4.3 %collective-permute-start.7 = (f32[4,32,128]{2,1,0:T(8,128)S(1)}, f32[4,32,128]{2,1,0:T(8,128)S(1)}, u32[]{:S(2)}, u32[]{:S(2)}) collective-permute-start(f32[4,32,128]{2,1,0:T(8,128)S(1)} %get-tuple-element.77), channel_id=1, source_target_pairs={{0,4},{1,5},{2,6},{3,7},{4,0},{5,1},{6,2},{7,3},{8,12},{9,13},{10,... | collective-permute-start | bytes 196616 | tf_op jit(solution)/shard_map/ppermute | solution.py:878
  24.3 7.5 %collective-permute-start.10 = (f32[1,32,128]{2,1,0:T(8,128)S(1)}, f32[1,32,128]{2,1,0:T(8,128)S(1)}, u32[]{:S(2)}, u32[]{:S(2)}) collective-permute-start(f32[1,32,128]{2,1,0:T(8,128)S(1)} %get-tuple-element.82), channel_id=1, source_target_pairs={{0,16},{1,17},{2,18},{3,19},{4,20},{5,21},{6,22},{7,23},{8,0},{9,1... | collective-permute-start | bytes 49160 | tf_op jit(solution)/shard_map/ppermute | solution.py:878
  27.0 4.8 %collective-permute-start.8 = (f32[1,32,128]{2,1,0:T(8,128)S(1)}, f32[1,32,128]{2,1,0:T(8,128)S(1)}, u32[]{:S(2)}, u32[]{:S(2)}) collective-permute-start(f32[1,32,128]{2,1,0:T(8,128)S(1)} %get-tuple-element.80), channel_id=1, source_target_pairs={{0,8},{1,9},{2,10},{3,11},{4,12},{5,13},{6,14},{7,15},{8,24},{9,25... | collective-permute-start | bytes 49160 | tf_op jit(solution)/shard_map/ppermute | solution.py:878
  27.0 5.5 %collective-permute-start.9 = (f32[1,32,128]{2,1,0:T(8,128)S(1)}, f32[1,32,128]{2,1,0:T(8,128)S(1)}, u32[]{:S(2)}, u32[]{:S(2)}) collective-permute-start(f32[1,32,128]{2,1,0:T(8,128)S(1)} %get-tuple-element.81), channel_id=1, source_target_pairs={{0,24},{1,25},{2,26},{3,27},{4,28},{5,29},{6,30},{7,31},{8,16},{9,... | collective-permute-start | bytes 49160 | tf_op jit(solution)/shard_map/ppermute | solution.py:878
